TPU v7x, 256 devices: a whole 4x4x8 slice. The times are simulated.
256 devices in a mesh: lon: 16 (over x, y), lat: 16 (over z, core).
Axes of the slice: x: 4, y: 4, z: 8, core: 2. Of those that a mesh axis runs over, the one named last changes fastest.
Arguments:
- level_patches: bfloat16 [16, 26624, 80], P('lat', 'lon'), may hold values from -6 to 6
- level_embed: bfloat16 [13, 512], replicated, may hold values from -6 to 6
- embed_weight: bfloat16 [80, 512], replicated, may hold values from -0.625 to 0.625
- kv_weight: bfloat16 [512, 1024], replicated, may hold values from -0.25 to 0.25
- query: bfloat16 [3, 512], replicated, may hold values from -420 to 420
- band_levels: int32 [16], P('lat'), may hold values from 7 to 13, as said below
- grad_out: bfloat16 [16, 2048, 3, 512], P('lat', 'lon'), may hold values from -0.078125 to 0.078125
Outputs:
- kv_grad: float32 [512, 1024], P(('lon', 'lat'))
- embed_grad: float32 [80, 512], P(None, 'lat')
- query_grad: float32 [3, 512], replicated
Inputs may be any that keep to these rules, and one draw needn't show every extreme that they name: `band_levels`: the number of leading pressure levels that the dataset of each latitude band provides; in every draw one band has all 13 and another has 7.
All inputs are finite; a program needn't handle non-finite values.
Results may differ from a plain program's by a relative error of at most 0.017.
The roundings to bfloat16 on the way count: a program that leaves them out, or rounds other values in their place, can miss the bound.
Values may be sent and summed in bfloat16 or wider, within the bound.
No kernel may reach another device: no remote copies, remote signals or barrier semaphores. Data moves between devices by JAX's collectives and lax.ppermute only.
A program may use at most 64 MiB of HBM per device.

v0:
```python
import jax
import jax.numpy as jnp
from jax import lax
from jax.sharding import PartitionSpec as P

HEADS = 16


SCORE_SCALE = 0.125
EPSILON = 1e-05
MASKED = -1e30


def embed_blocks(patches, block_levels, level_embed, embed_weight, kv_weight):
    blocks, row_count, feature_count = patches.shape
    model_width = embed_weight.shape[1]
    level_table = (
        block_levels[:, None] == jnp.arange(level_embed.shape[0], dtype=jnp.int32)[None, :]
    ).astype(jnp.bfloat16)
    level_rows = jnp.dot(level_table, level_embed, preferred_element_type=jnp.float32)
    embedded = jnp.dot(
        patches.reshape(blocks * row_count, feature_count),
        embed_weight,
        preferred_element_type=jnp.float32,
    )
    embedded = embedded.reshape(blocks, row_count, model_width) + level_rows[:, None, :]
    center = embedded - jnp.mean(embedded, axis=-1, keepdims=True)
    inv_std = lax.rsqrt(jnp.mean(center * center, axis=-1, keepdims=True) + EPSILON)
    normed = (center * inv_std).reshape(blocks * row_count, model_width)
    hidden = normed.astype(jnp.bfloat16)
    key_value = jnp.dot(hidden, kv_weight, preferred_element_type=jnp.float32).astype(jnp.bfloat16)
    return (
        hidden,
        normed,
        inv_std.reshape(blocks * row_count, 1),
        key_value.reshape(blocks, row_count, 2 * model_width),
    )


def attend_back(key_value, usable, query, grad_rows):
    slot_count, row_count, double_width = key_value.shape
    model_width = double_width // 2
    head_size = model_width // HEADS
    latent = query.shape[0]
    key_heads = key_value[:, :, :model_width].reshape(slot_count, row_count, HEADS, head_size)
    value_heads = key_value[:, :, model_width:].reshape(slot_count, row_count, HEADS, head_size)
    queries = query.reshape(latent, HEADS, head_size)
    grad_heads = grad_rows.reshape(row_count, latent, HEADS, head_size)
    score = (
        jnp.einsum("ahd,mthd->tahm", queries, key_heads, preferred_element_type=jnp.float32)
        * SCORE_SCALE
    )
    score = jnp.where(usable[None, None, None, :], score, MASKED)
    peak_score = jnp.max(score, axis=-1, keepdims=True)
    exponent = jnp.exp(score - peak_score)
    attention = exponent / jnp.sum(exponent, axis=-1, keepdims=True)
    attn_weights = attention.astype(jnp.bfloat16)
    grad_attn = jnp.einsum(
        "tahd,mthd->tahm", grad_heads, value_heads, preferred_element_type=jnp.float32
    )
    grad_score = attention * (grad_attn - jnp.sum(attention * grad_attn, axis=-1, keepdims=True))
    grad_keys = (
        jnp.einsum("tahm,ahd->mthd", grad_score, queries.astype(jnp.float32)) * SCORE_SCALE
    ).astype(jnp.bfloat16)
    grad_values = jnp.einsum(
        "tahm,tahd->mthd", attn_weights, grad_heads, preferred_element_type=jnp.float32
    ).astype(jnp.bfloat16)
    query_term = (
        jnp.einsum("tahm,mthd->ahd", grad_score, key_heads, preferred_element_type=jnp.float32)
        * SCORE_SCALE
    )
    grad_kv = jnp.concatenate(
        (
            grad_keys.reshape(slot_count, row_count, model_width),
            grad_values.reshape(slot_count, row_count, model_width),
        ),
        axis=-1,
    )
    return (grad_kv, query_term.reshape(latent, model_width))


def embed_back(patch_rows, normed, inv_std, grad_kv, kv_weight):
    grad_hidden = lax.dot_general(
        grad_kv, kv_weight, (((1,), (1,)), ((), ())), preferred_element_type=jnp.float32
    )
    grad_embedded = inv_std * (
        grad_hidden
        - jnp.mean(grad_hidden, axis=-1, keepdims=True)
        - normed * jnp.mean(grad_hidden * normed, axis=-1, keepdims=True)
    )
    grad_embedded = grad_embedded.astype(jnp.bfloat16)
    return lax.dot_general(
        patch_rows, grad_embedded, (((0,), (0,)), ((), ())), preferred_element_type=jnp.float32
    )


def on_device(level_patches, level_embed, embed_weight, kv_weight, query, band_levels, grad_out):
    lon_count = lax.axis_size("lon")
    lon_at = lax.axis_index("lon")
    model_width = kv_weight.shape[0]
    level_total = level_embed.shape[0]
    feature_count = level_patches.shape[2]
    row_count = grad_out.shape[1]
    wrap_count = -(-level_total // lon_count)
    slot_count = wrap_count * lon_count
    offset = lon_at * level_total % lon_count
    wrap_id = jnp.arange(wrap_count, dtype=jnp.int32)[:, None]
    source = jnp.arange(lon_count, dtype=jnp.int32)[None, :]
    slot_block = wrap_id * lon_count + (lon_at - source * level_total) % lon_count
    slot_level = ((source * level_total + slot_block) // lon_count).reshape(-1)
    real_slot = slot_block.reshape(-1) < level_total
    kept_slots = jnp.nonzero(real_slot, size=level_total)[0].astype(jnp.int32)
    kept_levels = slot_level[kept_slots]
    usable = kept_levels < band_levels[0]
    owned_rows = level_patches[0].reshape(level_total, row_count, feature_count)
    owned_levels = (lon_at * level_total + jnp.arange(level_total, dtype=jnp.int32)) // lon_count
    grad_rows = grad_out[0]
    hidden, normed, inv_std, key_value = embed_blocks(
        owned_rows, owned_levels, level_embed, embed_weight, kv_weight
    )
    filler = jnp.zeros((slot_count - level_total,) + key_value.shape[1:], key_value.dtype)
    widened = jnp.concatenate((key_value, filler), axis=0).reshape(
        (wrap_count, lon_count) + key_value.shape[1:]
    )
    incoming = lax.all_to_all(
        jnp.roll(widened, offset, axis=1), "lon", split_axis=1, concat_axis=1, tiled=True
    )
    kept_kv = incoming.reshape(slot_count, row_count, 2 * model_width)[kept_slots]
    grad_kept, query_term = attend_back(kept_kv, usable, query, grad_rows)
    grad_slots = (
        jnp.zeros((slot_count, row_count, 2 * model_width), jnp.bfloat16)
        .at[kept_slots]
        .set(grad_kept)
    )
    returned = lax.all_to_all(
        grad_slots.reshape(wrap_count, lon_count, row_count, 2 * model_width),
        "lon",
        split_axis=1,
        concat_axis=1,
        tiled=True,
    )
    unrolled = jnp.roll(returned, -offset, axis=1).reshape((slot_count,) + returned.shape[2:])
    grad_kv = unrolled[:level_total].reshape(level_total * row_count, 2 * model_width)
    patch_rows = owned_rows.reshape(level_total * row_count, feature_count)
    embed_term = embed_back(patch_rows, normed, inv_std, grad_kv, kv_weight)
    kv_grad = lax.psum_scatter(
        lax.dot_general(
            hidden, grad_kv, (((0,), (0,)), ((), ())), preferred_element_type=jnp.float32
        ),
        ("lon", "lat"),
        scatter_dimension=0,
        tiled=True,
    )
    embed_share = lax.psum_scatter(embed_term, "lat", scatter_dimension=1, tiled=True)
    embed_grad = lax.psum(embed_share, "lon")
    query_grad = lax.psum(query_term, ("lon", "lat"))
    return (kv_grad, embed_grad, query_grad)


def solution(mesh):
    placed = (P("lat", "lon", None), P(), P(), P(), P(), P("lat"), P("lat", "lon", None, None))
    return jax.shard_map(
        on_device,
        mesh=mesh,
        in_specs=placed,
        out_specs=(P(("lon", "lat"), None), P(None, "lat"), P()),
        check_vma=False,
    )
```

profile of v0, /device:TPU:1, one launch (start us, length us, event | category | flops | bytes accessed | tf_op | source)
XLA Modules:
  0.0 529.6 jit_solution(433896690729721634)
XLA Ops:
  19.2 4.5 fusion
  23.7 7.8 %all-to-all-start = ((bf16[1,16,128,1024]{3,2,0,1:T(8,128)(2,1)}), bf16[1,16,128,1024]{3,2,0,1:T(8,128)(2,1)}, u32[]{:S(2)}, u32[]{:S(2)}) async-start(bf16[1,16,128,1024]{3,2,0,1:T(8,128)(2,1)} %fusion), calls=%async_computation | async-start | bytes 8388608 | tf_op jit(solution)/shard_map/all_to_all | solution.py:125
  37.5 55.5 %all-to-all-done = bf16[1,16,128,1024]{3,2,0,1:T(8,128)(2,1)} async-done(((bf16[1,16,128,1024]{3,2,0,1:T(8,128)(2,1)}), bf16[1,16,128,1024]{3,2,0,1:T(8,128)(2,1)}, u32[]{:S(2)}, u32[]{:S(2)}) %all-to-all-start) | async-done | bytes 4194336 | tf_op jit(solution)/shard_map/all_to_all | solution.py:125
  92.9 4.8 gather_fusion.1
  97.7 4.0 fusion.46
  101.7 3.6 copy.58
  105.3 3.6 copy.61
  108.9 12.8 %copy.63 = bf16[13,128,16,32]{3,0,2,1:T(8,128)(2,1)} copy(bf16[13,128,16,32]{1,3,2,0:T(8,128)(2,1)} %bitcast.74) | data formatting | bytes 3407872 | tf_op jit(solution)/shard_map/reshape | solution.py:46
  121.7 9.8 %fusion.48 = f32[128,16,13,3]{2,3,1,0:T(4,128)} fusion(bf16[13,128,16,32]{3,0,2,1:T(8,128)(2,1)} %copy.63, bf16[128,3,16,32]{3,1,2,0:T(4,128)(2,1)S(1)} %copy.64), kind=kOutput, calls=%fused_computation.94 | convolution fusion | flops 5111808 | bytes 2416640 | tf_op jit(solution)/shard_map/tahd,mthd->tahm/dot_general | solution.py:58
  131.5 4.6 copy.65
  141.6 3.0 copy.68
  144.6 6.7 %convert_bitcast_fusion = bf16[13,128,16,32]{3,0,2,1:T(8,128)(2,1)} fusion(bf16[128,3,16,13]{3,1,2,0:T(4,128)(2,1)} %copy.68, bf16[128,3,16,32]{3,1,2,0:T(4,128)(2,1)S(1)} %copy.64), kind=kOutput, calls=%fused_computation.8 | convolution fusion | flops 5963776 | bytes 2256896 | tf_op jit(solution)/shard_map/tahm,tahd->mthd/dot_general | solution.py:65
  151.4 9.2 %copy.70 = bf16[13,128,16,32]{1,3,2,0:T(8,128)(2,1)S(1)} copy(bf16[13,128,16,32]{3,0,2,1:T(8,128)(2,1)} %convert_bitcast_fusion) | data formatting | bytes 3407872 | tf_op jit(solution)/shard_map/convert_element_type | solution.py:67
  160.6 3.5 pad_maximum_fusion
  164.1 5.6 %copy.71 = bf16[13,128,1024]{2,1,0:T(8,128)(2,1)} copy(bf16[13,128,1024]{1,2,0:T(8,128)(2,1)} %pad_maximum_fusion) | data formatting | bytes 6815744 | tf_op jit(solution)/shard_map/concatenate | solution.py:72
  172.2 10.4 %scatter_fusion = bf16[16,128,1024]{2,1,0:T(8,128)(2,1)} fusion(bf16[16,128,1024]{2,1,0:T(8,128)(2,1)} %broadcast_in_dim.12, s32[13]{0:T(128)S(1)} %fusion.39, bf16[13,128,1024]{2,1,0:T(8,128)(2,1)} %copy.71), kind=kCustom, calls=%fused_computation.3 | custom fusion | bytes 10223668 | tf_op jit(solution)/shard_map/scatter | solution.py:133
  182.6 9.6 %all-to-all-start.1 = ((bf16[1,16,128,1024]{3,2,0,1:T(8,128)(2,1)}), bf16[1,16,128,1024]{3,2,0,1:T(8,128)(2,1)}, u32[]{:S(2)}, u32[]{:S(2)}) async-start(bf16[1,16,128,1024]{3,2,0,1:T(8,128)(2,1)} %bitcast.71), calls=%async_computation.1 | async-start | bytes 8388608 | tf_op jit(solution)/shard_map/all_to_all | solution.py:135
  192.5 4.8 copy.74
  197.3 43.3 %all-to-all-done.1 = bf16[1,16,128,1024]{3,2,0,1:T(8,128)(2,1)} async-done(((bf16[1,16,128,1024]{3,2,0,1:T(8,128)(2,1)}), bf16[1,16,128,1024]{3,2,0,1:T(8,128)(2,1)}, u32[]{:S(2)}, u32[]{:S(2)}) %all-to-all-start.1) | async-done | bytes 4194336 | tf_op jit(solution)/shard_map/all_to_all | solution.py:135
  240.6 3.3 fusion.1
  247.9 5.4 %fusion.49 = f32[512,1024]{1,0:T(8,128)} fusion(bf16[1664,512]{1,0:T(8,128)(2,1)S(1)} %bitcast.80, bf16[1664,1024]{1,0:T(8,128)(2,1)} %bitcast.78), kind=kOutput, calls=%fused_computation.95 | convolution fusion | flops 1744830464 | bytes 7208960 | tf_op jit(solution)/shard_map/dot_general | solution.py:147
  255.5 84.4 %psum.15 = f32[3,512]{1,0:T(4,128)} all-reduce(f32[3,512]{1,0:T(4,128)S(1)} %reshape.287), channel_id=1, replica_groups=mesh['lon'=16,'lat'=16] {'lon','lat'}, use_global_device_ids=true, to_apply=%region_15.17 | all-reduce | flops 1536 | bytes 12288 | tf_op jit(solution)/shard_map/psum | solution.py:156
  340.7 57.3 %psum.14 = f32[80,32]{1,0:T(8,128)S(1)} all-reduce(f32[80,32]{1,0:T(8,128)S(1)} %copy.85), channel_id=1, replica_groups=mesh['lon'=16,'lat'=16] {'lon'}, use_global_device_ids=true, to_apply=%region_14.16 | all-reduce | flops 2560 | bytes 20480 | tf_op jit(solution)/shard_map/psum | solution.py:155
  398.7 122.1 %all-reduce.4.cloned.1.call-done = f32[512,1024]{1,0:T(8,128)} async-done(((f32[512,1024]{1,0:T(8,128)}), f32[512,1024]{1,0:T(8,128)}) %all-reduce.4.cloned.1.call-update) | async-done | bytes 2097168
  (71 shorter events, 33.4 us)
Async XLA Ops:
  8.0 6.9 %copy-start = (bf16[512,1024]{1,0:T(8,128)(2,1)S(1)}, bf16[512,1024]{1,0:T(8,128)(2,1)}, u32[]{:S(2)}) copy-start(bf16[512,1024]{1,0:T(8,128)(2,1)} %param.12) | copy-start | bytes 3145732
  14.9 1.9 copy-start.1
  23.7 9.6 %copy-start.11 = (bf16[3,512]{1,0:T(4,128)(2,1)S(1)}, bf16[3,512]{1,0:T(4,128)(2,1)}, u32[]{:S(2)}) copy-start(bf16[3,512]{1,0:T(4,128)(2,1)} %param.13) | copy-start | bytes 9220
  23.7 9.7 %copy-start.9 = (bf16[1,128,3,512]{3,1,2,0:T(8,128)(2,1)S(1)}, bf16[1,128,3,512]{3,1,2,0:T(8,128)(2,1)}, u32[]{:S(2)}) copy-start(bf16[1,128,3,512]{3,1,2,0:T(8,128)(2,1)} %param.15) | copy-start | bytes 1179652
  23.7 69.3 %all-to-all-start = ((bf16[1,16,128,1024]{3,2,0,1:T(8,128)(2,1)}), bf16[1,16,128,1024]{3,2,0,1:T(8,128)(2,1)}, u32[]{:S(2)}, u32[]{:S(2)}) async-start(bf16[1,16,128,1024]{3,2,0,1:T(8,128)(2,1)} %fusion), calls=%async_computation | async-start | bytes 8388608 | tf_op jit(solution)/shard_map/all_to_all | solution.py:125
  136.2 2.0 copy-start.3
  138.7 0.7 copy-start.7
  182.6 58.0 %all-to-all-start.1 = ((bf16[1,16,128,1024]{3,2,0,1:T(8,128)(2,1)}), bf16[1,16,128,1024]{3,2,0,1:T(8,128)(2,1)}, u32[]{:S(2)}, u32[]{:S(2)}) async-start(bf16[1,16,128,1024]{3,2,0,1:T(8,128)(2,1)} %bitcast.71), calls=%async_computation.1 | async-start | bytes 8388608 | tf_op jit(solution)/shard_map/all_to_all | solution.py:135
  192.2 147.7 %reduce-scatter.4.cloned.1.call-start = ((), (), s32[]{:S(2)}) async-start(), calls=%async_computation.3 | async-start | bytes 278528
  240.6 3.3 copy-start.2
  243.9 2.2 copy-start.4
  244.0 2.2 copy-start.6
  244.0 2.2 copy-start.10
  246.2 1.7 copy-start.5
  247.8 273.0 %all-reduce.4.cloned.1.call-start = ((), (), s32[]{:S(2)}) async-start(), calls=%async_computation.4 | async-start | bytes 4194304
  247.9 5.5 %copy-start.8 = (bf16[128,3,16,13]{0,1,3,2:T(4,128)(2,1)S(1)}, bf16[128,3,16,13]{0,1,3,2:T(4,128)(2,1)}, u32[]{:S(2)}) copy-start(bf16[128,3,16,13]{0,1,3,2:T(4,128)(2,1)} %copy-done.7) | copy-start | bytes 479236
Sparse Core Ops, SparseCore 0:
  247.9 61.8 reduce-scatter.3
Sparse Core Ops, SparseCore 1:
  253.7 267.1 all-reduce.3
where the time goes:
time: 532 us; the launch traced here: 530 us
  waiting for transfers between devices  221 us (42%)
  blocking collectives  142 us (27%)
  local copies, waits for them, and re-layouts  81.6 us (15%)
  matrix products  33.8 us (6%)
  starting transfers between devices  17.7 us (3%)
  other arithmetic  17.4 us (3%)
  between operations  16.5 us (3%)
    unnamed x4, waiting for transfers between devices  122 us
    psum x1, blocking collectives, on_device(): query_grad = lax.psum(query_term, ('lon', 'lat'))  84.4 us
    psum x1, blocking collectives, on_device(): embed_grad = lax.psum(embed_share, 'lon')  57.3 us
    all_to_all x1, waiting for transfers between devices, on_device(): lax.all_to_all(jnp.roll(widened, offset, axis=1), 'lon', split_axis=1, co...  55.5 us
    all_to_all x1, waiting for transfers between devices, on_device(): lax.all_to_all(grad_slots.reshape(wrap_count, lon_count, row_count, 2 * m...  43.3 us
    reshape x1, local copies, waits for them, and re-layouts, attend_back(): key_value[:, :, model_width:]  12.8 us
  transfers between devices with their start and end apart: 4, of which 3 were waited for; matrix products, arithmetic and copies ran while one was open for 4% of the time, Pallas kernels for 0%

commit v1 on v0

v1 whole, which is shorter than its diff:
```python
import functools

import jax
import jax.numpy as jnp
from jax import lax
from jax.experimental import pallas as pl
from jax.experimental.pallas import tpu as pltpu
from jax.sharding import PartitionSpec as P

HEADS = 16
SCORE_SCALE = 0.125
EPSILON = 1e-05
MASKED = -1e30
BF16 = jnp.bfloat16
F32 = jnp.float32

LEVELS = 13
TOK = 128
PAIRS = 7
WIDE = 2 * TOK
SPAN = PAIRS * WIDE
D = 512
FEAT = 80
AUG = 96
LATENT = 3
AH = LATENT * HEADS
NT = (((1,), (1,)), ((), ()))
RING = 16

VMEM = pl.BlockSpec(memory_space=pltpu.VMEM)
SMEM = pl.BlockSpec(memory_space=pltpu.SMEM)


def params(mib):
    return pltpu.CompilerParams(vmem_limit_bytes=mib * 1024 * 1024)


def slot_kernel(lon_ref, patch_ref, slot_ref):
    lon = lon_ref[0]
    for i in range(LEVELS):
        owner = lax.rem(lon * LEVELS + i, RING)
        block = patch_ref[i * TOK : (i + 1) * TOK, :].astype(F32)
        slot_ref[owner] = block.T.astype(BF16)


def prep_kernel(
    kvw_ref, embed_w_ref, level_ref, query_ref, grad_ref, kvwt_ref, waug_ref, qbdt_ref, qbd2_ref, gt_ref, rows
):
    for c in range(4):
        kvwt_ref[c * 256 : (c + 1) * 256, :] = kvw_ref[:, c * 256 : (c + 1) * 256].astype(F32).T.astype(BF16)
    rows[...] = jnp.zeros_like(rows)
    rows[:FEAT, :] = embed_w_ref[...].astype(F32)
    rows[FEAT : FEAT + LEVELS, :] = level_ref[...].astype(F32)
    waug_ref[...] = rows[...].T.astype(BF16)
    head = lax.broadcasted_iota(jnp.int32, (HEADS, D), 0)
    owner = lax.broadcasted_iota(jnp.int32, (HEADS, D), 1) // (D // HEADS)
    for a in range(LATENT):
        block = jnp.where(head == owner, query_ref[a : a + 1, :].astype(F32), 0.0)
        rows[a * HEADS : (a + 1) * HEADS, :] = block
        rows[AH + a * HEADS : AH + (a + 1) * HEADS, :] = block
    qbdt_ref[...] = rows[:AH, :].astype(BF16)
    qbd2_ref[...] = rows[...].T.astype(BF16)
    for a in range(LATENT):
        gt_ref[a] = grad_ref[:, a * D : (a + 1) * D].astype(F32).T.astype(BF16)


def main_kernel(
    lon_ref, count_ref, recv_ref, waug_ref, kvwt_ref, kvw_ref, qbdt_ref, qbd2_ref, gt_ref,
    kv_out, embed_out, query_out,
    g2, paug_s, hid_s, kv_s, gkv_s, ge_s, nrm_s, inv_s, sc_s, ga_s, w_s, gs_s,
):
    lon = lon_ref[0]
    count = count_ref[0]
    for a in range(LATENT):
        wide = gt_ref[a].astype(F32)
        g2[a, :, :TOK] = wide
        g2[a, :, TOK:] = wide

    def forward(p, carry):
        at = pl.ds(pl.multiple_of(p * WIDE, WIDE), WIDE)
        first = 2 * p
        second = jnp.minimum(2 * p + 1, LEVELS - 1)
        paug_s[:FEAT, at] = jnp.concatenate(
            [recv_ref[(RING * first + lon) // LEVELS], recv_ref[(RING * second + lon) // LEVELS]], axis=1
        )
        row = lax.broadcasted_iota(jnp.int32, (AUG - FEAT, WIDE), 0)
        lane = lax.broadcasted_iota(jnp.int32, (AUG - FEAT, WIDE), 1)
        level = jnp.where(lane >= TOK, second, first)
        paug_s[FEAT:, at] = jnp.where(row == level, 1.0, 0.0).astype(BF16)
        embedded = jnp.dot(waug_ref[...], paug_s[:, at], preferred_element_type=F32)
        center = embedded - jnp.mean(embedded, axis=0, keepdims=True)
        inv_std = lax.rsqrt(jnp.mean(center * center, axis=0, keepdims=True) + EPSILON)
        normed = center * inv_std
        inv_s[:, at] = inv_std
        nrm_s[:, at] = normed
        hid_s[:, at] = normed.astype(BF16)
        kv_s[:, at] = jnp.dot(kvwt_ref[...], hid_s[:, at], preferred_element_type=F32).astype(BF16)
        sc_s[:, at] = (
            jnp.dot(qbdt_ref[...], kv_s[:D, at], preferred_element_type=F32) * SCORE_SCALE
        )
        values = kv_s[D:, at].astype(F32)
        for a in range(LATENT):
            product = (g2[a] * values).reshape(HEADS, D // HEADS, WIDE)
            ga_s[a * HEADS : (a + 1) * HEADS, at] = jnp.sum(product, axis=1)
        return carry

    lax.fori_loop(0, PAIRS, forward, 0)

    score = [
        jnp.where(l < count, sc_s[:, l * TOK : (l + 1) * TOK], MASKED) for l in range(LEVELS)
    ]
    peak = functools.reduce(jnp.maximum, score)
    total = jnp.zeros_like(peak)
    for l in range(LEVELS):
        exponent = jnp.exp(score[l] - peak)
        sc_s[:, l * TOK : (l + 1) * TOK] = exponent
        total = total + exponent
    inverse = 1.0 / total
    inner = jnp.zeros_like(peak)
    for l in range(LEVELS):
        lanes = slice(l * TOK, (l + 1) * TOK)
        attention = sc_s[:, lanes] * inverse
        sc_s[:, lanes] = attention
        w_s[:, lanes] = attention.astype(BF16).astype(F32)
        inner = inner + attention * ga_s[:, lanes]
    for l in range(LEVELS):
        lanes = slice(l * TOK, (l + 1) * TOK)
        grad_score = sc_s[:, lanes] * (ga_s[:, lanes] - inner) * SCORE_SCALE
        high = grad_score.astype(BF16)
        gs_s[:AH, lanes] = high
        gs_s[AH:, lanes] = (grad_score - high.astype(F32)).astype(BF16)
    tail = slice(LEVELS * TOK, SPAN)
    w_s[:, tail] = jnp.zeros((AH, TOK), F32)
    gs_s[:, tail] = jnp.zeros((2 * AH, TOK), BF16)

    def backward(p, carry):
        at = pl.ds(pl.multiple_of(p * WIDE, WIDE), WIDE)
        gkv_s[:D, at] = jnp.dot(qbd2_ref[...], gs_s[:, at], preferred_element_type=F32).astype(BF16)
        grad_values = None
        for a in range(LATENT):
            weight = w_s[a * HEADS : (a + 1) * HEADS, at].reshape(HEADS, 1, WIDE)
            term = weight * g2[a].reshape(HEADS, D // HEADS, WIDE)
            grad_values = term if grad_values is None else grad_values + term
        gkv_s[D:, at] = grad_values.reshape(D, WIDE).astype(BF16)
        grad_hidden = jnp.dot(kvw_ref[...], gkv_s[:, at], preferred_element_type=F32)
        normed = nrm_s[:, at]
        mean = jnp.mean(grad_hidden, axis=0, keepdims=True)
        slope = jnp.mean(grad_hidden * normed, axis=0, keepdims=True)
        ge_s[:, at] = (inv_s[:, at] * (grad_hidden - mean - normed * slope)).astype(BF16)
        return carry

    lax.fori_loop(0, PAIRS, backward, 0)

    def project(c, carry):
        at = pl.ds(pl.multiple_of(c * WIDE, WIDE), WIDE)
        kv_out[:, at] = lax.dot_general(
            hid_s[...], gkv_s[at, :], NT, preferred_element_type=F32
        ).astype(BF16)
        return carry

    lax.fori_loop(0, 2 * D // WIDE, project, 0)
    embed_t = lax.dot_general(ge_s[...], paug_s[...], NT, preferred_element_type=F32)
    embed_out[:, :AUG] = embed_t.astype(BF16)
    embed_out[:, AUG:] = jnp.zeros((D, TOK - AUG), BF16)
    rows = lax.dot_general(gs_s[...], kv_s[:D, :], NT, preferred_element_type=F32)
    rows = rows[:AH] + rows[AH:]
    head = lax.broadcasted_iota(jnp.int32, (HEADS, D), 0)
    owner = lax.broadcasted_iota(jnp.int32, (HEADS, D), 1) // (D // HEADS)
    for a in range(LATENT):
        block = jnp.where(head == owner, rows[a * HEADS : (a + 1) * HEADS], 0.0)
        query_out[a : a + 1, :] = jnp.sum(block, axis=0, keepdims=True)


PACK = 64
SHARE = 48


def sum_lon_kernel(kv_ref, embed_ref, query_ref, pack_ref, total, tile):
    acc = kv_ref[0].astype(F32)
    for source in range(1, RING):
        acc = acc + kv_ref[source].astype(F32)
    total[...] = acc
    tile[...] = jnp.zeros_like(tile)
    for a in range(LATENT):
        for c in range(4):
            tile[16 + a * 4 + c : 17 + a * 4 + c, :] = query_ref[a : a + 1, c * TOK : (c + 1) * TOK]
    query_rows = tile[16:32, :].astype(BF16)
    for target in range(RING):
        for c in range(8):
            tile[2 * c : 2 * c + 2, :] = total[2 * target : 2 * target + 2, c * TOK : (c + 1) * TOK]
        pack_ref[target, 0:16, :] = tile[0:16, :].astype(BF16)
        pack_ref[target, 16:48, :] = embed_ref[target * 32 : (target + 1) * 32, :]
        pack_ref[target, 48:64, :] = query_rows


def sum_lat_kernel(pack_ref, kv_out, share_ref, tile):
    acc = pack_ref[0].astype(F32)
    for source in range(1, RING):
        acc = acc + pack_ref[source].astype(F32)
    tile[...] = acc
    for c in range(8):
        kv_out[:, c * TOK : (c + 1) * TOK] = tile[2 * c : 2 * c + 2, :]
    share = acc[16:, :].astype(BF16)
    for target in range(RING):
        share_ref[target] = share


def sum_share_kernel(share_ref, embed_out, query_out, tile):
    acc = share_ref[0].astype(F32)
    for source in range(1, RING):
        acc = acc + share_ref[source].astype(F32)
    tile[...] = acc
    embed_out[...] = tile[0:32, :].T[:FEAT, :]
    for a in range(LATENT):
        for c in range(4):
            query_out[a : a + 1, c * TOK : (c + 1) * TOK] = tile[32 + a * 4 + c : 33 + a * 4 + c, :]


def shape(*dims, dtype=BF16):
    return jax.ShapeDtypeStruct(dims, dtype)


def on_device(level_patches, level_embed, embed_weight, kv_weight, query, band_levels, grad_out):
    lon = lax.axis_index("lon").astype(jnp.int32).reshape(1)
    slots = pl.pallas_call(
        slot_kernel,
        out_shape=shape(RING, FEAT, TOK),
        in_specs=[SMEM, VMEM],
        out_specs=VMEM,
        compiler_params=params(16),
    )(lon, level_patches[0])
    kvwt, waug, qbdt, qbd2, grad_t = pl.pallas_call(
        prep_kernel,
        out_shape=(shape(2 * D, D), shape(D, AUG), shape(AH, D), shape(D, AUG), shape(LATENT, D, TOK)),
        in_specs=[VMEM] * 5,
        out_specs=(VMEM,) * 5,
        scratch_shapes=[pltpu.VMEM((AUG, D), F32)],
        compiler_params=params(24),
    )(kv_weight, embed_weight, level_embed, query, grad_out[0].reshape(TOK, LATENT * D))
    recv = lax.all_to_all(slots, "lon", 0, 0, tiled=True)
    kv_term, embed_term, query_term = pl.pallas_call(
        main_kernel,
        out_shape=(shape(D, 2 * D), shape(D, TOK), shape(LATENT, D, dtype=F32)),
        in_specs=[SMEM, SMEM] + [VMEM] * 7,
        out_specs=(VMEM,) * 3,
        scratch_shapes=[
            pltpu.VMEM((LATENT, D, WIDE), F32),
            pltpu.VMEM((AUG, SPAN), BF16),
            pltpu.VMEM((D, SPAN), BF16),
            pltpu.VMEM((2 * D, SPAN), BF16),
            pltpu.VMEM((2 * D, SPAN), BF16),
            pltpu.VMEM((D, SPAN), BF16),
            pltpu.VMEM((D, SPAN), F32),
            pltpu.VMEM((1, SPAN), F32),
            pltpu.VMEM((AH, SPAN), F32),
            pltpu.VMEM((AH, SPAN), F32),
            pltpu.VMEM((AH, SPAN), F32),
            pltpu.VMEM((2 * AH, SPAN), BF16),
        ],
        compiler_params=params(48),
    )(lon, band_levels, recv, waug, kvwt, kv_weight, qbdt, qbd2, grad_t)
    kv_lon = lax.all_to_all(kv_term.reshape(RING, D // RING, 2 * D), "lon", 0, 0, tiled=True)
    pack = pl.pallas_call(
        sum_lon_kernel,
        out_shape=shape(RING, PACK, TOK),
        in_specs=[VMEM] * 3,
        out_specs=VMEM,
        scratch_shapes=[pltpu.VMEM((D // RING, 2 * D), F32), pltpu.VMEM((32, TOK), F32)],
        compiler_params=params(16),
    )(kv_lon, embed_term, query_term)
    packed = lax.all_to_all(pack, "lat", 0, 0, tiled=True)
    kv_grad, share = pl.pallas_call(
        sum_lat_kernel,
        out_shape=(shape(2, 2 * D, dtype=F32), shape(RING, SHARE, TOK)),
        in_specs=[VMEM],
        out_specs=(VMEM, VMEM),
        scratch_shapes=[pltpu.VMEM((PACK, TOK), F32)],
        compiler_params=params(16),
    )(packed)
    shared = lax.all_to_all(share, "lon", 0, 0, tiled=True)
    embed_grad, query_grad = pl.pallas_call(
        sum_share_kernel,
        out_shape=(shape(FEAT, 32, dtype=F32), shape(LATENT, D, dtype=F32)),
        in_specs=[VMEM],
        out_specs=(VMEM, VMEM),
        scratch_shapes=[pltpu.VMEM((SHARE, TOK), F32)],
        compiler_params=params(16),
    )(shared)
    return (kv_grad, embed_grad, query_grad)


def solution(mesh):
    placed = (P("lat", "lon", None), P(), P(), P(), P(), P("lat"), P("lat", "lon", None, None))
    return jax.shard_map(
        on_device,
        mesh=mesh,
        in_specs=placed,
        out_specs=(P(("lon", "lat"), None), P(None, "lat"), P()),
        check_vma=False,
    )
```

time: 532 us -> 92.2 us (0.17)
  waiting for transfers between devices: 221 us -> 3.51 us
  blocking collectives: 142 us -> 52.2 us
  local copies, waits for them, and re-layouts: 81.6 us -> 5.81 us
  matrix products: 33.8 us -> 0 us
  Pallas kernels: 0 us -> 21.1 us
  other arithmetic: 17.4 us -> 0 us
  between operations: 16.5 us -> 1.36 us
  starting transfers between devices: 17.7 us -> 7.72 us
    psum x2 -> x0, blocking collectives: 142 us -> none  [the longest x1 84.4 us: on_device(): query_grad = lax.psum(query_term, ('lon', 'lat'))]
    unnamed x4 -> x0, waiting for transfers between devices: 122 us -> none
    all_to_all x2 -> x1, waiting for transfers between devices: 98.7 us -> 3.51 us  [on_device(): recv = lax.all_to_all(slots, 'lon', 0, 0, tiled=True)]
    all_to_all x0 -> x3, blocking collectives: none -> 52.2 us  [the longest x1 23 us: on_device(): packed = lax.all_to_all(pack, 'lat', 0, 0, tiled=True)]
    dot_general x11 -> x0, matrix products: 33.8 us -> none  [the longest x1 9.78 us: attend_back(): jnp.einsum('tahd,mthd->tahm', grad_heads, value_heads, preferred_element_...]
    pallas_call x0 -> x6, Pallas kernels: none -> 21.1 us  [the longest x1 18.1 us: on_device(): pl.pallas_call(main_kernel, out_shape=(shape(D, 2 * D), shape(D, TOK), sh...]
    reshape x5 -> x0, local copies, waits for them, and re-layouts: 20.1 us -> none  [the longest x1 12.8 us: attend_back(): key_value[:, :, model_width:]]
    convert_element_type x3 -> x0, local copies, waits for them, and re-layouts: 13.9 us -> none  [the longest x1 9.24 us: attend_back(): grad_values = jnp.einsum('tahm,tahd->mthd', attn_weights, grad_heads, pre...]
  transfers between devices with their start and end apart: 4 -> 1, of which waited for: 3 -> 1; matrix products, arithmetic and copies ran while one was open for 4% -> 0% of each run, Pallas kernels for 0% -> 1%
where the time goes in v1:
time: 92.2 us; the launch traced here: 91.7 us
  blocking collectives  52.2 us (57%)
  Pallas kernels  21.1 us (23%)
  starting transfers between devices  7.72 us (8%)
  local copies, waits for them, and re-layouts  5.81 us (6%)
  waiting for transfers between devices  3.51 us (4%)
  between operations  1.36 us (1%)
    all_to_all x1, blocking collectives, on_device(): packed = lax.all_to_all(pack, 'lat', 0, 0, tiled=True)  23 us
    all_to_all x1, blocking collectives, on_device(): lax.all_to_all(kv_term.reshape(RING, D // RING, 2 * D), 'lon', 0, 0, tile...  18.6 us
    pallas_call x1, Pallas kernels, on_device(): pl.pallas_call(main_kernel, out_shape=(shape(D, 2 * D), shape(D, TOK), sh...  18.1 us
    all_to_all x1, blocking collectives, on_device(): shared = lax.all_to_all(share, 'lon', 0, 0, tiled=True)  10.6 us
    all_to_all x1, starting transfers between devices, on_device(): recv = lax.all_to_all(slots, 'lon', 0, 0, tiled=True)  7.72 us
    unnamed x17, local copies, waits for them, and re-layouts  5.63 us
    all_to_all x1, waiting for transfers between devices, on_device(): recv = lax.all_to_all(slots, 'lon', 0, 0, tiled=True)  3.51 us
  transfers between devices with their start and end apart: 1, of which 1 were waited for; matrix products, arithmetic and copies ran while one was open for 0% of the time, Pallas kernels for 1%

profile of v1, /device:TPU:1, one launch (start us, length us, event | category | flops | bytes accessed | tf_op | source)
XLA Modules:
  0.0 91.7 jit_solution(13690763322615614327)
XLA Ops:
  0.6 1.2 %copy.13 = bf16[1,1664,80]{2,1,0:T(8,128)(2,1)S(1)} copy(bf16[1,1664,80]{1,2,0:T(8,128)(2,1)} %param.7) | data formatting | bytes 532480 | tf_op args[0]
  1.9 0.9 %shard_map.94 = bf16[16,80,128]{2,1,0:T(8,128)(2,1)} custom-call(s32[1]{0:T(128)} %bitcast.lon_ref, bf16[1664,80]{1,0:T(8,128)(2,1)S(1)} %bitcast.4), custom_call_target="tpu_custom_call" | custom-call | tf_op jit(solution)/shard_map/pallas_call | solution.py:225
  2.8 7.7 %all-to-all-start = ((bf16[16,80,128]{2,1,0:T(8,128)(2,1)}), bf16[16,80,128]{2,1,0:T(8,128)(2,1)S(1)}, u32[]{:S(2)}, u32[]{:S(2)}) async-start(bf16[16,80,128]{2,1,0:T(8,128)(2,1)} %shard_map.94), calls=%async_computation | async-start | bytes 655360 | tf_op jit(solution)/shard_map/all_to_all | solution.py:240
  11.2 0.0 copy-done.6
  11.2 0.2 copy.14
  11.4 0.0 copy-start.1
  11.4 0.2 copy.15.grad_ref
  11.6 0.0 copy-done
  11.6 0.7 copy-done.1
  12.3 0.7 copy-done.4
  13.0 0.7 copy-done.5
  13.7 0.5 shard_map.95
  14.2 0.0 copy-start.2
  14.2 0.6 copy-done.2
  14.8 3.5 %all-to-all-done.recv_ref = bf16[16,80,128]{2,1,0:T(8,128)(2,1)S(1)} async-done(((bf16[16,80,128]{2,1,0:T(8,128)(2,1)}), bf16[16,80,128]{2,1,0:T(8,128)(2,1)S(1)}, u32[]{:S(2)}, u32[]{:S(2)}) %all-to-all-start) | async-done | bytes 327712 | tf_op jit(solution)/shard_map/all_to_all | solution.py:240
  18.3 0.8 copy-done.3
  19.1 18.1 %shard_map.96 = (bf16[512,1024]{1,0:T(8,128)(2,1)S(1)}, bf16[512,128]{1,0:T(8,128)(2,1)S(1)}, f32[3,512]{1,0:T(4,128)S(1)}) custom-call(s32[1]{0:T(128)} %bitcast.lon_ref, s32[1]{0:T(128)S(6)} %copy.17.count_ref, bf16[16,80,128]{2,1,0:T(8,128)(2,1)S(1)} %all-to-all-done.recv_ref, bf16[512,96]{1,0:T(8,128)(2,1)S(1)} %get-tuple-element.15.waug_ref, ...), custom_call_target="tpu_custom_call" | custom-call | tf_op jit(solution)/shard_map/pallas_call | solution.py:241
  37.2 18.6 %all_to_all.20.kv_ref = bf16[16,32,1024]{2,1,0:T(8,128)(2,1)S(1)} all-to-all(bf16[16,32,1024]{2,1,0:T(8,128)(2,1)S(1)} %bitcast.5), channel_id=1, replica_groups=mesh['lon'=16,'lat'=16] {'lon'}, dimensions={0} | all-to-all | bytes 2097152 | tf_op jit(solution)/shard_map/all_to_all | solution.py:262
  55.8 0.3 shard_map.97
  56.1 23.0 %all_to_all.21.pack_ref = bf16[16,64,128]{2,1,0:T(8,128)(2,1)S(1)} all-to-all(bf16[16,64,128]{2,1,0:T(8,128)(2,1)S(1)} %shard_map.97), channel_id=1, replica_groups=mesh['lon'=16,'lat'=16] {'lat'}, dimensions={0} | all-to-all | bytes 524288 | tf_op jit(solution)/shard_map/all_to_all | solution.py:271
  79.1 0.6 shard_map.98
  79.8 10.6 %all_to_all.22.share_ref = bf16[16,48,128]{2,1,0:T(8,128)(2,1)S(1)} all-to-all(bf16[16,48,128]{2,1,0:T(8,128)(2,1)S(1)} %get-tuple-element.24), channel_id=1, replica_groups=mesh['lon'=16,'lat'=16] {'lon'}, dimensions={0} | all-to-all | bytes 393216 | tf_op jit(solution)/shard_map/all_to_all | solution.py:280
  90.4 0.6 shard_map.99
  91.0 0.7 copy.16
  (5 shorter events, 0.0 us)
Async XLA Ops:
  1.9 9.3 %copy-start.6 = (bf16[1,128,3,512]{3,1,2,0:T(8,128)(2,1)S(1)}, bf16[1,128,3,512]{3,1,2,0:T(8,128)(2,1)}, u32[]{:S(2)}) copy-start(bf16[1,128,3,512]{3,1,2,0:T(8,128)(2,1)} %param.13) | copy-start | bytes 1179652
  2.8 8.8 %copy-start = (bf16[512,1024]{1,0:T(8,128)(2,1)S(1)}, bf16[512,1024]{1,0:T(8,128)(2,1)}, u32[]{:S(2)}) copy-start(bf16[512,1024]{1,0:T(8,128)(2,1)} %kvw_ref.3) | copy-start | bytes 3145732
  2.8 15.5 %all-to-all-start = ((bf16[16,80,128]{2,1,0:T(8,128)(2,1)}), bf16[16,80,128]{2,1,0:T(8,128)(2,1)S(1)}, u32[]{:S(2)}, u32[]{:S(2)}) async-start(bf16[16,80,128]{2,1,0:T(8,128)(2,1)} %shard_map.94), calls=%async_computation | async-start | bytes 655360 | tf_op jit(solution)/shard_map/all_to_all | solution.py:240
  11.4 0.9 copy-start.1
  12.3 0.7 copy-start.4
  13.0 0.7 copy-start.5
  14.2 0.6 copy-start.2
  18.3 0.8 copy-start.3

commit v2 on v1

v2 whole, which is shorter than its diff:
```python
import functools

import jax
import jax.numpy as jnp
from jax import lax
from jax.experimental import pallas as pl
from jax.experimental.pallas import tpu as pltpu
from jax.sharding import PartitionSpec as P

HEADS = 16
SCORE_SCALE = 0.125
EPSILON = 1e-05
MASKED = -1e30
BF16 = jnp.bfloat16
F32 = jnp.float32

LEVELS = 13
TOK = 128
PAIRS = 7
WIDE = 2 * TOK
SPAN = PAIRS * WIDE
D = 512
HEAD = D // HEADS
FEAT = 80
AUG = 96
LATENT = 3
AH = LATENT * HEADS
GS = 128
NT = (((1,), (1,)), ((), ()))
RING = 16
ZED = 8
HALF = D // 2
ROW = 2 * D + TOK
SHARE = 48

VMEM = pl.BlockSpec(memory_space=pltpu.VMEM)
SMEM = pl.BlockSpec(memory_space=pltpu.SMEM)


def params(mib):
    return pltpu.CompilerParams(vmem_limit_bytes=mib * 1024 * 1024)


def shape(*dims, dtype=BF16):
    return jax.ShapeDtypeStruct(dims, dtype)


def slot_kernel(lon_ref, patch_ref, slot_ref):
    lon = lon_ref[0]
    for i in range(LEVELS):
        owner = lax.rem(lon * LEVELS + i, RING)
        slot_ref[owner] = patch_ref[:, i * TOK : (i + 1) * TOK]


def feature_of(position):
    core, z, lon, pair = position >> 8, (position >> 5) & 7, (position >> 1) & 15, position & 1
    return lon * 32 + z * 4 + core * 2 + pair


def prep_kernel(
    core_ref, kvw_ref, embed_w_ref, level_ref, query_ref, grad_ref,
    tall_ref, wide_ref,
    rows, spread,
):
    core = core_ref[0]
    down = lax.broadcasted_iota(jnp.int32, (D, D), 0)
    across = lax.broadcasted_iota(jnp.int32, (D, D), 1)
    reorder = jnp.where(feature_of(down) == across, 1.0, 0.0).astype(BF16)
    side = (core + (down >> 8)) & 1
    target = ((down >> 5) & 7) * 64 + side * 32 + (down & 31)
    wide_ref[:, 2 * D : 3 * D] = jnp.where(feature_of(across) == target, 1.0, 0.0).astype(BF16)
    for c in range(4):
        part = jnp.dot(reorder, kvw_ref[:, c * 256 : (c + 1) * 256], preferred_element_type=F32)
        wide_ref[:, c * 256 : (c + 1) * 256] = part.astype(BF16)
        tall_ref[c * 256 : (c + 1) * 256, :] = part.T.astype(BF16)
    rows[...] = jnp.zeros_like(rows)
    rows[:FEAT, :] = embed_w_ref[...].astype(F32)
    rows[FEAT : FEAT + LEVELS, :] = level_ref[...].astype(F32)
    weights = rows[...]
    weights = weights - jnp.mean(weights, axis=1, keepdims=True)
    high = weights.astype(BF16)
    spread[...] = jnp.zeros_like(spread)
    spread[:AUG, :] = high.astype(F32)
    spread[AUG : 2 * AUG, :] = weights - high.astype(F32)
    wide_ref[:, 3 * D : 3 * D + 256] = jnp.dot(
        reorder, spread[...].T.astype(BF16), preferred_element_type=F32
    ).astype(BF16)
    head = lax.broadcasted_iota(jnp.int32, (HEADS, D), 0)
    owner = lax.broadcasted_iota(jnp.int32, (HEADS, D), 1) >> 5
    spread[:32, :] = jnp.zeros((32, D), F32)
    for a in range(LATENT):
        block = jnp.where(head == owner, query_ref[a : a + 1, :].astype(F32), 0.0)
        spread[32 + a * HEADS : 32 + (a + 1) * HEADS, :] = block
        spread[80 + a * HEADS : 80 + (a + 1) * HEADS, :] = block
    tall_ref[2 * D : 2 * D + AH, :] = spread[80:128, :].astype(BF16)
    tall_ref[2 * D + AH :, :] = jnp.zeros((16, D), BF16)
    wide_ref[:, 3 * D + 256 : 3 * D + 384] = spread[:GS, :].T.astype(BF16)
    for a in range(LATENT):
        at = 4 * D + a * TOK
        wide_ref[:, at : at + TOK] = grad_ref[a].astype(F32).T.astype(BF16)


def main_kernel(
    place_ref, count_ref, recv_ref, tall_ref, wide_ref,
    keep_out, send_out,
    g2, paug_s, hid_s, kv_s, gkv_s, ge_s, nrm_s, inv_s, sc_s, ga_s, w_s, gs_s,
):
    lon = place_ref[0]
    core = place_ref[1]
    count = count_ref[0]
    for a in range(LATENT):
        wide = wide_ref[:, 4 * D + a * TOK : 4 * D + (a + 1) * TOK].astype(F32)
        g2[a, :, :TOK] = wide
        g2[a, :, TOK:] = wide
    gs_s[:32, :] = jnp.zeros((32, SPAN), BF16)

    def embed(p):
        at = slice(p * WIDE, (p + 1) * WIDE)
        first, second = 2 * p, min(2 * p + 1, LEVELS - 1)
        patches = jnp.concatenate(
            [recv_ref[(RING * first + lon) // LEVELS], recv_ref[(RING * second + lon) // LEVELS]], axis=1
        )
        row = lax.broadcasted_iota(jnp.int32, (AUG - FEAT, WIDE), 0)
        lane = lax.broadcasted_iota(jnp.int32, (AUG - FEAT, WIDE), 1)
        level = jnp.where(lane >= TOK, second, first)
        one_hot = jnp.where(row == level, 1.0, 0.0).astype(BF16)
        paug_s[:FEAT, at] = patches
        paug_s[FEAT:AUG, at] = one_hot
        paug_s[AUG : AUG + FEAT, at] = patches
        paug_s[AUG + FEAT :, at] = one_hot
        center = jnp.dot(
            wide_ref[:, 3 * D : 3 * D + 2 * AUG], paug_s[:, at], preferred_element_type=F32
        )
        inv_std = lax.rsqrt(jnp.mean(center * center, axis=0, keepdims=True) + EPSILON)
        normed = center * inv_std
        inv_s[:, at] = inv_std
        nrm_s[:, at] = normed
        hid_s[:, at] = normed.astype(BF16)

    def score(p):
        at = slice(p * WIDE, (p + 1) * WIDE)
        kv_s[:, at] = jnp.dot(tall_ref[: 2 * D, :], hid_s[:, at], preferred_element_type=F32).astype(BF16)
        sc_s[:, at] = (
            jnp.dot(tall_ref[2 * D : 2 * D + AH, :], kv_s[:D, at], preferred_element_type=F32) * SCORE_SCALE
        )
        values = kv_s[D:, at].astype(F32)
        for a in range(LATENT):
            product = (g2[a] * values).reshape(HEADS, HEAD, WIDE)
            ga_s[a * HEADS : (a + 1) * HEADS, at] = jnp.sum(product, axis=1)

    embed(0)
    for p in range(PAIRS):
        if p + 1 < PAIRS:
            embed(p + 1)
        score(p)

    masked = [
        jnp.where(l < count, sc_s[:, l * TOK : (l + 1) * TOK], MASKED) for l in range(LEVELS)
    ]
    peak = functools.reduce(jnp.maximum, masked)
    total = jnp.zeros_like(peak)
    for l in range(LEVELS):
        exponent = jnp.exp(masked[l] - peak)
        sc_s[:, l * TOK : (l + 1) * TOK] = exponent
        total = total + exponent
    inverse = 1.0 / total
    inner = jnp.zeros_like(peak)
    for l in range(LEVELS):
        lanes = slice(l * TOK, (l + 1) * TOK)
        attention = sc_s[:, lanes] * inverse
        sc_s[:, lanes] = attention
        w_s[:, lanes] = attention.astype(BF16).astype(F32)
        inner = inner + attention * ga_s[:, lanes]
    for l in range(LEVELS):
        lanes = slice(l * TOK, (l + 1) * TOK)
        grad_score = sc_s[:, lanes] * (ga_s[:, lanes] - inner) * SCORE_SCALE
        high = grad_score.astype(BF16)
        gs_s[32:80, lanes] = (grad_score - high.astype(F32)).astype(BF16)
        gs_s[80:, lanes] = high
    tail = slice(LEVELS * TOK, SPAN)
    w_s[:, tail] = jnp.zeros((AH, TOK), F32)
    gs_s[32:, tail] = jnp.zeros((2 * AH, TOK), BF16)

    def grad_kv(p):
        at = slice(p * WIDE, (p + 1) * WIDE)
        gkv_s[:D, at] = jnp.dot(
            wide_ref[:, 3 * D + 256 : 3 * D + 384], gs_s[:, at], preferred_element_type=F32
        ).astype(BF16)
        grad_values = None
        for a in range(LATENT):
            weight = w_s[a * HEADS : (a + 1) * HEADS, at].reshape(HEADS, 1, WIDE)
            term = weight * g2[a].reshape(HEADS, HEAD, WIDE)
            grad_values = term if grad_values is None else grad_values + term
        gkv_s[D:, at] = grad_values.reshape(D, WIDE).astype(BF16)

    def embed_back(p):
        at = slice(p * WIDE, (p + 1) * WIDE)
        grad_hidden = jnp.dot(wide_ref[:, : 2 * D], gkv_s[:, at], preferred_element_type=F32)
        normed = nrm_s[:, at]
        mean = jnp.mean(grad_hidden, axis=0, keepdims=True)
        slope = jnp.mean(grad_hidden * normed, axis=0, keepdims=True)
        ge_s[:, at] = (inv_s[:, at] * (grad_hidden - mean - normed * slope)).astype(BF16)

    grad_kv(0)
    for p in range(PAIRS):
        if p + 1 < PAIRS:
            grad_kv(p + 1)
        embed_back(p)

    mine = hid_s[pl.ds(pl.multiple_of(core * HALF, HALF), HALF), :]
    other = hid_s[pl.ds(pl.multiple_of((1 - core) * HALF, HALF), HALF), :]
    for c in range(4):
        at = slice(c * WIDE, (c + 1) * WIDE)
        send_out[:, at] = lax.dot_general(other, gkv_s[at, :], NT, preferred_element_type=F32).astype(BF16)
        keep_out[:, at] = lax.dot_general(mine, gkv_s[at, :], NT, preferred_element_type=F32)
    grads = lax.dot_general(ge_s[...], paug_s[:GS, :], NT, preferred_element_type=F32).astype(BF16)
    grads = jnp.dot(wide_ref[:, 2 * D : 3 * D], grads, preferred_element_type=F32)
    queries = lax.dot_general(kv_s[:D, :], gs_s[...], NT, preferred_element_type=F32)
    head = lax.broadcasted_iota(jnp.int32, (D, GS), 0) >> 5
    lane = lax.broadcasted_iota(jnp.int32, (D, GS), 1)
    queries = jnp.where((lane & 15) == head, queries, 0.0).reshape(HEADS, HEAD, GS)
    queries = jnp.sum(queries, axis=0)
    queries = queries + pltpu.roll(queries, AH, 1)
    queries = jnp.concatenate([queries] * HEADS, axis=0)
    block = jnp.where(lane < FEAT, grads, queries)
    keep_out[:, 2 * D :] = block[:HALF]
    send_out[:, 2 * D :] = block[HALF:].astype(BF16)


def pair_kernel(keep_ref, recv_ref, sum_ref):
    sum_ref[...] = (keep_ref[...] + recv_ref[...].astype(F32)).astype(BF16)


def sum_z_kernel(part_ref, share_ref, total, tile):
    acc = part_ref[0].astype(F32)
    for source in range(1, ZED):
        acc = acc + part_ref[source].astype(F32)
    total[...] = acc
    block = acc[:, 2 * D :].astype(BF16)
    for target in range(RING):
        for c in range(8):
            tile[target, 2 * c : 2 * c + 2, :] = total[2 * target : 2 * target + 2, c * TOK : (c + 1) * TOK]
        share_ref[target, 0:16, :] = tile[target].astype(BF16)
        share_ref[target, 16:48, :] = block


def sum_lon_kernel(share_ref, kv_out, embed_out, query_out, tile, turned):
    acc = share_ref[0].astype(F32)
    for source in range(1, RING):
        acc = acc + share_ref[source].astype(F32)
    tile[...] = acc[:16]
    for c in range(8):
        kv_out[:, c * TOK : (c + 1) * TOK] = tile[2 * c : 2 * c + 2, :]
    embed_out[...] = acc[16:, :FEAT]
    turned[...] = acc[16:, :].T
    for a in range(LATENT):
        for h in range(HEADS):
            at = FEAT + a * HEADS + h
            query_out[a : a + 1, h * HEAD : (h + 1) * HEAD] = turned[at : at + 1, :]


def on_device(level_patches, level_embed, embed_weight, kv_weight, query, band_levels, grad_out):
    lon = lax.axis_index("lon").astype(jnp.int32)
    core = (lax.axis_index("lat") % 2).astype(jnp.int32)
    place = jnp.stack([lon, core])
    slots = pl.pallas_call(
        slot_kernel,
        out_shape=shape(RING, FEAT, TOK),
        in_specs=[SMEM, VMEM],
        out_specs=VMEM,
        compiler_params=params(16),
        name="slots",
    )(lon.reshape(1), level_patches[0].T)
    tall, wide = pl.pallas_call(
        prep_kernel,
        out_shape=(shape(2 * D + 64, D), shape(D, 4 * D + LATENT * TOK)),
        in_specs=[SMEM] + [VMEM] * 5,
        out_specs=(VMEM,) * 2,
        scratch_shapes=[pltpu.VMEM((AUG, D), F32), pltpu.VMEM((256, D), F32)],
        compiler_params=params(24),
        name="prep",
    )(core.reshape(1), kv_weight, embed_weight, level_embed, query, grad_out[0].transpose(1, 0, 2))
    recv = lax.all_to_all(slots, "lon", 0, 0, tiled=True)
    keep, send = pl.pallas_call(
        main_kernel,
        out_shape=(shape(HALF, ROW, dtype=F32), shape(HALF, ROW)),
        in_specs=[SMEM, SMEM] + [VMEM] * 3,
        out_specs=(VMEM,) * 2,
        scratch_shapes=[
            pltpu.VMEM((LATENT, D, WIDE), F32),
            pltpu.VMEM((2 * AUG, SPAN), BF16),
            pltpu.VMEM((D, SPAN), BF16),
            pltpu.VMEM((2 * D, SPAN), BF16),
            pltpu.VMEM((2 * D, SPAN), BF16),
            pltpu.VMEM((D, SPAN), BF16),
            pltpu.VMEM((D, SPAN), F32),
            pltpu.VMEM((1, SPAN), F32),
            pltpu.VMEM((AH, SPAN), F32),
            pltpu.VMEM((AH, SPAN), F32),
            pltpu.VMEM((AH, SPAN), F32),
            pltpu.VMEM((GS, SPAN), BF16),
        ],
        compiler_params=params(28),
        name="main",
    )(place, band_levels, recv, tall, wide)
    lats = lax.axis_size("lat")
    other = lax.ppermute(send, "lat", [(i, i ^ 1) for i in range(lats)])
    paired = pl.pallas_call(
        pair_kernel,
        out_shape=shape(HALF, ROW),
        in_specs=[VMEM] * 2,
        out_specs=VMEM,
        compiler_params=params(16),
        name="pair",
    )(keep, other)
    parts = lax.all_to_all(
        paired.reshape(ZED, HALF // ZED, ROW),
        "lat",
        0,
        0,
        tiled=True,
        axis_index_groups=[[2 * z + c for z in range(ZED)] for c in range(2)],
    )
    share = pl.pallas_call(
        sum_z_kernel,
        out_shape=shape(RING, SHARE, TOK),
        in_specs=[VMEM],
        out_specs=VMEM,
        scratch_shapes=[pltpu.VMEM((HALF // ZED, ROW), F32), pltpu.VMEM((RING, 16, TOK), F32)],
        compiler_params=params(16),
        name="sum_z",
    )(parts)
    shared = lax.all_to_all(share, "lon", 0, 0, tiled=True)
    kv_grad, embed_grad, query_grad = pl.pallas_call(
        sum_lon_kernel,
        out_shape=(shape(2, 2 * D, dtype=F32), shape(32, FEAT, dtype=F32), shape(LATENT, D, dtype=F32)),
        in_specs=[VMEM],
        out_specs=(VMEM,) * 3,
        scratch_shapes=[pltpu.VMEM((16, TOK), F32), pltpu.VMEM((TOK, 32), F32)],
        compiler_params=params(16),
        name="sum_lon",
    )(shared)
    return (kv_grad, embed_grad.T, query_grad)


def solution(mesh):
    placed = (P("lat", "lon", None), P(), P(), P(), P(), P("lat"), P("lat", "lon", None, None))
    return jax.shard_map(
        on_device,
        mesh=mesh,
        in_specs=placed,
        out_specs=(P(("lon", "lat"), None), P(None, "lat"), P()),
        check_vma=False,
    )
```

time: 92.2 us -> 74.1 us (0.80)
  blocking collectives: 52.2 us -> 36.6 us
  Pallas kernels: 21.1 us -> 16.2 us
  starting transfers between devices: 7.72 us -> 9.96 us
  local copies, waits for them, and re-layouts: 5.81 us -> 4.47 us
  waiting for transfers between devices: 3.51 us -> 4.79 us
    all_to_all x2 -> x1, blocking collectives: 41.6 us -> 26.4 us  [on_device(): lax.all_to_all(paired.reshape(ZED, HALF // ZED, ROW), 'lat', 0, 0, tiled=...]
    pallas_call x5, Pallas kernels: 20.1 us -> 15.4 us  [the longest x1 12.6 us: on_device(): pl.pallas_call(main_kernel, out_shape=(shape(HALF, ROW, dtype=F32), shape...]
    ppermute x0 -> x1, starting transfers between devices: none -> 2.38 us  [on_device(): other = lax.ppermute(send, 'lat', [(i, i ^ 1) for i in range(lats)])]
    ppermute x0 -> x1, waiting for transfers between devices: none -> 1.63 us  [on_device(): other = lax.ppermute(send, 'lat', [(i, i ^ 1) for i in range(lats)])]
    unnamed x17 -> x16, local copies, waits for them, and re-layouts: 5.63 us -> 4.47 us
  transfers between devices with their start and end apart: 1 -> 2, of which waited for: 1 -> 2; matrix products, arithmetic and copies ran while one was open for 0% -> 0% of each run, Pallas kernels for 1% -> 2%
where the time goes in v2:
time: 74.1 us; the launch traced here: 73.5 us
  blocking collectives  36.6 us (49%)
  Pallas kernels  16.2 us (22%)
  starting transfers between devices  9.96 us (13%)
  waiting for transfers between devices  4.79 us (6%)
  local copies, waits for them, and re-layouts  4.47 us (6%)
  between operations  1.39 us (2%)
    all_to_all x1, blocking collectives, on_device(): lax.all_to_all(paired.reshape(ZED, HALF // ZED, ROW), 'lat', 0, 0, tiled=...  26.4 us
    pallas_call x1, Pallas kernels, on_device(): pl.pallas_call(main_kernel, out_shape=(shape(HALF, ROW, dtype=F32), shape...  12.6 us
    all_to_all x1, blocking collectives, on_device(): shared = lax.all_to_all(share, 'lon', 0, 0, tiled=True)  10.2 us
    all_to_all x1, starting transfers between devices, on_device(): recv = lax.all_to_all(slots, 'lon', 0, 0, tiled=True)  7.58 us
    unnamed x16, local copies, waits for them, and re-layouts  4.47 us
    all_to_all x1, waiting for transfers between devices, on_device(): recv = lax.all_to_all(slots, 'lon', 0, 0, tiled=True)  3.16 us
    ppermute x1, starting transfers between devices, on_device(): other = lax.ppermute(send, 'lat', [(i, i ^ 1) for i in range(lats)])  2.38 us
    pallas_call x1, Pallas kernels, on_device(): pl.pallas_call(prep_kernel, out_shape=(shape(2 * D + 64, D), shape(D, 4 *...  1.65 us
  transfers between devices with their start and end apart: 2, of which 2 were waited for; matrix products, arithmetic and copies ran while one was open for 0% of the time, Pallas kernels for 2%

profile of v2, /device:TPU:1, one launch (start us, length us, event | category | flops | bytes accessed | tf_op | source)
XLA Modules:
  0.0 73.5 jit_solution(6762204822960007837)
XLA Ops:
  0.6 0.0 copy-start.3
  0.6 0.0 copy-start.4
  0.7 1.0 %copy-done.4 = bf16[1,1664,80]{1,2,0:T(8,128)(2,1)S(1)} copy-done((bf16[1,1664,80]{1,2,0:T(8,128)(2,1)S(1)}, bf16[1,1664,80]{1,2,0:T(8,128)(2,1)}, u32[]{:S(2)}) %copy-start.4) | copy-done | bytes 266264
  1.7 0.8 %slots.1 = bf16[16,80,128]{2,1,0:T(8,128)(2,1)} custom-call(s32[1]{0:T(128)} %bitcast.lon_ref, bf16[80,1664]{1,0:T(8,128)(2,1)S(1)} %bitcast.12), custom_call_target="tpu_custom_call" | custom-call | tf_op jit(solution)/shard_map/slots/pallas_call | solution.py:266
  2.5 7.6 %all-to-all-start = ((bf16[16,80,128]{2,1,0:T(8,128)(2,1)}), bf16[16,80,128]{2,1,0:T(8,128)(2,1)S(1)}, u32[]{:S(2)}, u32[]{:S(2)}) async-start(bf16[16,80,128]{2,1,0:T(8,128)(2,1)} %slots.1), calls=%async_computation | async-start | bytes 655360 | tf_op jit(solution)/shard_map/all_to_all | solution.py:283
  10.7 0.0 copy-done.3
  10.7 0.0 copy-done.5
  10.7 0.0 copy-done.6
  10.7 0.0 copy-done.7
  10.7 0.0 copy-start.2
  10.8 1.2 %copy-done.2 = bf16[512,1024]{1,0:T(8,128)(2,1)S(1)} copy-done((bf16[512,1024]{1,0:T(8,128)(2,1)S(1)}, bf16[512,1024]{1,0:T(8,128)(2,1)}, u32[]{:S(2)}) %copy-start.2) | copy-done | bytes 1048600
  12.0 1.7 %prep.1 = (bf16[1088,512]{1,0:T(8,128)(2,1)S(1)}, bf16[512,2432]{1,0:T(8,128)(2,1)S(1)}) custom-call(s32[1]{0:T(128)} %bitcast.1.core_ref, bf16[512,1024]{1,0:T(8,128)(2,1)S(1)} %copy-done.2, bf16[80,512]{1,0:T(8,128)(2,1)S(1)} %copy-done.5, bf16[13,512]{1,0:T(8,128)(2,1)S(1)} %copy-done.6, bf16[3,512]{1,0:T(4,128)(2,1)S(1)} %copy-done.7, ...), custom_call_target="tpu_custom_call" | custom-call | tf_op jit(solution)/shard_map/prep/pallas_call | solution.py:274
  13.6 1.0 %copy-done = bf16[1088,512]{1,0:T(8,128)(2,1)} copy-done((bf16[1088,512]{1,0:T(8,128)(2,1)}, bf16[1088,512]{1,0:T(8,128)(2,1)S(1)}, u32[]{:S(2)}) %copy-start) | copy-done | bytes 1114136
  14.6 0.1 pad_add_fusion.place_ref
  14.7 3.2 %all-to-all-done.recv_ref = bf16[16,80,128]{2,1,0:T(8,128)(2,1)S(1)} async-done(((bf16[16,80,128]{2,1,0:T(8,128)(2,1)}), bf16[16,80,128]{2,1,0:T(8,128)(2,1)S(1)}, u32[]{:S(2)}, u32[]{:S(2)}) %all-to-all-start) | async-done | bytes 327712 | tf_op jit(solution)/shard_map/all_to_all | solution.py:283
  17.9 1.2 %copy-done.1 = bf16[1088,512]{1,0:T(8,128)(2,1)S(1)} copy-done((bf16[1088,512]{1,0:T(8,128)(2,1)S(1)}, bf16[1088,512]{1,0:T(8,128)(2,1)}, u32[]{:S(2)}) %copy-start.1) | copy-done | bytes 1114136
  19.1 12.6 %main.1 = (f32[256,1152]{1,0:T(8,128)S(1)}, bf16[256,1152]{1,0:T(8,128)(2,1)S(1)}) custom-call(s32[2]{0:T(128)S(1)} %pad_add_fusion.place_ref, s32[1]{0:T(128)S(6)} %copy.10.count_ref, bf16[16,80,128]{2,1,0:T(8,128)(2,1)S(1)} %all-to-all-done.recv_ref, bf16[1088,512]{1,0:T(8,128)(2,1)S(1)} %copy-done.1, bf16[512,2432]{1,0:T(8,128)(2,1)S(1)} %get-tuple-element.11.wide_ref), custom_call_target="tpu_custom_call" | custom-call | tf_op jit(solution)/shard_map/main/pallas_call | solution.py:284
  31.8 2.4 %collective-permute-start = (bf16[256,1152]{1,0:T(8,128)(2,1)S(1)}, bf16[256,1152]{1,0:T(8,128)(2,1)S(1)}, u32[]{:S(2)}, u32[]{:S(2)}) collective-permute-start(bf16[256,1152]{1,0:T(8,128)(2,1)S(1)} %get-tuple-element.13), channel_id=1, source_target_pairs={{0,1},{1,0},{2,3},{3,2},{4,5},{5,4},{6,7},{7,6},{8,9},{9,8},{10,11... | collective-permute-start | bytes 1769480 | tf_op jit(solution)/shard_map/ppermute | solution.py:307
  34.2 1.6 %collective-permute-done.recv_ref = bf16[256,1152]{1,0:T(8,128)(2,1)S(1)} collective-permute-done((bf16[256,1152]{1,0:T(8,128)(2,1)S(1)}, bf16[256,1152]{1,0:T(8,128)(2,1)S(1)}, u32[]{:S(2)}, u32[]{:S(2)}) %collective-permute-start) | collective-permute-done | bytes 589856 | tf_op jit(solution)/shard_map/ppermute | solution.py:307
  35.8 0.1 pair.1
  35.9 26.4 %all_to_all.15.part_ref = bf16[8,32,1152]{2,1,0:T(8,128)(2,1)S(1)} all-to-all(bf16[8,32,1152]{2,1,0:T(8,128)(2,1)S(1)} %bitcast.10), channel_id=1, replica_groups={{0,2,4,6,8,10,12,14},{1,3,5,7,9,11,13,15},{16,18,20,22,24,26,28,30},{17..., dimensions={0} | all-to-all | bytes 1179648 | tf_op jit(solution)/shard_map/all_to_all | solution.py:316
  62.3 0.2 sum_z.1
  62.5 10.2 %all_to_all.16.share_ref = bf16[16,48,128]{2,1,0:T(8,128)(2,1)S(1)} all-to-all(bf16[16,48,128]{2,1,0:T(8,128)(2,1)S(1)} %sum_z.1), channel_id=1, replica_groups=mesh['lon'=16,'lat'=16] {'lon'}, dimensions={0} | all-to-all | bytes 393216 | tf_op jit(solution)/shard_map/all_to_all | solution.py:333
  72.7 0.8 %sum_lon.1 = (f32[2,1024]{1,0:T(2,128)}, f32[32,80]{1,0:T(8,128)}, f32[3,512]{1,0:T(4,128)}) custom-call(bf16[16,48,128]{2,1,0:T(8,128)(2,1)S(1)} %all_to_all.16.share_ref), custom_call_target="tpu_custom_call" | custom-call | tf_op jit(solution)/shard_map/sum_lon/pallas_call | solution.py:334
  (5 shorter events, 0.0 us)
Async XLA Ops:
  0.6 10.1 %copy-start.3 = (bf16[1,128,3,512]{3,1,2,0:T(8,128)(2,1)S(1)}, bf16[1,128,3,512]{3,1,2,0:T(8,128)(2,1)}, u32[]{:S(2)}) copy-start(bf16[1,128,3,512]{3,1,2,0:T(8,128)(2,1)} %param.13) | copy-start | bytes 1179652
  0.6 1.0 %copy-start.4 = (bf16[1,1664,80]{1,2,0:T(8,128)(2,1)S(1)}, bf16[1,1664,80]{1,2,0:T(8,128)(2,1)}, u32[]{:S(2)}) copy-start(bf16[1,1664,80]{1,2,0:T(8,128)(2,1)} %param.7) | copy-start | bytes 798724
  1.6 9.1 %copy-start.5 = (bf16[80,512]{1,0:T(8,128)(2,1)S(1)}, bf16[80,512]{1,0:T(8,128)(2,1)}, u32[]{:S(2)}) copy-start(bf16[80,512]{1,0:T(8,128)(2,1)} %embed_w_ref.1) | copy-start | bytes 245764
  1.7 9.1 %copy-start.6 = (bf16[13,512]{1,0:T(8,128)(2,1)S(1)}, bf16[13,512]{1,0:T(8,128)(2,1)}, u32[]{:S(2)}) copy-start(bf16[13,512]{1,0:T(8,128)(2,1)} %level_ref.1) | copy-start | bytes 39940
  1.7 9.1 %copy-start.7 = (bf16[3,512]{1,0:T(4,128)(2,1)S(1)}, bf16[3,512]{1,0:T(4,128)(2,1)}, u32[]{:S(2)}) copy-start(bf16[3,512]{1,0:T(4,128)(2,1)} %query_ref.1) | copy-start | bytes 9220
  2.5 15.4 %all-to-all-start = ((bf16[16,80,128]{2,1,0:T(8,128)(2,1)}), bf16[16,80,128]{2,1,0:T(8,128)(2,1)S(1)}, u32[]{:S(2)}, u32[]{:S(2)}) async-start(bf16[16,80,128]{2,1,0:T(8,128)(2,1)} %slots.1), calls=%async_computation | async-start | bytes 655360 | tf_op jit(solution)/shard_map/all_to_all | solution.py:283
  10.7 1.2 %copy-start.2 = (bf16[512,1024]{1,0:T(8,128)(2,1)S(1)}, bf16[512,1024]{1,0:T(8,128)(2,1)}, u32[]{:S(2)}) copy-start(bf16[512,1024]{1,0:T(8,128)(2,1)} %kvw_ref.1) | copy-start | bytes 3145732
  13.6 1.0 %copy-start = (bf16[1088,512]{1,0:T(8,128)(2,1)}, bf16[1088,512]{1,0:T(8,128)(2,1)S(1)}, u32[]{:S(2)}) copy-start(bf16[1088,512]{1,0:T(8,128)(2,1)S(1)} %get-tuple-element.10.tall_ref) | copy-start | bytes 3342340
  17.9 1.2 %copy-start.1 = (bf16[1088,512]{1,0:T(8,128)(2,1)S(1)}, bf16[1088,512]{1,0:T(8,128)(2,1)}, u32[]{:S(2)}) copy-start(bf16[1088,512]{1,0:T(8,128)(2,1)} %copy-done) | copy-start | bytes 3342340
  31.8 4.0 %collective-permute-start = (bf16[256,1152]{1,0:T(8,128)(2,1)S(1)}, bf16[256,1152]{1,0:T(8,128)(2,1)S(1)}, u32[]{:S(2)}, u32[]{:S(2)}) collective-permute-start(bf16[256,1152]{1,0:T(8,128)(2,1)S(1)} %get-tuple-element.13), channel_id=1, source_target_pairs={{0,1},{1,0},{2,3},{3,2},{4,5},{5,4},{6,7},{7,6},{8,9},{9,8},{10,11... | collective-permute-start | bytes 1769480 | tf_op jit(solution)/shard_map/ppermute | solution.py:307

commit v3 on v2

--- a/solution.py
+++ b/solution.py
@@ -30,8 +30,9 @@
 RING = 16
 ZED = 8
 HALF = D // 2
-ROW = 2 * D + TOK
-SHARE = 48
+PACKED = 768
+SHARE = 80
+LAST = 48
 
 VMEM = pl.BlockSpec(memory_space=pltpu.VMEM)
 SMEM = pl.BlockSpec(memory_space=pltpu.SMEM)
@@ -53,7 +54,7 @@
 
 
 def feature_of(position):
-    core, z, lon, pair = position >> 8, (position >> 5) & 7, (position >> 1) & 15, position & 1
+    core, lon, z, pair = position >> 8, (position >> 4) & 15, (position >> 1) & 7, position & 1
     return lon * 32 + z * 4 + core * 2 + pair
 
 
@@ -102,7 +103,7 @@
 
 def main_kernel(
     place_ref, count_ref, recv_ref, tall_ref, wide_ref,
-    keep_out, send_out,
+    keep_out, block_out, send_out,
     g2, paug_s, hid_s, kv_s, gkv_s, ge_s, nrm_s, inv_s, sc_s, ga_s, w_s, gs_s,
 ):
     lon = place_ref[0]
@@ -211,7 +212,7 @@
     other = hid_s[pl.ds(pl.multiple_of((1 - core) * HALF, HALF), HALF), :]
     for c in range(4):
         at = slice(c * WIDE, (c + 1) * WIDE)
-        send_out[:, at] = lax.dot_general(other, gkv_s[at, :], NT, preferred_element_type=F32).astype(BF16)
+        send_out[:HALF, at] = lax.dot_general(other, gkv_s[at, :], NT, preferred_element_type=F32).astype(BF16)
         keep_out[:, at] = lax.dot_general(mine, gkv_s[at, :], NT, preferred_element_type=F32)
     grads = lax.dot_general(ge_s[...], paug_s[:GS, :], NT, preferred_element_type=F32).astype(BF16)
     grads = jnp.dot(wide_ref[:, 2 * D : 3 * D], grads, preferred_element_type=F32)
@@ -220,34 +221,54 @@
     lane = lax.broadcasted_iota(jnp.int32, (D, GS), 1)
     queries = jnp.where((lane & 15) == head, queries, 0.0).reshape(HEADS, HEAD, GS)
     queries = jnp.sum(queries, axis=0)
-    queries = queries + pltpu.roll(queries, AH, 1)
-    queries = jnp.concatenate([queries] * HEADS, axis=0)
-    block = jnp.where(lane < FEAT, grads, queries)
-    keep_out[:, 2 * D :] = block[:HALF]
-    send_out[:, 2 * D :] = block[HALF:].astype(BF16)
-
-
-def pair_kernel(keep_ref, recv_ref, sum_ref):
-    sum_ref[...] = (keep_ref[...] + recv_ref[...].astype(F32)).astype(BF16)
-
-
-def sum_z_kernel(part_ref, share_ref, total, tile):
-    acc = part_ref[0].astype(F32)
-    for source in range(1, ZED):
-        acc = acc + part_ref[source].astype(F32)
-    total[...] = acc
-    block = acc[:, 2 * D :].astype(BF16)
+    queries = queries[:, 80:GS] + queries[:, 32:80]
+    blank = jnp.zeros((HEAD, PACKED - ZED * FEAT - AH), F32)
+
+    def packed(half):
+        parts = [grads[half * HALF + z * HEAD : half * HALF + (z + 1) * HEAD, :FEAT] for z in range(ZED)]
+        return jnp.concatenate(parts + [queries, blank], axis=1)
+
+    block_out[...] = packed(0)
+    send_out[HALF:, :PACKED] = packed(1).astype(BF16)
+    send_out[HALF:, PACKED:] = jnp.zeros((HEAD, 2 * D - PACKED), BF16)
+
+
+def pair_kernel(keep_ref, block_ref, recv_ref, share_ref):
     for target in range(RING):
-        for c in range(8):
-            tile[target, 2 * c : 2 * c + 2, :] = total[2 * target : 2 * target + 2, c * TOK : (c + 1) * TOK]
-        share_ref[target, 0:16, :] = tile[target].astype(BF16)
-        share_ref[target, 16:48, :] = block
-
-
-def sum_lon_kernel(share_ref, kv_out, embed_out, query_out, tile, turned):
+        rows = slice(target * 16, (target + 1) * 16)
+        total = (keep_ref[rows, :] + recv_ref[rows, :].astype(F32)).astype(BF16)
+        share_ref[target, 0:16, :] = total[:, :D]
+        share_ref[target, 16:32, :] = total[:, D:]
+    block = (block_ref[...] + recv_ref[HALF:, :PACKED].astype(F32)).astype(BF16)
+    for target in range(RING):
+        share_ref[target, 32:64, :] = block[:, :D]
+        share_ref[target, 64:80, :256] = block[:16, D:PACKED]
+        share_ref[target, 64:80, 256:] = block[16:, D:PACKED]
+
+
+def sum_lon_kernel(share_ref, last_ref, total, tile):
     acc = share_ref[0].astype(F32)
     for source in range(1, RING):
         acc = acc + share_ref[source].astype(F32)
+    total[...] = acc[:32]
+    block = jnp.concatenate(
+        [acc[32:64], jnp.concatenate([acc[64:80, :256], acc[64:80, 256:]], axis=0)], axis=1
+    )
+    queries = block[:, ZED * FEAT : ZED * FEAT + AH]
+    for z in range(ZED):
+        for c in range(8):
+            row = 16 * (c // 4) + 2 * z
+            tile[z, 2 * c : 2 * c + 2, :] = total[row : row + 2, (c % 4) * TOK : (c % 4 + 1) * TOK]
+        last_ref[z, 0:16, :] = tile[z].astype(BF16)
+        last_ref[z, 16:48, :] = jnp.concatenate(
+            [block[:, z * FEAT : (z + 1) * FEAT], queries], axis=1
+        ).astype(BF16)
+
+
+def sum_z_kernel(last_ref, kv_out, embed_out, query_out, tile, turned):
+    acc = last_ref[0].astype(F32)
+    for source in range(1, ZED):
+        acc = acc + last_ref[source].astype(F32)
     tile[...] = acc[:16]
     for c in range(8):
         kv_out[:, c * TOK : (c + 1) * TOK] = tile[2 * c : 2 * c + 2, :]
@@ -281,11 +302,15 @@
         name="prep",
     )(core.reshape(1), kv_weight, embed_weight, level_embed, query, grad_out[0].transpose(1, 0, 2))
     recv = lax.all_to_all(slots, "lon", 0, 0, tiled=True)
-    keep, send = pl.pallas_call(
+    keep, block, send = pl.pallas_call(
         main_kernel,
-        out_shape=(shape(HALF, ROW, dtype=F32), shape(HALF, ROW)),
+        out_shape=(
+            shape(HALF, 2 * D, dtype=F32),
+            shape(HEAD, PACKED, dtype=F32),
+            shape(HALF + HEAD, 2 * D),
+        ),
         in_specs=[SMEM, SMEM] + [VMEM] * 3,
-        out_specs=(VMEM,) * 2,
+        out_specs=(VMEM,) * 3,
         scratch_shapes=[
             pltpu.VMEM((LATENT, D, WIDE), F32),
             pltpu.VMEM((2 * AUG, SPAN), BF16),
@@ -305,41 +330,41 @@
     )(place, band_levels, recv, tall, wide)
     lats = lax.axis_size("lat")
     other = lax.ppermute(send, "lat", [(i, i ^ 1) for i in range(lats)])
-    paired = pl.pallas_call(
+    share = pl.pallas_call(
         pair_kernel,
-        out_shape=shape(HALF, ROW),
-        in_specs=[VMEM] * 2,
+        out_shape=shape(RING, SHARE, D),
+        in_specs=[VMEM] * 3,
         out_specs=VMEM,
         compiler_params=params(16),
         name="pair",
-    )(keep, other)
-    parts = lax.all_to_all(
-        paired.reshape(ZED, HALF // ZED, ROW),
+    )(keep, block, other)
+    shared = lax.all_to_all(share, "lon", 0, 0, tiled=True)
+    last = pl.pallas_call(
+        sum_lon_kernel,
+        out_shape=shape(ZED, LAST, TOK),
+        in_specs=[VMEM],
+        out_specs=VMEM,
+        scratch_shapes=[pltpu.VMEM((32, D), F32), pltpu.VMEM((ZED, 16, TOK), F32)],
+        compiler_params=params(16),
+        name="sum_lon",
+    )(shared)
+    lasts = lax.all_to_all(
+        last,
         "lat",
         0,
         0,
         tiled=True,
         axis_index_groups=[[2 * z + c for z in range(ZED)] for c in range(2)],
     )
-    share = pl.pallas_call(
+    kv_grad, embed_grad, query_grad = pl.pallas_call(
         sum_z_kernel,
-        out_shape=shape(RING, SHARE, TOK),
-        in_specs=[VMEM],
-        out_specs=VMEM,
-        scratch_shapes=[pltpu.VMEM((HALF // ZED, ROW), F32), pltpu.VMEM((RING, 16, TOK), F32)],
-        compiler_params=params(16),
-        name="sum_z",
-    )(parts)
-    shared = lax.all_to_all(share, "lon", 0, 0, tiled=True)
-    kv_grad, embed_grad, query_grad = pl.pallas_call(
-        sum_lon_kernel,
         out_shape=(shape(2, 2 * D, dtype=F32), shape(32, FEAT, dtype=F32), shape(LATENT, D, dtype=F32)),
         in_specs=[VMEM],
         out_specs=(VMEM,) * 3,
         scratch_shapes=[pltpu.VMEM((16, TOK), F32), pltpu.VMEM((TOK, 32), F32)],
         compiler_params=params(16),
-        name="sum_lon",
-    )(shared)
+        name="sum_z",
+    )(lasts)
     return (kv_grad, embed_grad.T, query_grad)
 
 

time: 74.1 us -> 76.1 us (1.027)
  blocking collectives: 36.6 us -> 38.2 us
  local copies, waits for them, and re-layouts: 4.47 us -> 5.87 us
  waiting for transfers between devices: 4.79 us -> 3.43 us
    all_to_all x1, blocking collectives: 10.2 us -> 22.5 us  [on_device(): shared = lax.all_to_all(share, 'lon', 0, 0, tiled=True)]
    all_to_all x1, blocking collectives: 26.4 us -> 15.7 us  [on_device(): lax.all_to_all(last, 'lat', 0, 0, tiled=True, axis_index_groups=[[2 * z +...]
    unnamed x16, local copies, waits for them, and re-layouts: 4.47 us -> 5.87 us
    all_to_all x1, waiting for transfers between devices: 3.16 us -> 1.8 us  [on_device(): recv = lax.all_to_all(slots, 'lon', 0, 0, tiled=True)]
where the time goes in v3:
time: 76.1 us; the launch traced here: 75.3 us
  blocking collectives  38.2 us (50%)
  Pallas kernels  16.4 us (22%)
  starting transfers between devices  9.95 us (13%)
  local copies, waits for them, and re-layouts  5.87 us (8%)
  waiting for transfers between devices  3.43 us (5%)
  between operations  1.37 us (2%)
    all_to_all x1, blocking collectives, on_device(): shared = lax.all_to_all(share, 'lon', 0, 0, tiled=True)  22.5 us
    all_to_all x1, blocking collectives, on_device(): lax.all_to_all(last, 'lat', 0, 0, tiled=True, axis_index_groups=[[2 * z +...  15.7 us
    pallas_call x1, Pallas kernels, on_device(): pl.pallas_call(main_kernel, out_shape=(shape(HALF, 2 * D, dtype=F32), sha...  12.7 us
    all_to_all x1, starting transfers between devices, on_device(): recv = lax.all_to_all(slots, 'lon', 0, 0, tiled=True)  7.58 us
    unnamed x16, local copies, waits for them, and re-layouts  5.87 us
    ppermute x1, starting transfers between devices, on_device(): other = lax.ppermute(send, 'lat', [(i, i ^ 1) for i in range(lats)])  2.36 us
    all_to_all x1, waiting for transfers between devices, on_device(): recv = lax.all_to_all(slots, 'lon', 0, 0, tiled=True)  1.8 us
    ppermute x1, waiting for transfers between devices, on_device(): other = lax.ppermute(send, 'lat', [(i, i ^ 1) for i in range(lats)])  1.63 us
  transfers between devices with their start and end apart: 2, of which 2 were waited for; matrix products, arithmetic and copies ran while one was open for 0% of the time, Pallas kernels for 2%

profile of v3, /device:TPU:1, one launch (start us, length us, event | category | flops | bytes accessed | tf_op | source)
XLA Modules:
  0.0 75.3 jit_solution(18257197647239433301)
XLA Ops:
  0.6 0.0 copy-start.3
  0.6 0.0 copy-start.4
  0.7 1.0 %copy-done.4 = bf16[1,1664,80]{1,2,0:T(8,128)(2,1)S(1)} copy-done((bf16[1,1664,80]{1,2,0:T(8,128)(2,1)S(1)}, bf16[1,1664,80]{1,2,0:T(8,128)(2,1)}, u32[]{:S(2)}) %copy-start.4) | copy-done | bytes 266264
  1.6 0.8 %slots.1 = bf16[16,80,128]{2,1,0:T(8,128)(2,1)} custom-call(s32[1]{0:T(128)} %bitcast.lon_ref, bf16[80,1664]{1,0:T(8,128)(2,1)S(1)} %bitcast.10), custom_call_target="tpu_custom_call" | custom-call | tf_op jit(solution)/shard_map/slots/pallas_call | solution.py:287
  2.5 7.6 %all-to-all-start = ((bf16[16,80,128]{2,1,0:T(8,128)(2,1)}), bf16[16,80,128]{2,1,0:T(8,128)(2,1)S(1)}, u32[]{:S(2)}, u32[]{:S(2)}) async-start(bf16[16,80,128]{2,1,0:T(8,128)(2,1)} %slots.1), calls=%async_computation | async-start | bytes 655360 | tf_op jit(solution)/shard_map/all_to_all | solution.py:304
  10.7 0.0 copy-done.3
  10.7 0.0 copy-done.5
  10.7 0.0 copy-start.2
  10.7 1.2 %copy-done.2 = bf16[512,1024]{1,0:T(8,128)(2,1)S(1)} copy-done((bf16[512,1024]{1,0:T(8,128)(2,1)S(1)}, bf16[512,1024]{1,0:T(8,128)(2,1)}, u32[]{:S(2)}) %copy-start.2) | copy-done | bytes 1048600
  12.0 0.7 copy-done.6
  12.7 0.7 copy-done.7
  13.4 1.6 %prep.1 = (bf16[1088,512]{1,0:T(8,128)(2,1)S(1)}, bf16[512,2432]{1,0:T(8,128)(2,1)S(1)}) custom-call(s32[1]{0:T(128)} %bitcast.1.core_ref, bf16[512,1024]{1,0:T(8,128)(2,1)S(1)} %copy-done.2, bf16[80,512]{1,0:T(8,128)(2,1)S(1)} %copy-done.5, bf16[13,512]{1,0:T(8,128)(2,1)S(1)} %copy-done.6, bf16[3,512]{1,0:T(4,128)(2,1)S(1)} %copy-done.7, ...), custom_call_target="tpu_custom_call" | custom-call | tf_op jit(solution)/shard_map/prep/pallas_call | solution.py:295
  15.0 1.0 %copy-done = bf16[1088,512]{1,0:T(8,128)(2,1)} copy-done((bf16[1088,512]{1,0:T(8,128)(2,1)}, bf16[1088,512]{1,0:T(8,128)(2,1)S(1)}, u32[]{:S(2)}) %copy-start) | copy-done | bytes 1114136
  16.0 0.1 pad_add_fusion.place_ref
  16.1 1.8 %all-to-all-done.recv_ref = bf16[16,80,128]{2,1,0:T(8,128)(2,1)S(1)} async-done(((bf16[16,80,128]{2,1,0:T(8,128)(2,1)}), bf16[16,80,128]{2,1,0:T(8,128)(2,1)S(1)}, u32[]{:S(2)}, u32[]{:S(2)}) %all-to-all-start) | async-done | bytes 327712 | tf_op jit(solution)/shard_map/all_to_all | solution.py:304
  17.9 1.2 %copy-done.1 = bf16[1088,512]{1,0:T(8,128)(2,1)S(1)} copy-done((bf16[1088,512]{1,0:T(8,128)(2,1)S(1)}, bf16[1088,512]{1,0:T(8,128)(2,1)}, u32[]{:S(2)}) %copy-start.1) | copy-done | bytes 1114136
  19.1 12.7 %main.1 = (f32[256,1024]{1,0:T(8,128)S(1)}, f32[32,768]{1,0:T(8,128)S(1)}, bf16[288,1024]{1,0:T(8,128)(2,1)S(1)}) custom-call(s32[2]{0:T(128)S(1)} %pad_add_fusion.place_ref, s32[1]{0:T(128)S(6)} %copy.10.count_ref, bf16[16,80,128]{2,1,0:T(8,128)(2,1)S(1)} %all-to-all-done.recv_ref, bf16[1088,512]{1,0:T(8,128)(2,1)S(1)} %copy-done.1, ...), custom_call_target="tpu_custom_call" | custom-call | tf_op jit(solution)/shard_map/main/pallas_call | solution.py:305
  31.8 2.4 %collective-permute-start = (bf16[288,1024]{1,0:T(8,128)(2,1)S(1)}, bf16[288,1024]{1,0:T(8,128)(2,1)S(1)}, u32[]{:S(2)}, u32[]{:S(2)}) collective-permute-start(bf16[288,1024]{1,0:T(8,128)(2,1)S(1)} %get-tuple-element.15), channel_id=1, source_target_pairs={{0,1},{1,0},{2,3},{3,2},{4,5},{5,4},{6,7},{7,6},{8,9},{9,8},{10,11... | collective-permute-start | bytes 1769480 | tf_op jit(solution)/shard_map/ppermute | solution.py:332
  34.2 1.6 %collective-permute-done.recv_ref = bf16[288,1024]{1,0:T(8,128)(2,1)S(1)} collective-permute-done((bf16[288,1024]{1,0:T(8,128)(2,1)S(1)}, bf16[288,1024]{1,0:T(8,128)(2,1)S(1)}, u32[]{:S(2)}, u32[]{:S(2)}) %collective-permute-start) | collective-permute-done | bytes 589856 | tf_op jit(solution)/shard_map/ppermute | solution.py:332
  35.8 0.2 pair.1
  36.0 22.5 %all_to_all.15.share_ref = bf16[16,80,512]{2,1,0:T(8,128)(2,1)S(1)} all-to-all(bf16[16,80,512]{2,1,0:T(8,128)(2,1)S(1)} %pair.1), channel_id=1, replica_groups=mesh['lon'=16,'lat'=16] {'lon'}, dimensions={0} | all-to-all | bytes 2621440 | tf_op jit(solution)/shard_map/all_to_all | solution.py:341
  58.5 0.2 sum_lon.1
  58.8 15.7 %all_to_all.16.last_ref = bf16[8,48,128]{2,1,0:T(8,128)(2,1)S(1)} all-to-all(bf16[8,48,128]{2,1,0:T(8,128)(2,1)S(1)} %sum_lon.1), channel_id=1, replica_groups={{0,2,4,6,8,10,12,14},{1,3,5,7,9,11,13,15},{16,18,20,22,24,26,28,30},{17..., dimensions={0} | all-to-all | bytes 196608 | tf_op jit(solution)/shard_map/all_to_all | solution.py:351
  74.4 0.8 %sum_z.1 = (f32[2,1024]{1,0:T(2,128)}, f32[32,80]{1,0:T(8,128)}, f32[3,512]{1,0:T(4,128)}) custom-call(bf16[8,48,128]{2,1,0:T(8,128)(2,1)S(1)} %all_to_all.16.last_ref), custom_call_target="tpu_custom_call" | custom-call | tf_op jit(solution)/shard_map/sum_z/pallas_call | solution.py:359
  (5 shorter events, 0.0 us)
Async XLA Ops:
  0.6 10.1 %copy-start.3 = (bf16[1,128,3,512]{3,1,2,0:T(8,128)(2,1)S(1)}, bf16[1,128,3,512]{3,1,2,0:T(8,128)(2,1)}, u32[]{:S(2)}) copy-start(bf16[1,128,3,512]{3,1,2,0:T(8,128)(2,1)} %param.13) | copy-start | bytes 1179652
  0.6 1.0 %copy-start.4 = (bf16[1,1664,80]{1,2,0:T(8,128)(2,1)S(1)}, bf16[1,1664,80]{1,2,0:T(8,128)(2,1)}, u32[]{:S(2)}) copy-start(bf16[1,1664,80]{1,2,0:T(8,128)(2,1)} %param.7) | copy-start | bytes 798724
  1.6 9.1 %copy-start.5 = (bf16[80,512]{1,0:T(8,128)(2,1)S(1)}, bf16[80,512]{1,0:T(8,128)(2,1)}, u32[]{:S(2)}) copy-start(bf16[80,512]{1,0:T(8,128)(2,1)} %embed_w_ref.1) | copy-start | bytes 245764
  2.5 15.4 %all-to-all-start = ((bf16[16,80,128]{2,1,0:T(8,128)(2,1)}), bf16[16,80,128]{2,1,0:T(8,128)(2,1)S(1)}, u32[]{:S(2)}, u32[]{:S(2)}) async-start(bf16[16,80,128]{2,1,0:T(8,128)(2,1)} %slots.1), calls=%async_computation | async-start | bytes 655360 | tf_op jit(solution)/shard_map/all_to_all | solution.py:304
  10.7 1.2 %copy-start.2 = (bf16[512,1024]{1,0:T(8,128)(2,1)S(1)}, bf16[512,1024]{1,0:T(8,128)(2,1)}, u32[]{:S(2)}) copy-start(bf16[512,1024]{1,0:T(8,128)(2,1)} %kvw_ref.1) | copy-start | bytes 3145732
  11.9 0.7 copy-start.6
  12.7 0.7 copy-start.7
  15.0 1.0 %copy-start = (bf16[1088,512]{1,0:T(8,128)(2,1)}, bf16[1088,512]{1,0:T(8,128)(2,1)S(1)}, u32[]{:S(2)}) copy-start(bf16[1088,512]{1,0:T(8,128)(2,1)S(1)} %get-tuple-element.11.tall_ref) | copy-start | bytes 3342340
  17.9 1.2 %copy-start.1 = (bf16[1088,512]{1,0:T(8,128)(2,1)S(1)}, bf16[1088,512]{1,0:T(8,128)(2,1)}, u32[]{:S(2)}) copy-start(bf16[1088,512]{1,0:T(8,128)(2,1)} %copy-done) | copy-start | bytes 3342340
  31.8 4.0 %collective-permute-start = (bf16[288,1024]{1,0:T(8,128)(2,1)S(1)}, bf16[288,1024]{1,0:T(8,128)(2,1)S(1)}, u32[]{:S(2)}, u32[]{:S(2)}) collective-permute-start(bf16[288,1024]{1,0:T(8,128)(2,1)S(1)} %get-tuple-element.15), channel_id=1, source_target_pairs={{0,1},{1,0},{2,3},{3,2},{4,5},{5,4},{6,7},{7,6},{8,9},{9,8},{10,11... | collective-permute-start | bytes 1769480 | tf_op jit(solution)/shard_map/ppermute | solution.py:332

commit v4 on v2

v4 whole, which is shorter than its diff:
```python
import functools

import jax
import jax.numpy as jnp
from jax import lax
from jax.experimental import pallas as pl
from jax.experimental.pallas import tpu as pltpu
from jax.sharding import PartitionSpec as P

HEADS = 16
SCORE_SCALE = 0.125
EPSILON = 1e-05
MASKED = -1e30
BF16 = jnp.bfloat16
F32 = jnp.float32

LEVELS = 13
TOK = 128
PAIRS = 7
WIDE = 2 * TOK
SPAN = PAIRS * WIDE
D = 512
HEAD = D // HEADS
FEAT = 80
AUG = 96
LATENT = 3
AH = LATENT * HEADS
GS = 128
NT = (((1,), (1,)), ((), ()))
RING = 16
ZED = 8
HALF = D // 2
WAUG = 0
QBD = 256
GRAD = 384
PLAIN = 768

VMEM = pl.BlockSpec(memory_space=pltpu.VMEM)
SMEM = pl.BlockSpec(memory_space=pltpu.SMEM)


def params(mib):
    return pltpu.CompilerParams(vmem_limit_bytes=mib * 1024 * 1024)


def shape(*dims, dtype=BF16):
    return jax.ShapeDtypeStruct(dims, dtype)


def slot_kernel(lon_ref, patch_ref, slot_ref):
    lon = lon_ref[0]
    for i in range(LEVELS):
        owner = lax.rem(lon * LEVELS + i, RING)
        slot_ref[owner] = patch_ref[:, i * TOK : (i + 1) * TOK]


def prep_kernel(kvw_ref, embed_w_ref, level_ref, query_ref, grad_ref, tall_ref, wide_ref, rows, spread):
    position = lax.broadcasted_iota(jnp.int32, (D, D), 0)
    feature = lax.broadcasted_iota(jnp.int32, (D, D), 1)
    core, lon, z, pair = position >> 8, (position >> 4) & 15, (position >> 1) & 7, position & 1
    reorder = jnp.where(lon * 32 + z * 4 + core * 2 + pair == feature, 1.0, 0.0).astype(BF16)
    for c in range(4):
        part = jnp.dot(reorder, kvw_ref[:, c * 256 : (c + 1) * 256], preferred_element_type=F32)
        tall_ref[c * 256 : (c + 1) * 256, :] = part.T.astype(BF16)
    rows[...] = jnp.zeros_like(rows)
    rows[:FEAT, :] = embed_w_ref[...].astype(F32)
    rows[FEAT : FEAT + LEVELS, :] = level_ref[...].astype(F32)
    weights = rows[...]
    weights = weights - jnp.mean(weights, axis=1, keepdims=True)
    high = weights.astype(BF16)
    spread[...] = jnp.zeros_like(spread)
    spread[:AUG, :] = high.astype(F32)
    spread[AUG : 2 * AUG, :] = weights - high.astype(F32)
    plain = spread[...].T.astype(BF16)
    wide_ref[:, PLAIN : PLAIN + 256] = plain
    wide_ref[:, WAUG : WAUG + 256] = jnp.dot(reorder, plain, preferred_element_type=F32).astype(BF16)
    head = lax.broadcasted_iota(jnp.int32, (HEADS, D), 0)
    owner = lax.broadcasted_iota(jnp.int32, (HEADS, D), 1) >> 5
    spread[:32, :] = jnp.zeros((32, D), F32)
    for a in range(LATENT):
        block = jnp.where(head == owner, query_ref[a : a + 1, :].astype(F32), 0.0)
        spread[32 + a * HEADS : 32 + (a + 1) * HEADS, :] = block
        spread[80 + a * HEADS : 80 + (a + 1) * HEADS, :] = block
    tall_ref[2 * D : 2 * D + AH, :] = spread[80:128, :].astype(BF16)
    tall_ref[2 * D + AH :, :] = jnp.zeros((16, D), BF16)
    wide_ref[:, QBD : QBD + GS] = spread[:GS, :].T.astype(BF16)
    for a in range(LATENT):
        at = GRAD + a * TOK
        wide_ref[:, at : at + TOK] = grad_ref[a].astype(F32).T.astype(BF16)


def main_kernel(
    lon_ref, count_ref, recv_ref, kvw_ref, tall_ref, wide_ref,
    hid_s, gkv_s, eq_out,
    g2, paug_s, kv_s, pin_s, inv_s, sc_s, ga_s, w_s, gs_s, xs_s,
):
    lon = lon_ref[0]
    count = count_ref[0]
    for a in range(LATENT):
        wide = wide_ref[:, GRAD + a * TOK : GRAD + (a + 1) * TOK].astype(F32)
        g2[a, :, :TOK] = wide
        g2[a, :, TOK:] = wide
    gs_s[:32, :] = jnp.zeros((32, SPAN), BF16)
    pin_s[FEAT:, :] = jnp.zeros((TOK - FEAT, SPAN), BF16)

    def embed(p):
        at = slice(p * WIDE, (p + 1) * WIDE)
        first, second = 2 * p, min(2 * p + 1, LEVELS - 1)
        patches = jnp.concatenate(
            [recv_ref[(RING * first + lon) // LEVELS], recv_ref[(RING * second + lon) // LEVELS]], axis=1
        )
        row = lax.broadcasted_iota(jnp.int32, (AUG - FEAT, WIDE), 0)
        lane = lax.broadcasted_iota(jnp.int32, (AUG - FEAT, WIDE), 1)
        level = jnp.where(lane >= TOK, second, first)
        one_hot = jnp.where(row == level, 1.0, 0.0).astype(BF16)
        paug_s[:FEAT, at] = patches
        paug_s[FEAT:AUG, at] = one_hot
        paug_s[AUG : AUG + FEAT, at] = patches
        paug_s[AUG + FEAT :, at] = one_hot
        center = jnp.dot(wide_ref[:, WAUG : WAUG + 2 * AUG], paug_s[:, at], preferred_element_type=F32)
        inv_std = lax.rsqrt(jnp.mean(center * center, axis=0, keepdims=True) + EPSILON)
        inv_s[:, at] = inv_std
        hid_s[:, at] = (center * inv_std).astype(BF16)
        pin_s[:FEAT, at] = (patches.astype(F32) * inv_std).astype(BF16)

    def score(p):
        at = slice(p * WIDE, (p + 1) * WIDE)
        kv_s[:, at] = jnp.dot(tall_ref[: 2 * D, :], hid_s[:, at], preferred_element_type=F32).astype(BF16)
        sc_s[:, at] = (
            jnp.dot(tall_ref[2 * D : 2 * D + AH, :], kv_s[:D, at], preferred_element_type=F32) * SCORE_SCALE
        )
        values = kv_s[D:, at].astype(F32)
        for a in range(LATENT):
            product = (g2[a] * values).reshape(HEADS, HEAD, WIDE)
            ga_s[a * HEADS : (a + 1) * HEADS, at] = jnp.sum(product, axis=1)

    embed(0)
    for p in range(PAIRS):
        if p + 1 < PAIRS:
            embed(p + 1)
        score(p)

    masked = [jnp.where(l < count, sc_s[:, l * TOK : (l + 1) * TOK], MASKED) for l in range(LEVELS)]
    peak = functools.reduce(jnp.maximum, masked)
    total = jnp.zeros_like(peak)
    for l in range(LEVELS):
        exponent = jnp.exp(masked[l] - peak)
        w_s[:, l * TOK : (l + 1) * TOK] = exponent
        total = total + exponent
    inverse = 1.0 / total
    inner = jnp.zeros_like(peak)
    for l in range(LEVELS):
        lanes = slice(l * TOK, (l + 1) * TOK)
        inner = inner + w_s[:, lanes] * inverse * ga_s[:, lanes]
    for l in range(LEVELS):
        lanes = slice(l * TOK, (l + 1) * TOK)
        attention = w_s[:, lanes] * inverse
        weight = attention.astype(BF16).astype(F32)
        w_s[:, lanes] = weight
        grad_attn = ga_s[:, lanes]
        grad_score = attention * (grad_attn - inner)
        slope = jnp.sum(grad_score * sc_s[:, lanes] + weight * grad_attn, axis=0, keepdims=True)
        scale = slope * inv_s[:, lanes] * (1.0 / D)
        xs_s[:, lanes] = (paug_s[:AUG, lanes].astype(F32) * scale).astype(BF16)
        grad_score = grad_score * SCORE_SCALE
        high = grad_score.astype(BF16)
        gs_s[32:80, lanes] = (grad_score - high.astype(F32)).astype(BF16)
        gs_s[80:, lanes] = high
    tail = slice(LEVELS * TOK, SPAN)
    w_s[:, tail] = jnp.zeros((AH, TOK), F32)
    gs_s[32:, tail] = jnp.zeros((2 * AH, TOK), BF16)
    xs_s[:, tail] = jnp.zeros((AUG, TOK), BF16)

    for p in range(PAIRS):
        at = slice(p * WIDE, (p + 1) * WIDE)
        gkv_s[:D, at] = jnp.dot(
            wide_ref[:, QBD : QBD + GS], gs_s[:, at], preferred_element_type=F32
        ).astype(BF16)
        grad_values = None
        for a in range(LATENT):
            weight = w_s[a * HEADS : (a + 1) * HEADS, at].reshape(HEADS, 1, WIDE)
            term = weight * g2[a].reshape(HEADS, HEAD, WIDE)
            grad_values = term if grad_values is None else grad_values + term
        gkv_s[D:, at] = grad_values.reshape(D, WIDE).astype(BF16)

    outer = lax.dot_general(gkv_s[...], pin_s[...], NT, preferred_element_type=F32)
    high = outer.astype(BF16)
    low = (outer - high.astype(F32)).astype(BF16)
    grads = jnp.dot(kvw_ref[...], jnp.concatenate([high, low], axis=1), preferred_element_type=F32)
    grads = grads[:, :TOK] + grads[:, TOK:]
    gram = lax.dot_general(xs_s[...], pin_s[...], NT, preferred_element_type=F32).astype(BF16)
    grads = grads - jnp.dot(
        wide_ref[:, PLAIN : PLAIN + 2 * AUG], jnp.concatenate([gram, gram], axis=0), preferred_element_type=F32
    )
    grads = grads - jnp.mean(grads, axis=0, keepdims=True)
    queries = lax.dot_general(kv_s[:D, :], gs_s[...], NT, preferred_element_type=F32)
    head = lax.broadcasted_iota(jnp.int32, (D, GS), 0) >> 5
    lane = lax.broadcasted_iota(jnp.int32, (D, GS), 1)
    queries = jnp.where((lane & 15) == head, queries, 0.0).reshape(HEADS, HEAD, GS)
    queries = jnp.sum(queries, axis=0)
    queries = queries + pltpu.roll(queries, AH, 1)
    queries = jnp.concatenate([queries] * HEADS, axis=0)
    eq_out[...] = jnp.where(lane < FEAT, grads, queries).astype(BF16)


def project_kernel(core_ref, hid_ref, gkv_ref, keep_out, send_out):
    core = core_ref[0]
    mine = hid_ref[pl.ds(pl.multiple_of(core * HALF, HALF), HALF), :]
    other = hid_ref[pl.ds(pl.multiple_of((1 - core) * HALF, HALF), HALF), :]
    for c in range(4):
        at = slice(c * WIDE, (c + 1) * WIDE)
        send_out[:, at] = lax.dot_general(other, gkv_ref[at, :], NT, preferred_element_type=F32).astype(BF16)
        keep_out[:, at] = lax.dot_general(mine, gkv_ref[at, :], NT, preferred_element_type=F32)


def pair_kernel(keep_ref, recv_ref, eq_ref, share_ref):
    for target in range(RING):
        rows = slice(target * 16, (target + 1) * 16)
        share_ref[target, :, : 2 * D] = (keep_ref[rows, :] + recv_ref[rows, :].astype(F32)).astype(BF16)
    block = eq_ref[0].astype(F32)
    for source in range(1, RING):
        block = block + eq_ref[source].astype(F32)
    block = block.astype(BF16)
    for target in range(RING):
        share_ref[target, :, 2 * D : 2 * D + TOK] = block[:16]
        share_ref[target, :, 2 * D + TOK :] = block[16:]


def sum_lon_kernel(share_ref, last_ref, embed_out, query_out, total, tile, turned):
    acc = share_ref[0].astype(F32)
    for source in range(1, RING):
        acc = acc + share_ref[source].astype(F32)
    total[...] = acc
    for z in range(ZED):
        for c in range(8):
            tile[z, 2 * c : 2 * c + 2, :] = total[2 * z : 2 * z + 2, c * TOK : (c + 1) * TOK]
        last_ref[z] = tile[z].astype(BF16)
    block = jnp.concatenate([acc[:, 2 * D : 2 * D + TOK], acc[:, 2 * D + TOK :]], axis=0)
    embed_out[...] = block[:, :FEAT]
    turned[...] = block.T
    for a in range(LATENT):
        for h in range(HEADS):
            at = FEAT + a * HEADS + h
            query_out[a : a + 1, h * HEAD : (h + 1) * HEAD] = turned[at : at + 1, :]


def sum_z_kernel(last_ref, kv_out, tile):
    acc = last_ref[0].astype(F32)
    for source in range(1, ZED):
        acc = acc + last_ref[source].astype(F32)
    tile[...] = acc
    for c in range(8):
        kv_out[:, c * TOK : (c + 1) * TOK] = tile[2 * c : 2 * c + 2, :]


def call(kernel, outs, in_specs, scratch, mib, name, flops=10**8, size=10**6):
    return pl.pallas_call(
        kernel,
        out_shape=outs,
        in_specs=in_specs,
        out_specs=jax.tree.map(lambda _: VMEM, outs),
        scratch_shapes=scratch,
        compiler_params=params(mib),
        cost_estimate=pl.CostEstimate(flops=flops, bytes_accessed=size, transcendentals=0),
        name=name,
    )


def on_device(level_patches, level_embed, embed_weight, kv_weight, query, band_levels, grad_out):
    lon = lax.axis_index("lon").astype(jnp.int32).reshape(1)
    core = (lax.axis_index("lat").astype(jnp.int32) & 1).reshape(1)
    slots = call(slot_kernel, shape(RING, FEAT, TOK), [SMEM, VMEM], [], 16, "slots")(lon, level_patches[0].T)
    tall, wide = call(
        prep_kernel,
        (shape(2 * D + 64, D), shape(D, 2 * D)),
        [VMEM] * 5,
        [pltpu.VMEM((AUG, D), F32), pltpu.VMEM((256, D), F32)],
        24,
        "prep",
    )(kv_weight, embed_weight, level_embed, query, grad_out[0].transpose(1, 0, 2))
    recv = lax.all_to_all(slots, "lon", 0, 0, tiled=True)
    hidden, grad_kv, block = call(
        main_kernel,
        (shape(D, SPAN), shape(2 * D, SPAN), shape(D, TOK)),
        [SMEM, SMEM] + [VMEM] * 4,
        [
            pltpu.VMEM((LATENT, D, WIDE), F32),
            pltpu.VMEM((2 * AUG, SPAN), BF16),
            pltpu.VMEM((2 * D, SPAN), BF16),
            pltpu.VMEM((TOK, SPAN), BF16),
            pltpu.VMEM((1, SPAN), F32),
            pltpu.VMEM((AH, SPAN), F32),
            pltpu.VMEM((AH, SPAN), F32),
            pltpu.VMEM((AH, SPAN), F32),
            pltpu.VMEM((GS, SPAN), BF16),
            pltpu.VMEM((AUG, SPAN), BF16),
        ],
        24,
        "main",
    )(lon, band_levels, recv, kv_weight, tall, wide)
    blocks = lax.all_to_all(block.reshape(RING, D // RING, TOK), "lat", 0, 0, tiled=True)
    keep, send = call(
        project_kernel,
        (shape(HALF, 2 * D, dtype=F32), shape(HALF, 2 * D)),
        [SMEM] + [VMEM] * 2,
        [],
        16,
        "project",
        4 * 10**9,
        8 * 10**6,
    )(core, hidden, grad_kv)
    lats = lax.axis_size("lat")
    other = lax.ppermute(send, "lat", [(i, i ^ 1) for i in range(lats)])
    share = call(pair_kernel, shape(RING, 16, 2 * D + 2 * TOK), [VMEM] * 3, [], 16, "pair")(keep, other, blocks)
    shared = lax.all_to_all(share, "lon", 0, 0, tiled=True)
    last, embed_grad, query_grad = call(
        sum_lon_kernel,
        (shape(ZED, 16, TOK), shape(32, FEAT, dtype=F32), shape(LATENT, D, dtype=F32)),
        [VMEM],
        [
            pltpu.VMEM((16, 2 * D + 2 * TOK), F32),
            pltpu.VMEM((ZED, 16, TOK), F32),
            pltpu.VMEM((TOK, 32), F32),
        ],
        16,
        "sum_lon",
    )(shared)
    lasts = lax.all_to_all(
        last,
        "lat",
        0,
        0,
        tiled=True,
        axis_index_groups=[[2 * z + c for z in range(ZED)] for c in range(2)],
    )
    kv_grad = call(
        sum_z_kernel, shape(2, 2 * D, dtype=F32), [VMEM], [pltpu.VMEM((16, TOK), F32)], 16, "sum_z"
    )(lasts)
    return (kv_grad, embed_grad.T, query_grad)


def solution(mesh):
    placed = (P("lat", "lon", None), P(), P(), P(), P(), P("lat"), P("lat", "lon", None, None))
    return jax.shard_map(
        on_device,
        mesh=mesh,
        in_specs=placed,
        out_specs=(P(("lon", "lat"), None), P(None, "lat"), P()),
        check_vma=False,
    )
```

time: 74.1 us -> 77.3 us (1.043)
  blocking collectives: 36.6 us -> 42.7 us
  waiting for transfers between devices: 4.79 us -> 2.43 us
    all_to_all x1, blocking collectives: 10.2 us -> 16 us  [on_device(): shared = lax.all_to_all(share, 'lon', 0, 0, tiled=True)]
    ppermute x1, waiting for transfers between devices: 1.63 us -> 0.01 us  [on_device(): other = lax.ppermute(send, 'lat', [(i, i ^ 1) for i in range(lats)])]
    all_to_all x1 -> x2, blocking collectives: 26.4 us -> 26.8 us  [the longest x1 17.5 us: on_device(): lax.all_to_all(block.reshape(RING, D // RING, TOK), 'lat', 0, 0, tiled=True)]
    pallas_call x6 -> x7, Pallas kernels: 16.2 us -> 16 us  [the longest x1 10.1 us: on_device(): call(main_kernel, (shape(D, SPAN), shape(2 * D, SPAN), shape(D, TOK)), [S...]
    unnamed x16 -> x12, local copies, waits for them, and re-layouts: 4.47 us -> 4.32 us
  transfers between devices with their start and end apart: 2 -> 2, of which waited for: 2 -> 1; matrix products, arithmetic and copies ran while one was open for 0% -> 0% of each run, Pallas kernels for 2% -> 2%
where the time goes in v4:
time: 77.3 us; the launch traced here: 76.8 us
  blocking collectives  42.7 us (55%)
  Pallas kernels  16 us (21%)
  starting transfers between devices  9.96 us (13%)
  local copies, waits for them, and re-layouts  4.32 us (6%)
  waiting for transfers between devices  2.43 us (3%)
  between operations  1.36 us (2%)
    all_to_all x1, blocking collectives, on_device(): lax.all_to_all(block.reshape(RING, D // RING, TOK), 'lat', 0, 0, tiled=True)  17.5 us
    all_to_all x1, blocking collectives, on_device(): shared = lax.all_to_all(share, 'lon', 0, 0, tiled=True)  16 us
    pallas_call x1, Pallas kernels, on_device(): call(main_kernel, (shape(D, SPAN), shape(2 * D, SPAN), shape(D, TOK)), [S...  10.1 us
    all_to_all x1, blocking collectives, on_device(): lax.all_to_all(last, 'lat', 0, 0, tiled=True, axis_index_groups=[[2 * z +...  9.23 us
    all_to_all x1, starting transfers between devices, on_device(): recv = lax.all_to_all(slots, 'lon', 0, 0, tiled=True)  7.58 us
    unnamed x12, local copies, waits for them, and re-layouts  4.32 us
    all_to_all x1, waiting for transfers between devices, on_device(): recv = lax.all_to_all(slots, 'lon', 0, 0, tiled=True)  2.43 us
    ppermute x1, starting transfers between devices, on_device(): other = lax.ppermute(send, 'lat', [(i, i ^ 1) for i in range(lats)])  2.38 us
  transfers between devices with their start and end apart: 2, of which 1 were waited for; matrix products, arithmetic and copies ran while one was open for 0% of the time, Pallas kernels for 2%

profile of v4, /device:TPU:1, one launch (start us, length us, event | category | flops | bytes accessed | tf_op | source)
XLA Modules:
  0.0 76.8 jit_solution(3431745516517472642)
XLA Ops:
  0.6 0.0 copy-start
  0.6 0.0 copy-start.2
  0.7 1.0 %copy-done.2 = bf16[1,1664,80]{1,2,0:T(8,128)(2,1)S(1)} copy-done((bf16[1,1664,80]{1,2,0:T(8,128)(2,1)S(1)}, bf16[1,1664,80]{1,2,0:T(8,128)(2,1)}, u32[]{:S(2)}) %copy-start.2) | copy-done | bytes 266264
  1.7 0.8 %slots.1 = bf16[16,80,128]{2,1,0:T(8,128)(2,1)} custom-call(s32[1]{0:T(128)} %bitcast.1.lon_ref, bf16[80,1664]{1,0:T(8,128)(2,1)S(1)} %bitcast.11), custom_call_target="tpu_custom_call" | custom-call | flops 100000000 | bytes 1000000 | tf_op jit(solution)/shard_map/slots/pallas_call | solution.py:272
  2.5 7.6 %all-to-all-start = ((bf16[16,80,128]{2,1,0:T(8,128)(2,1)}), bf16[16,80,128]{2,1,0:T(8,128)(2,1)S(1)}, u32[]{:S(2)}, u32[]{:S(2)}) async-start(bf16[16,80,128]{2,1,0:T(8,128)(2,1)} %slots.1), calls=%async_computation | async-start | bytes 655360 | tf_op jit(solution)/shard_map/all_to_all | solution.py:281
  10.7 0.0 copy-done
  10.7 0.0 copy-start.1
  10.7 1.0 %copy-done.1 = bf16[1,128,3,512]{3,1,2,0:T(8,128)(2,1)S(1)} copy-done((bf16[1,128,3,512]{3,1,2,0:T(8,128)(2,1)S(1)}, bf16[1,128,3,512]{3,1,2,0:T(8,128)(2,1)}, u32[]{:S(2)}) %copy-start.1) | copy-done | bytes 393240
  11.7 0.0 copy-start.3
  11.7 0.9 %copy-done.3 = bf16[80,512]{1,0:T(8,128)(2,1)S(1)} copy-done((bf16[80,512]{1,0:T(8,128)(2,1)S(1)}, bf16[80,512]{1,0:T(8,128)(2,1)}, u32[]{:S(2)}) %copy-start.3) | copy-done | bytes 81944
  12.6 0.7 copy-done.4
  13.3 0.7 copy-done.5
  14.0 1.4 %prep.1 = (bf16[1088,512]{1,0:T(8,128)(2,1)S(1)}, bf16[512,1024]{1,0:T(8,128)(2,1)S(1)}) custom-call(bf16[512,1024]{1,0:T(8,128)(2,1)S(1)} %copy-done, bf16[80,512]{1,0:T(8,128)(2,1)S(1)} %copy-done.3, bf16[13,512]{1,0:T(8,128)(2,1)S(1)} %copy-done.4, bf16[3,512]{1,0:T(4,128)(2,1)S(1)} %copy-done.5, bf16[3,128,512]{2,1,0:T(8,128)(2,1)S(1)} %bitcast.10), custom_call_target="tpu_custom_call" | custom-call | flops 100000000 | bytes 1000000 | tf_op jit(solution)/shard_map/prep/pallas_call | solution.py:273
  15.4 2.4 %all-to-all-done.recv_ref = bf16[16,80,128]{2,1,0:T(8,128)(2,1)S(1)} async-done(((bf16[16,80,128]{2,1,0:T(8,128)(2,1)}), bf16[16,80,128]{2,1,0:T(8,128)(2,1)S(1)}, u32[]{:S(2)}, u32[]{:S(2)}) %all-to-all-start) | async-done | bytes 327712 | tf_op jit(solution)/shard_map/all_to_all | solution.py:281
  17.9 10.1 %main.1 = (bf16[512,1792]{1,0:T(8,128)(2,1)S(1)}, bf16[1024,1792]{1,0:T(8,128)(2,1)S(1)}, bf16[512,128]{1,0:T(8,128)(2,1)S(1)}) custom-call(s32[1]{0:T(128)} %bitcast.1.lon_ref, s32[1]{0:T(128)S(6)} %copy.10.count_ref, bf16[16,80,128]{2,1,0:T(8,128)(2,1)S(1)} %all-to-all-done.recv_ref, bf16[512,1024]{1,0:T(8,128)(2,1)S(1)} %copy-done, ...), custom_call_target="tpu_custom_call" | custom-call | flops 100000000 | bytes 1000000 | tf_op jit(solution)/shard_map/main/pallas_call | solution.py:282
  28.0 2.1 %project.1 = (f32[256,1024]{1,0:T(8,128)S(1)}, bf16[256,1024]{1,0:T(8,128)(2,1)S(1)}) custom-call(s32[1]{0:T(128)} %bitcast.core_ref, bf16[512,1792]{1,0:T(8,128)(2,1)S(1)} %get-tuple-element.15.hid_ref, bf16[1024,1792]{1,0:T(8,128)(2,1)S(1)} %get-tuple-element.16.gkv_ref), custom_call_target="tpu_custom_call" | custom-call | flops 4000000000 | bytes 8000000 | tf_op jit(solution)/shard_map/project/pallas_call | solution.py:302
  30.1 2.4 %collective-permute-start = (bf16[256,1024]{1,0:T(8,128)(2,1)S(1)}, bf16[256,1024]{1,0:T(8,128)(2,1)S(1)}, u32[]{:S(2)}, u32[]{:S(2)}) collective-permute-start(bf16[256,1024]{1,0:T(8,128)(2,1)S(1)} %get-tuple-element.18), channel_id=1, source_target_pairs={{0,1},{1,0},{2,3},{3,2},{4,5},{5,4},{6,7},{7,6},{8,9},{9,8},{10,11... | collective-permute-start | bytes 1572872 | tf_op jit(solution)/shard_map/ppermute | solution.py:313
  32.5 17.5 %all_to_all.20.eq_ref = bf16[16,32,128]{2,1,0:T(8,128)(2,1)S(1)} all-to-all(bf16[16,32,128]{2,1,0:T(8,128)(2,1)S(1)} %bitcast.12), channel_id=1, replica_groups=mesh['lon'=16,'lat'=16] {'lat'}, dimensions={0} | all-to-all | bytes 262144 | tf_op jit(solution)/shard_map/all_to_all | solution.py:301
  50.0 0.0 collective-permute-done.recv_ref
  50.0 0.1 pair.1
  50.2 16.0 %all_to_all.21.share_ref = bf16[16,16,1280]{2,1,0:T(8,128)(2,1)S(1)} all-to-all(bf16[16,16,1280]{2,1,0:T(8,128)(2,1)S(1)} %pair.1), channel_id=1, replica_groups=mesh['lon'=16,'lat'=16] {'lon'}, dimensions={0} | all-to-all | bytes 1310720 | tf_op jit(solution)/shard_map/all_to_all | solution.py:315
  66.1 0.9 %sum_lon.1 = (bf16[8,16,128]{2,1,0:T(8,128)(2,1)S(1)}, f32[32,80]{1,0:T(8,128)}, f32[3,512]{1,0:T(4,128)}) custom-call(bf16[16,16,1280]{2,1,0:T(8,128)(2,1)S(1)} %all_to_all.21.share_ref), custom_call_target="tpu_custom_call" | custom-call | flops 100000000 | bytes 1000000 | tf_op jit(solution)/shard_map/sum_lon/pallas_call | solution.py:316
  67.0 9.2 %all_to_all.22.last_ref = bf16[8,16,128]{2,1,0:T(8,128)(2,1)S(1)} all-to-all(bf16[8,16,128]{2,1,0:T(8,128)(2,1)S(1)} %get-tuple-element.20), channel_id=1, replica_groups={{0,2,4,6,8,10,12,14},{1,3,5,7,9,11,13,15},{16,18,20,22,24,26,28,30},{17..., dimensions={0} | all-to-all | bytes 65536 | tf_op jit(solution)/shard_map/all_to_all | solution.py:328
  76.2 0.6 sum_z.1
  (2 shorter events, 0.0 us)
Async XLA Ops:
  0.6 10.1 %copy-start = (bf16[512,1024]{1,0:T(8,128)(2,1)S(1)}, bf16[512,1024]{1,0:T(8,128)(2,1)}, u32[]{:S(2)}) copy-start(bf16[512,1024]{1,0:T(8,128)(2,1)} %kvw_ref.3) | copy-start | bytes 3145732
  0.6 1.0 %copy-start.2 = (bf16[1,1664,80]{1,2,0:T(8,128)(2,1)S(1)}, bf16[1,1664,80]{1,2,0:T(8,128)(2,1)}, u32[]{:S(2)}) copy-start(bf16[1,1664,80]{1,2,0:T(8,128)(2,1)} %param.7) | copy-start | bytes 798724
  2.5 15.4 %all-to-all-start = ((bf16[16,80,128]{2,1,0:T(8,128)(2,1)}), bf16[16,80,128]{2,1,0:T(8,128)(2,1)S(1)}, u32[]{:S(2)}, u32[]{:S(2)}) async-start(bf16[16,80,128]{2,1,0:T(8,128)(2,1)} %slots.1), calls=%async_computation | async-start | bytes 655360 | tf_op jit(solution)/shard_map/all_to_all | solution.py:281
  10.7 1.0 %copy-start.1 = (bf16[1,128,3,512]{3,1,2,0:T(8,128)(2,1)S(1)}, bf16[1,128,3,512]{3,1,2,0:T(8,128)(2,1)}, u32[]{:S(2)}) copy-start(bf16[1,128,3,512]{3,1,2,0:T(8,128)(2,1)} %param.13) | copy-start | bytes 1179652
  11.7 0.9 %copy-start.3 = (bf16[80,512]{1,0:T(8,128)(2,1)S(1)}, bf16[80,512]{1,0:T(8,128)(2,1)}, u32[]{:S(2)}) copy-start(bf16[80,512]{1,0:T(8,128)(2,1)} %embed_w_ref.1) | copy-start | bytes 245764
  12.6 0.7 copy-start.4
  13.3 0.7 copy-start.5
  30.1 19.9 %collective-permute-start = (bf16[256,1024]{1,0:T(8,128)(2,1)S(1)}, bf16[256,1024]{1,0:T(8,128)(2,1)S(1)}, u32[]{:S(2)}, u32[]{:S(2)}) collective-permute-start(bf16[256,1024]{1,0:T(8,128)(2,1)S(1)} %get-tuple-element.18), channel_id=1, source_target_pairs={{0,1},{1,0},{2,3},{3,2},{4,5},{5,4},{6,7},{7,6},{8,9},{9,8},{10,11... | collective-permute-start | bytes 1572872 | tf_op jit(solution)/shard_map/ppermute | solution.py:313

commit v5 on v4

v5 whole, which is shorter than its diff:
```python
import functools

import jax
import jax.numpy as jnp
from jax import lax
from jax.experimental import pallas as pl
from jax.experimental.pallas import tpu as pltpu
from jax.sharding import PartitionSpec as P

HEADS = 16
SCORE_SCALE = 0.125
EPSILON = 1e-05
MASKED = -1e30
BF16 = jnp.bfloat16
F32 = jnp.float32

LEVELS = 13
TOK = 128
PAIRS = 7
WIDE = 2 * TOK
SPAN = PAIRS * WIDE
D = 512
HEAD = D // HEADS
FEAT = 80
AUG = 96
LATENT = 3
AH = LATENT * HEADS
GS = 128
NT = (((1,), (1,)), ((), ()))
RING = 16
ZED = 8
HALF = D // 2
WAUG = 0
QBD = 256
GRAD = 384
PLAIN = 768
DEEP = 256
ROW = 2 * D + TOK
SHARE = 48

VMEM = pl.BlockSpec(memory_space=pltpu.VMEM)
SMEM = pl.BlockSpec(memory_space=pltpu.SMEM)
HBM = pl.BlockSpec(memory_space=pltpu.HBM)


def params(mib):
    return pltpu.CompilerParams(vmem_limit_bytes=mib * 1024 * 1024)


def shape(*dims, dtype=BF16):
    return jax.ShapeDtypeStruct(dims, dtype)


def slot_kernel(lon_ref, patch_ref, slot_ref, sems):
    lon = lon_ref[0]
    copies = [
        pltpu.make_async_copy(
            patch_ref.at[:, pl.ds(i * TOK, TOK)], slot_ref.at[lax.rem(lon * LEVELS + i, RING)], sems.at[i]
        )
        for i in range(LEVELS)
    ]
    for copy in copies:
        copy.start()
    for copy in copies:
        copy.wait()


def prep_kernel(kvw_ref, embed_w_ref, level_ref, query_ref, grad_ref, tall_ref, wide_ref, rows, spread):
    position = lax.broadcasted_iota(jnp.int32, (D, D), 0)
    feature = lax.broadcasted_iota(jnp.int32, (D, D), 1)
    core, z, lon, pair = position >> 8, (position >> 5) & 7, (position >> 1) & 15, position & 1
    reorder = jnp.where(lon * 32 + z * 4 + core * 2 + pair == feature, 1.0, 0.0).astype(BF16)
    for c in range(4):
        part = jnp.dot(reorder, kvw_ref[:, c * 256 : (c + 1) * 256], preferred_element_type=F32)
        tall_ref[c * 256 : (c + 1) * 256, :] = part.T.astype(BF16)
    rows[...] = jnp.zeros_like(rows)
    rows[:FEAT, :] = embed_w_ref[...].astype(F32)
    rows[FEAT : FEAT + LEVELS, :] = level_ref[...].astype(F32)
    weights = rows[...]
    weights = weights - jnp.mean(weights, axis=1, keepdims=True)
    high = weights.astype(BF16)
    spread[...] = jnp.zeros_like(spread)
    spread[:AUG, :] = high.astype(F32)
    spread[TOK : TOK + AUG, :] = weights - high.astype(F32)
    plain = spread[...].T.astype(BF16)
    wide_ref[:, PLAIN : PLAIN + 256] = plain
    wide_ref[:, WAUG : WAUG + 256] = jnp.dot(reorder, plain, preferred_element_type=F32).astype(BF16)
    head = lax.broadcasted_iota(jnp.int32, (HEADS, D), 0)
    owner = lax.broadcasted_iota(jnp.int32, (HEADS, D), 1) >> 5
    spread[:32, :] = jnp.zeros((32, D), F32)
    for a in range(LATENT):
        block = jnp.where(head == owner, query_ref[a : a + 1, :].astype(F32), 0.0)
        spread[32 + a * HEADS : 32 + (a + 1) * HEADS, :] = block
        spread[80 + a * HEADS : 80 + (a + 1) * HEADS, :] = block
    tall_ref[2 * D : 2 * D + AH, :] = spread[80:128, :].astype(BF16)
    tall_ref[2 * D + AH :, :] = jnp.zeros((16, D), BF16)
    wide_ref[:, QBD : QBD + GS] = spread[:GS, :].T.astype(BF16)
    for a in range(LATENT):
        at = GRAD + a * TOK
        wide_ref[:, at : at + TOK] = grad_ref[a].astype(F32).T.astype(BF16)


def main_kernel(
    place_ref, count_ref, recv_ref, kvw_ref, tall_ref, wide_ref,
    keep_out, send_out,
    g2, paug_s, hid_s, kv_s, gkv_s, pin_s, inv_s, sc_s, ga_s, w_s, gs_s, xs_s, eq_s,
):
    lon = place_ref[0]
    core = place_ref[1]
    count = count_ref[0]
    for a in range(LATENT):
        wide = wide_ref[:, GRAD + a * TOK : GRAD + (a + 1) * TOK].astype(F32)
        g2[a, :, :TOK] = wide
        g2[a, :, TOK:] = wide
    gs_s[:32, :] = jnp.zeros((32, SPAN), BF16)
    pin_s[AUG:, :] = jnp.zeros((TOK - AUG, SPAN), BF16)
    paug_s[AUG:TOK, :] = jnp.zeros((TOK - AUG, SPAN), BF16)
    paug_s[TOK + AUG :, :] = jnp.zeros((TOK - AUG, SPAN), BF16)

    def embed(p):
        at = slice(p * WIDE, (p + 1) * WIDE)
        first, second = 2 * p, min(2 * p + 1, LEVELS - 1)
        patches = jnp.concatenate(
            [recv_ref[(RING * first + lon) // LEVELS], recv_ref[(RING * second + lon) // LEVELS]], axis=1
        )
        row = lax.broadcasted_iota(jnp.int32, (AUG - FEAT, WIDE), 0)
        lane = lax.broadcasted_iota(jnp.int32, (AUG - FEAT, WIDE), 1)
        level = jnp.where(lane >= TOK, second, first)
        one_hot = jnp.where(row == level, 1.0, 0.0).astype(BF16)
        paug_s[:FEAT, at] = patches
        paug_s[FEAT:AUG, at] = one_hot
        paug_s[TOK : TOK + FEAT, at] = patches
        paug_s[TOK + FEAT : TOK + AUG, at] = one_hot
        center = jnp.dot(wide_ref[:, WAUG : WAUG + DEEP], paug_s[:, at], preferred_element_type=F32)
        inv_std = lax.rsqrt(jnp.mean(center * center, axis=0, keepdims=True) + EPSILON)
        inv_s[:, at] = inv_std
        hid_s[:, at] = (center * inv_std).astype(BF16)
        pin_s[:FEAT, at] = (patches.astype(F32) * inv_std).astype(BF16)
        pin_s[FEAT:AUG, at] = jnp.where(row == level, inv_std, 0.0).astype(BF16)

    def score(p):
        at = slice(p * WIDE, (p + 1) * WIDE)
        kv_s[:, at] = jnp.dot(tall_ref[: 2 * D, :], hid_s[:, at], preferred_element_type=F32).astype(BF16)
        sc_s[:, at] = (
            jnp.dot(tall_ref[2 * D : 2 * D + AH, :], kv_s[:D, at], preferred_element_type=F32) * SCORE_SCALE
        )
        values = kv_s[D:, at].astype(F32)
        for a in range(LATENT):
            product = (g2[a] * values).reshape(HEADS, HEAD, WIDE)
            ga_s[a * HEADS : (a + 1) * HEADS, at] = jnp.sum(product, axis=1)

    embed(0)
    for p in range(PAIRS):
        if p + 1 < PAIRS:
            embed(p + 1)
        score(p)

    masked = [jnp.where(l < count, sc_s[:, l * TOK : (l + 1) * TOK], MASKED) for l in range(LEVELS)]
    peak = functools.reduce(jnp.maximum, masked)
    total = jnp.zeros_like(peak)
    for l in range(LEVELS):
        exponent = jnp.exp(masked[l] - peak)
        w_s[:, l * TOK : (l + 1) * TOK] = exponent
        total = total + exponent
    inverse = 1.0 / total
    inner = jnp.zeros_like(peak)
    for l in range(LEVELS):
        lanes = slice(l * TOK, (l + 1) * TOK)
        inner = inner + w_s[:, lanes] * inverse * ga_s[:, lanes]
    for l in range(LEVELS):
        lanes = slice(l * TOK, (l + 1) * TOK)
        attention = w_s[:, lanes] * inverse
        weight = attention.astype(BF16).astype(F32)
        w_s[:, lanes] = weight
        grad_attn = ga_s[:, lanes]
        grad_score = attention * (grad_attn - inner)
        slope = jnp.sum(grad_score * sc_s[:, lanes] + weight * grad_attn, axis=0, keepdims=True)
        scale = slope * inv_s[:, lanes] * (1.0 / D)
        xs_s[:AUG, lanes] = (paug_s[:AUG, lanes].astype(F32) * scale).astype(BF16)
        grad_score = grad_score * SCORE_SCALE
        high = grad_score.astype(BF16)
        gs_s[32:80, lanes] = (grad_score - high.astype(F32)).astype(BF16)
        gs_s[80:, lanes] = high
    tail = slice(LEVELS * TOK, SPAN)
    w_s[:, tail] = jnp.zeros((AH, TOK), F32)
    gs_s[32:, tail] = jnp.zeros((2 * AH, TOK), BF16)
    xs_s[:AUG, tail] = jnp.zeros((AUG, TOK), BF16)
    xs_s[AUG:, :] = jnp.zeros((TOK - AUG, SPAN), BF16)

    for p in range(PAIRS):
        at = slice(p * WIDE, (p + 1) * WIDE)
        gkv_s[:D, at] = jnp.dot(
            wide_ref[:, QBD : QBD + GS], gs_s[:, at], preferred_element_type=F32
        ).astype(BF16)
        grad_values = None
        for a in range(LATENT):
            weight = w_s[a * HEADS : (a + 1) * HEADS, at].reshape(HEADS, 1, WIDE)
            term = weight * g2[a].reshape(HEADS, HEAD, WIDE)
            grad_values = term if grad_values is None else grad_values + term
        gkv_s[D:, at] = grad_values.reshape(D, WIDE).astype(BF16)

    outer = lax.dot_general(gkv_s[...], pin_s[...], NT, preferred_element_type=F32)
    high = outer.astype(BF16)
    low = (outer - high.astype(F32)).astype(BF16)
    twice = jnp.concatenate([high, high], axis=1)
    mine = wide_ref[pl.ds(pl.multiple_of(core * HALF, HALF), HALF), WAUG : WAUG + DEEP]
    other = wide_ref[pl.ds(pl.multiple_of((1 - core) * HALF, HALF), HALF), WAUG : WAUG + DEEP]
    send_out[:, : 2 * D] = lax.dot_general(other, twice, NT, preferred_element_type=F32).astype(BF16)
    keep_out[:, : 2 * D] = lax.dot_general(mine, twice, NT, preferred_element_type=F32)
    grads = jnp.dot(kvw_ref[...], jnp.concatenate([high, low], axis=1), preferred_element_type=F32)
    grads = grads[:, :TOK] + grads[:, TOK:]
    gram = lax.dot_general(xs_s[...], pin_s[...], NT, preferred_element_type=F32).astype(BF16)
    grads = grads - jnp.dot(
        wide_ref[:, PLAIN : PLAIN + DEEP], jnp.concatenate([gram, gram], axis=0), preferred_element_type=F32
    )
    grads = grads - jnp.mean(grads, axis=0, keepdims=True)
    queries = lax.dot_general(kv_s[:D, :], gs_s[...], NT, preferred_element_type=F32)
    head = lax.broadcasted_iota(jnp.int32, (D, GS), 0) >> 5
    lane = lax.broadcasted_iota(jnp.int32, (D, GS), 1)
    queries = jnp.where((lane & 15) == head, queries, 0.0).reshape(HEADS, HEAD, GS)
    queries = jnp.sum(queries, axis=0)
    queries = queries + pltpu.roll(queries, AH, 1)
    queries = jnp.concatenate([queries] * HEADS, axis=0)
    eq_s[...] = jnp.where(lane < FEAT, grads, queries)
    for z in range(ZED):
        rows = slice(z * HEAD, (z + 1) * HEAD)
        start = z * 2 * HEAD
        keep_out[rows, 2 * D :] = eq_s[pl.ds(pl.multiple_of(start + core * HEAD, HEAD), HEAD), :]
        send_out[rows, 2 * D :] = eq_s[pl.ds(pl.multiple_of(start + (1 - core) * HEAD, HEAD), HEAD), :].astype(BF16)


def pair_kernel(keep_ref, recv_ref, sum_ref):
    sum_ref[...] = (keep_ref[...] + recv_ref[...].astype(F32)).astype(BF16)


def sum_z_kernel(part_ref, share_ref, total, tile):
    acc = part_ref[0].astype(F32)
    for source in range(1, ZED):
        acc = acc + part_ref[source].astype(F32)
    total[...] = acc
    block = acc[:, 2 * D :].astype(BF16)
    for target in range(RING):
        for c in range(8):
            tile[target, 2 * c : 2 * c + 2, :] = total[2 * target : 2 * target + 2, c * TOK : (c + 1) * TOK]
        share_ref[target, 0:16, :] = tile[target].astype(BF16)
        share_ref[target, 16:48, :] = block


def sum_lon_kernel(share_ref, kv_out, embed_out, query_out, tile, turned):
    acc = share_ref[0].astype(F32)
    for source in range(1, RING):
        acc = acc + share_ref[source].astype(F32)
    tile[...] = acc[:16]
    for c in range(8):
        kv_out[:, c * TOK : (c + 1) * TOK] = tile[2 * c : 2 * c + 2, :]
    embed_out[...] = acc[16:, :FEAT]
    turned[...] = acc[16:, :].T
    for a in range(LATENT):
        for h in range(HEADS):
            at = FEAT + a * HEADS + h
            query_out[a : a + 1, h * HEAD : (h + 1) * HEAD] = turned[at : at + 1, :]


def call(kernel, outs, in_specs, scratch, mib, name):
    return pl.pallas_call(
        kernel,
        out_shape=outs,
        in_specs=in_specs,
        out_specs=jax.tree.map(lambda _: VMEM, outs),
        scratch_shapes=scratch,
        compiler_params=params(mib),
        name=name,
    )


def on_device(level_patches, level_embed, embed_weight, kv_weight, query, band_levels, grad_out):
    lon = lax.axis_index("lon").astype(jnp.int32)
    core = lax.axis_index("lat").astype(jnp.int32) & 1
    slots = pl.pallas_call(
        slot_kernel,
        out_shape=shape(RING, FEAT, TOK),
        in_specs=[SMEM, HBM],
        out_specs=HBM,
        scratch_shapes=[pltpu.SemaphoreType.DMA((LEVELS,))],
        compiler_params=params(8),
        name="slots",
    )(lon.reshape(1), level_patches[0].T)
    tall, wide = call(
        prep_kernel,
        (shape(2 * D + 64, D), shape(D, 2 * D)),
        [VMEM] * 5,
        [pltpu.VMEM((AUG, D), F32), pltpu.VMEM((DEEP, D), F32)],
        24,
        "prep",
    )(kv_weight, embed_weight, level_embed, query, grad_out[0].transpose(1, 0, 2))
    recv = lax.all_to_all(slots, "lon", 0, 0, tiled=True)
    keep, send = call(
        main_kernel,
        (shape(HALF, ROW, dtype=F32), shape(HALF, ROW)),
        [SMEM, SMEM] + [VMEM] * 4,
        [
            pltpu.VMEM((LATENT, D, WIDE), F32),
            pltpu.VMEM((DEEP, SPAN), BF16),
            pltpu.VMEM((D, SPAN), BF16),
            pltpu.VMEM((2 * D, SPAN), BF16),
            pltpu.VMEM((2 * D, SPAN), BF16),
            pltpu.VMEM((TOK, SPAN), BF16),
            pltpu.VMEM((1, SPAN), F32),
            pltpu.VMEM((AH, SPAN), F32),
            pltpu.VMEM((AH, SPAN), F32),
            pltpu.VMEM((AH, SPAN), F32),
            pltpu.VMEM((GS, SPAN), BF16),
            pltpu.VMEM((TOK, SPAN), BF16),
            pltpu.VMEM((D, TOK), F32),
        ],
        24,
        "main",
    )(jnp.stack([lon, core]), band_levels, recv, kv_weight, tall, wide)
    lats = lax.axis_size("lat")
    other = lax.ppermute(send, "lat", [(i, i ^ 1) for i in range(lats)])
    paired = call(pair_kernel, shape(HALF, ROW), [VMEM] * 2, [], 8, "pair")(keep, other)
    parts = lax.all_to_all(
        paired.reshape(ZED, HALF // ZED, ROW),
        "lat",
        0,
        0,
        tiled=True,
        axis_index_groups=[[2 * z + c for z in range(ZED)] for c in range(2)],
    )
    share = call(
        sum_z_kernel,
        shape(RING, SHARE, TOK),
        [VMEM],
        [pltpu.VMEM((HALF // ZED, ROW), F32), pltpu.VMEM((RING, 16, TOK), F32)],
        8,
        "sum_z",
    )(parts)
    shared = lax.all_to_all(share, "lon", 0, 0, tiled=True)
    kv_grad, embed_grad, query_grad = call(
        sum_lon_kernel,
        (shape(2, 2 * D, dtype=F32), shape(32, FEAT, dtype=F32), shape(LATENT, D, dtype=F32)),
        [VMEM],
        [pltpu.VMEM((16, TOK), F32), pltpu.VMEM((TOK, 32), F32)],
        8,
        "sum_lon",
    )(shared)
    return (kv_grad, embed_grad.T, query_grad)


def solution(mesh):
    placed = (P("lat", "lon", None), P(), P(), P(), P(), P("lat"), P("lat", "lon", None, None))
    return jax.shard_map(
        on_device,
        mesh=mesh,
        in_specs=placed,
        out_specs=(P(("lon", "lat"), None), P(None, "lat"), P()),
        check_vma=False,
    )
```

time: 77.3 us -> 71.2 us (0.921)
  blocking collectives: 42.7 us -> 36.6 us
  waiting for transfers between devices: 2.43 us -> 5.02 us
  Pallas kernels: 16 us -> 14 us
    all_to_all x1, blocking collectives: 16 us -> 10.2 us  [on_device(): shared = lax.all_to_all(share, 'lon', 0, 0, tiled=True)]
    pallas_call x6 -> x5, Pallas kernels: 14.6 us -> 12.9 us  [the longest x1 10.9 us: on_device(): call(main_kernel, (shape(HALF, ROW, dtype=F32), shape(HALF, ROW)), [SMEM,...]
    ppermute x1, waiting for transfers between devices: 0.01 us -> 1.63 us  [on_device(): other = lax.ppermute(send, 'lat', [(i, i ^ 1) for i in range(lats)])]
    all_to_all x1, waiting for transfers between devices: 2.43 us -> 3.39 us  [on_device(): recv = lax.all_to_all(slots, 'lon', 0, 0, tiled=True)]
    all_to_all x2 -> x1, blocking collectives: 26.8 us -> 26.4 us  [on_device(): lax.all_to_all(paired.reshape(ZED, HALF // ZED, ROW), 'lat', 0, 0, tiled=...]
  transfers between devices with their start and end apart: 2 -> 2, of which waited for: 1 -> 2; matrix products, arithmetic and copies ran while one was open for 0% -> 0% of each run, Pallas kernels for 2% -> 2%
where the time goes in v5:
time: 71.2 us; the launch traced here: 70.6 us
  blocking collectives  36.6 us (51%)
  Pallas kernels  14 us (20%)
  starting transfers between devices  9.97 us (14%)
  waiting for transfers between devices  5.02 us (7%)
  local copies, waits for them, and re-layouts  3.6 us (5%)
  between operations  1.37 us (2%)
    all_to_all x1, blocking collectives, on_device(): lax.all_to_all(paired.reshape(ZED, HALF // ZED, ROW), 'lat', 0, 0, tiled=...  26.4 us
    pallas_call x1, Pallas kernels, on_device(): call(main_kernel, (shape(HALF, ROW, dtype=F32), shape(HALF, ROW)), [SMEM,...  10.9 us
    all_to_all x1, blocking collectives, on_device(): shared = lax.all_to_all(share, 'lon', 0, 0, tiled=True)  10.2 us
    all_to_all x1, starting transfers between devices, on_device(): recv = lax.all_to_all(slots, 'lon', 0, 0, tiled=True)  7.6 us
    unnamed x12, local copies, waits for them, and re-layouts  3.6 us
    all_to_all x1, waiting for transfers between devices, on_device(): recv = lax.all_to_all(slots, 'lon', 0, 0, tiled=True)  3.39 us
    ppermute x1, starting transfers between devices, on_device(): other = lax.ppermute(send, 'lat', [(i, i ^ 1) for i in range(lats)])  2.38 us
    ppermute x1, waiting for transfers between devices, on_device(): other = lax.ppermute(send, 'lat', [(i, i ^ 1) for i in range(lats)])  1.63 us
  transfers between devices with their start and end apart: 2, of which 2 were waited for; matrix products, arithmetic and copies ran while one was open for 0% of the time, Pallas kernels for 2%

profile of v5, /device:TPU:1, one launch (start us, length us, event | category | flops | bytes accessed | tf_op | source)
XLA Modules:
  0.0 70.6 jit_solution(6065278719793841470)
XLA Ops:
  0.6 0.0 copy-start
  0.6 0.0 copy-start.2
  0.7 1.0 %copy-done.2 = bf16[1,1664,80]{1,2,0:T(8,128)(2,1)S(1)} copy-done((bf16[1,1664,80]{1,2,0:T(8,128)(2,1)S(1)}, bf16[1,1664,80]{1,2,0:T(8,128)(2,1)}, u32[]{:S(2)}) %copy-start.2) | copy-done | bytes 266264
  1.7 0.0 copy-start.4
  1.7 0.8 %slots.1 = bf16[16,80,128]{2,1,0:T(8,128)(2,1)} custom-call(s32[1]{0:T(128)} %bitcast.lon_ref, bf16[80,1664]{1,0:T(8,128)(2,1)S(1)} %bitcast.12), custom_call_target="tpu_custom_call" | custom-call | tf_op jit(solution)/shard_map/slots/pallas_call | solution.py:279
  2.5 7.6 %all-to-all-start = ((bf16[16,80,128]{2,1,0:T(8,128)(2,1)}), bf16[16,80,128]{2,1,0:T(8,128)(2,1)S(1)}, u32[]{:S(2)}, u32[]{:S(2)}) async-start(bf16[16,80,128]{2,1,0:T(8,128)(2,1)} %slots.1), calls=%async_computation | async-start | bytes 655360 | tf_op jit(solution)/shard_map/all_to_all | solution.py:296
  10.8 0.0 copy-done
  10.8 0.0 copy-done.4
  10.8 0.0 copy-start.1
  10.8 1.0 %copy-done.1 = bf16[1,128,3,512]{3,1,2,0:T(8,128)(2,1)S(1)} copy-done((bf16[1,128,3,512]{3,1,2,0:T(8,128)(2,1)S(1)}, bf16[1,128,3,512]{3,1,2,0:T(8,128)(2,1)}, u32[]{:S(2)}) %copy-start.1) | copy-done | bytes 393240
  11.8 0.0 copy-start.3
  11.8 0.9 %copy-done.3 = bf16[80,512]{1,0:T(8,128)(2,1)S(1)} copy-done((bf16[80,512]{1,0:T(8,128)(2,1)S(1)}, bf16[80,512]{1,0:T(8,128)(2,1)}, u32[]{:S(2)}) %copy-start.3) | copy-done | bytes 81944
  12.7 0.7 copy-done.5
  13.4 1.1 %prep.1 = (bf16[1088,512]{1,0:T(8,128)(2,1)S(1)}, bf16[512,1024]{1,0:T(8,128)(2,1)S(1)}) custom-call(bf16[512,1024]{1,0:T(8,128)(2,1)S(1)} %copy-done, bf16[80,512]{1,0:T(8,128)(2,1)S(1)} %copy-done.3, bf16[13,512]{1,0:T(8,128)(2,1)S(1)} %copy-done.4, bf16[3,512]{1,0:T(4,128)(2,1)S(1)} %copy-done.5, bf16[3,128,512]{2,1,0:T(8,128)(2,1)S(1)} %bitcast.11), custom_call_target="tpu_custom_call" | custom-call | tf_op jit(solution)/shard_map/prep/pallas_call | solution.py:288
  14.5 0.1 pad_add_fusion.place_ref
  14.6 3.4 %all-to-all-done.recv_ref = bf16[16,80,128]{2,1,0:T(8,128)(2,1)S(1)} async-done(((bf16[16,80,128]{2,1,0:T(8,128)(2,1)}), bf16[16,80,128]{2,1,0:T(8,128)(2,1)S(1)}, u32[]{:S(2)}, u32[]{:S(2)}) %all-to-all-start) | async-done | bytes 327712 | tf_op jit(solution)/shard_map/all_to_all | solution.py:296
  17.9 10.9 %main.1 = (f32[256,1152]{1,0:T(8,128)S(1)}, bf16[256,1152]{1,0:T(8,128)(2,1)S(1)}) custom-call(s32[2]{0:T(128)S(1)} %pad_add_fusion.place_ref, s32[1]{0:T(128)S(6)} %copy.10.count_ref, bf16[16,80,128]{2,1,0:T(8,128)(2,1)S(1)} %all-to-all-done.recv_ref, bf16[512,1024]{1,0:T(8,128)(2,1)S(1)} %copy-done, bf16[1088,512]{1,0:T(8,128)(2,1)S(1)} %get-tuple-element.10.tall_ref, ...), custom_call_target="tpu_custom_call" | custom-call | tf_op jit(solution)/shard_map/main/pallas_call | solution.py:297
  28.9 2.4 %collective-permute-start = (bf16[256,1152]{1,0:T(8,128)(2,1)S(1)}, bf16[256,1152]{1,0:T(8,128)(2,1)S(1)}, u32[]{:S(2)}, u32[]{:S(2)}) collective-permute-start(bf16[256,1152]{1,0:T(8,128)(2,1)S(1)} %get-tuple-element.13), channel_id=1, source_target_pairs={{0,1},{1,0},{2,3},{3,2},{4,5},{5,4},{6,7},{7,6},{8,9},{9,8},{10,11... | collective-permute-start | bytes 1769480 | tf_op jit(solution)/shard_map/ppermute | solution.py:320
  31.2 1.6 %collective-permute-done.recv_ref = bf16[256,1152]{1,0:T(8,128)(2,1)S(1)} collective-permute-done((bf16[256,1152]{1,0:T(8,128)(2,1)S(1)}, bf16[256,1152]{1,0:T(8,128)(2,1)S(1)}, u32[]{:S(2)}, u32[]{:S(2)}) %collective-permute-start) | collective-permute-done | bytes 589856 | tf_op jit(solution)/shard_map/ppermute | solution.py:320
  32.9 0.1 pair.1
  33.0 26.4 %all_to_all.15.part_ref = bf16[8,32,1152]{2,1,0:T(8,128)(2,1)S(1)} all-to-all(bf16[8,32,1152]{2,1,0:T(8,128)(2,1)S(1)} %bitcast.10), channel_id=1, replica_groups={{0,2,4,6,8,10,12,14},{1,3,5,7,9,11,13,15},{16,18,20,22,24,26,28,30},{17..., dimensions={0} | all-to-all | bytes 1179648 | tf_op jit(solution)/shard_map/all_to_all | solution.py:322
  59.4 0.2 sum_z.1
  59.5 10.2 %all_to_all.16.share_ref = bf16[16,48,128]{2,1,0:T(8,128)(2,1)S(1)} all-to-all(bf16[16,48,128]{2,1,0:T(8,128)(2,1)S(1)} %sum_z.1), channel_id=1, replica_groups=mesh['lon'=16,'lat'=16] {'lon'}, dimensions={0} | all-to-all | bytes 393216 | tf_op jit(solution)/shard_map/all_to_all | solution.py:338
  69.7 0.8 %sum_lon.1 = (f32[2,1024]{1,0:T(2,128)}, f32[32,80]{1,0:T(8,128)}, f32[3,512]{1,0:T(4,128)}) custom-call(bf16[16,48,128]{2,1,0:T(8,128)(2,1)S(1)} %all_to_all.16.share_ref), custom_call_target="tpu_custom_call" | custom-call | tf_op jit(solution)/shard_map/sum_lon/pallas_call | solution.py:339
  (1 shorter events, 0.0 us)
Async XLA Ops:
  0.6 10.1 %copy-start = (bf16[512,1024]{1,0:T(8,128)(2,1)S(1)}, bf16[512,1024]{1,0:T(8,128)(2,1)}, u32[]{:S(2)}) copy-start(bf16[512,1024]{1,0:T(8,128)(2,1)} %kvw_ref.3) | copy-start | bytes 3145732
  0.6 1.0 %copy-start.2 = (bf16[1,1664,80]{1,2,0:T(8,128)(2,1)S(1)}, bf16[1,1664,80]{1,2,0:T(8,128)(2,1)}, u32[]{:S(2)}) copy-start(bf16[1,1664,80]{1,2,0:T(8,128)(2,1)} %param.7) | copy-start | bytes 798724
  1.7 9.1 %copy-start.4 = (bf16[13,512]{1,0:T(8,128)(2,1)S(1)}, bf16[13,512]{1,0:T(8,128)(2,1)}, u32[]{:S(2)}) copy-start(bf16[13,512]{1,0:T(8,128)(2,1)} %level_ref.1) | copy-start | bytes 39940
  2.5 15.4 %all-to-all-start = ((bf16[16,80,128]{2,1,0:T(8,128)(2,1)}), bf16[16,80,128]{2,1,0:T(8,128)(2,1)S(1)}, u32[]{:S(2)}, u32[]{:S(2)}) async-start(bf16[16,80,128]{2,1,0:T(8,128)(2,1)} %slots.1), calls=%async_computation | async-start | bytes 655360 | tf_op jit(solution)/shard_map/all_to_all | solution.py:296
  10.8 1.0 %copy-start.1 = (bf16[1,128,3,512]{3,1,2,0:T(8,128)(2,1)S(1)}, bf16[1,128,3,512]{3,1,2,0:T(8,128)(2,1)}, u32[]{:S(2)}) copy-start(bf16[1,128,3,512]{3,1,2,0:T(8,128)(2,1)} %param.13) | copy-start | bytes 1179652
  11.8 0.9 %copy-start.3 = (bf16[80,512]{1,0:T(8,128)(2,1)S(1)}, bf16[80,512]{1,0:T(8,128)(2,1)}, u32[]{:S(2)}) copy-start(bf16[80,512]{1,0:T(8,128)(2,1)} %embed_w_ref.1) | copy-start | bytes 245764
  12.7 0.7 copy-start.5
  28.9 4.0 %collective-permute-start = (bf16[256,1152]{1,0:T(8,128)(2,1)S(1)}, bf16[256,1152]{1,0:T(8,128)(2,1)S(1)}, u32[]{:S(2)}, u32[]{:S(2)}) collective-permute-start(bf16[256,1152]{1,0:T(8,128)(2,1)S(1)} %get-tuple-element.13), channel_id=1, source_target_pairs={{0,1},{1,0},{2,3},{3,2},{4,5},{5,4},{6,7},{7,6},{8,9},{9,8},{10,11... | collective-permute-start | bytes 1769480 | tf_op jit(solution)/shard_map/ppermute | solution.py:320

commit v6 on v5

v6 whole, which is shorter than its diff:
```python
import functools

import jax
import jax.numpy as jnp
from jax import lax
from jax.experimental import pallas as pl
from jax.experimental.pallas import tpu as pltpu
from jax.sharding import PartitionSpec as P

HEADS = 16
SCORE_SCALE = 0.125
EPSILON = 1e-05
MASKED = -1e30
BF16 = jnp.bfloat16
F32 = jnp.float32

LEVELS = 13
TOK = 128
SPAN = LEVELS * TOK
D = 512
HEAD = D // HEADS
FEAT = 80
AUG = 96
LATENT = 3
AH = LATENT * HEADS
GS = 128
LEFT = 2 * D + 2 * GS
OWN = D // 2 + 32
NT = (((1,), (1,)), ((), ()))
RING = 16
ZED = 8
HALF = D // 2
WAUG = 0
QBD = 256
GRAD = 384
QUERY = 768
DEEP = 256
ROW = 2 * D + TOK
SHARE = 48

VMEM = pl.BlockSpec(memory_space=pltpu.VMEM)
SMEM = pl.BlockSpec(memory_space=pltpu.SMEM)
HBM = pl.BlockSpec(memory_space=pltpu.HBM)


def params(mib):
    return pltpu.CompilerParams(vmem_limit_bytes=mib * 1024 * 1024)


def shape(*dims, dtype=BF16):
    return jax.ShapeDtypeStruct(dims, dtype)


def slot_kernel(lon_ref, patch_ref, slot_ref, sems):
    lon = lon_ref[0]
    copies = [
        pltpu.make_async_copy(
            patch_ref.at[:, pl.ds(i * TOK, TOK)], slot_ref.at[lax.rem(lon * LEVELS + i, RING)], sems.at[i]
        )
        for i in range(LEVELS)
    ]
    for copy in copies:
        copy.start()
    for copy in copies:
        copy.wait()


def prep_kernel(
    core_ref, kvw_ref, embed_w_ref, level_ref, query_ref, grad_ref, tall_ref, wide_ref, own_ref, rows, spread, plain
):
    position = lax.broadcasted_iota(jnp.int32, (D, D), 0)
    feature = lax.broadcasted_iota(jnp.int32, (D, D), 1)
    core, z, lon, pair = position >> 8, (position >> 5) & 7, (position >> 1) & 15, position & 1
    reorder = jnp.where(lon * 32 + z * 4 + core * 2 + pair == feature, 1.0, 0.0).astype(BF16)
    for c in range(4):
        part = jnp.dot(reorder, kvw_ref[:, c * 256 : (c + 1) * 256], preferred_element_type=F32)
        tall_ref[c * 256 : (c + 1) * 256, :] = part.T.astype(BF16)
    rows[...] = jnp.zeros_like(rows)
    rows[:FEAT, :] = embed_w_ref[...].astype(F32)
    rows[FEAT : FEAT + LEVELS, :] = level_ref[...].astype(F32)
    weights = rows[...]
    weights = weights - jnp.mean(weights, axis=1, keepdims=True)
    high = weights.astype(BF16)
    spread[...] = jnp.zeros_like(spread)
    spread[:AUG, :] = high.astype(F32)
    spread[TOK : TOK + AUG, :] = weights - high.astype(F32)
    plain[...] = spread[...].T.astype(BF16)
    wide_ref[:, WAUG : WAUG + 256] = jnp.dot(reorder, plain[...], preferred_element_type=F32).astype(BF16)
    product = jnp.dot(tall_ref[:D, :], wide_ref[:, WAUG : WAUG + 256], preferred_element_type=F32)
    product = product[:, :TOK] + product[:, TOK:]
    high = product.astype(BF16)
    wide_ref[:, QUERY : QUERY + TOK] = high
    wide_ref[:, QUERY + TOK : QUERY + 256] = (product - high.astype(F32)).astype(BF16)
    side = core_ref[0] * HEAD
    for z in range(ZED):
        rows_here = slice(z * HEAD, (z + 1) * HEAD)
        start = pl.multiple_of(z * 2 * HEAD + side, HEAD)
        own_ref[rows_here, : 2 * D] = kvw_ref[pl.ds(start, HEAD), :]
        own_ref[rows_here, 2 * D :] = plain[pl.ds(start, HEAD), :]
    mean = jnp.mean(kvw_ref[...].astype(F32), axis=0, keepdims=True)
    high = mean.astype(BF16).astype(F32)
    row = lax.broadcasted_iota(jnp.int32, (OWN - HALF, 2 * D), 0)
    own_ref[HALF:, : 2 * D] = jnp.where(row == 0, high, jnp.where(row == 1, mean - high, 0.0)).astype(BF16)
    own_ref[HALF:, 2 * D :] = jnp.zeros((OWN - HALF, DEEP), BF16)
    head = lax.broadcasted_iota(jnp.int32, (HEADS, D), 0)
    owner = lax.broadcasted_iota(jnp.int32, (HEADS, D), 1) >> 5
    spread[:32, :] = jnp.zeros((32, D), F32)
    for a in range(LATENT):
        block = jnp.where(head == owner, query_ref[a : a + 1, :].astype(F32), 0.0)
        spread[32 + a * HEADS : 32 + (a + 1) * HEADS, :] = block
        spread[80 + a * HEADS : 80 + (a + 1) * HEADS, :] = block
    tall_ref[2 * D : 2 * D + AH, :] = spread[80:128, :].astype(BF16)
    tall_ref[2 * D + AH :, :] = jnp.zeros((16, D), BF16)
    wide_ref[:, QBD : QBD + GS] = spread[:GS, :].T.astype(BF16)
    for a in range(LATENT):
        at = GRAD + a * TOK
        wide_ref[:, at : at + TOK] = grad_ref[a].astype(F32).T.astype(BF16)


def main_kernel(
    lon_ref, count_ref, recv_ref, tall_ref, wide_ref,
    keep_out, send_out,
    g_s, paug_s, hid_s, kv_s, left_s, pin_s, inv_s, sc_s, ga_s, w_s,
):
    lon = lon_ref[0]
    count = count_ref[0]
    for a in range(LATENT):
        g_s[a] = wide_ref[:, GRAD + a * TOK : GRAD + (a + 1) * TOK].astype(F32)
    left_s[2 * D : 2 * D + 32, :] = jnp.zeros((32, SPAN), BF16)
    left_s[2 * D + GS + AUG :, :] = jnp.zeros((TOK - AUG, SPAN), BF16)
    pin_s[AUG:, :] = jnp.zeros((TOK - AUG, SPAN), BF16)
    for start in (AUG, TOK + AUG):
        paug_s[start : start + TOK - AUG, :] = jnp.zeros((TOK - AUG, SPAN), BF16)

    def lanes_of(group):
        return slice(group[0] * TOK, (group[-1] + 1) * TOK)

    def embed(group):
        at = lanes_of(group)
        row = lax.broadcasted_iota(jnp.int32, (AUG - FEAT, TOK), 0)
        for l in group:
            lanes = slice(l * TOK, (l + 1) * TOK)
            patches = recv_ref[(RING * l + lon) // LEVELS]
            one_hot = jnp.where(row == l, 1.0, 0.0).astype(BF16)
            for start in (0, TOK):
                paug_s[start : start + FEAT, lanes] = patches
                paug_s[start + FEAT : start + AUG, lanes] = one_hot
        center = jnp.dot(wide_ref[:, WAUG : WAUG + DEEP], paug_s[:, at], preferred_element_type=F32)
        inv_std = lax.rsqrt(jnp.mean(center * center, axis=0, keepdims=True) + EPSILON)
        inv_s[:, at] = inv_std
        hid_s[:, at] = (center * inv_std).astype(BF16)
        pin_s[:AUG, at] = (paug_s[:AUG, at].astype(F32) * inv_std).astype(BF16)

    def keys(group):
        at = lanes_of(group)
        kv_s[:, at] = jnp.dot(tall_ref[: 2 * D, :], hid_s[:, at], preferred_element_type=F32).astype(BF16)

    def score(group):
        at = lanes_of(group)
        sc_s[:, at] = (
            jnp.dot(tall_ref[2 * D : 2 * D + AH, :], kv_s[:D, at], preferred_element_type=F32) * SCORE_SCALE
        )
        for h in range(HEADS):
            rows = slice(h * HEAD, (h + 1) * HEAD)
            grads = [g_s[a, rows, :] for a in range(LATENT)]
            for l in group:
                lanes = slice(l * TOK, (l + 1) * TOK)
                values = kv_s[D + h * HEAD : D + (h + 1) * HEAD, lanes].astype(F32)
                for a in range(LATENT):
                    product = (grads[a] * values).reshape(4, 8, TOK)
                    ah = a * HEADS + h
                    ga_s[ah : ah + 1, lanes] = jnp.sum(jnp.sum(product, axis=0), axis=0, keepdims=True)

    every = tuple(range(LEVELS))
    embed(every)
    keys(every)
    score(every)

    masked = [jnp.where(l < count, sc_s[:, l * TOK : (l + 1) * TOK], MASKED) for l in range(LEVELS)]
    peak = functools.reduce(jnp.maximum, masked)
    total = jnp.zeros_like(peak)
    for l in range(LEVELS):
        exponent = jnp.exp(masked[l] - peak)
        w_s[:, l * TOK : (l + 1) * TOK] = exponent
        total = total + exponent
    inverse = 1.0 / total
    inner = jnp.zeros_like(peak)
    for l in range(LEVELS):
        lanes = slice(l * TOK, (l + 1) * TOK)
        inner = inner + w_s[:, lanes] * inverse * ga_s[:, lanes]
    for l in range(LEVELS):
        lanes = slice(l * TOK, (l + 1) * TOK)
        attention = w_s[:, lanes] * inverse
        weight = attention.astype(BF16).astype(F32)
        w_s[:, lanes] = weight
        grad_attn = ga_s[:, lanes]
        grad_score = attention * (grad_attn - inner)
        slope = jnp.sum(grad_score * sc_s[:, lanes] + weight * grad_attn, axis=0, keepdims=True)
        scale = slope * inv_s[:, lanes] * (1.0 / D)
        left_s[2 * D + GS : 2 * D + GS + AUG, lanes] = (paug_s[:AUG, lanes].astype(F32) * scale).astype(BF16)
        grad_score = grad_score * SCORE_SCALE
        high = grad_score.astype(BF16)
        left_s[2 * D + 32 : 2 * D + 80, lanes] = (grad_score - high.astype(F32)).astype(BF16)
        left_s[2 * D + 80 : 2 * D + GS, lanes] = high

    def grad_kv(group):
        at = lanes_of(group)
        left_s[:D, at] = jnp.dot(
            wide_ref[:, QBD : QBD + GS], left_s[2 * D : 2 * D + GS, at], preferred_element_type=F32
        ).astype(BF16)
        for h in range(HEADS):
            rows = slice(h * HEAD, (h + 1) * HEAD)
            grads = [g_s[a, rows, :] for a in range(LATENT)]
            for l in group:
                lanes = slice(l * TOK, (l + 1) * TOK)
                grad_values = None
                for a in range(LATENT):
                    term = w_s[a * HEADS + h : a * HEADS + h + 1, lanes] * grads[a]
                    grad_values = term if grad_values is None else grad_values + term
                left_s[D + h * HEAD : D + (h + 1) * HEAD, lanes] = grad_values.astype(BF16)

    grad_kv(every)

    outer = lax.dot_general(left_s[...], pin_s[...], NT, preferred_element_type=F32)
    keep_out[...] = outer
    send_out[...] = outer.astype(BF16)


def post_kernel(core_ref, keep_ref, recv_ref, wide_ref, own_ref, part_ref):
    total = keep_ref[...] + recv_ref[...].astype(F32)
    outer = total[: 2 * D]
    high = outer.astype(BF16)
    low = (outer - high.astype(F32)).astype(BF16)
    start = pl.multiple_of(core_ref[0] * HALF, HALF)
    part_ref[:, : 2 * D] = lax.dot_general(
        wide_ref[pl.ds(start, HALF), WAUG : WAUG + DEEP],
        jnp.concatenate([high, high], axis=1),
        NT,
        preferred_element_type=F32,
    ).astype(BF16)
    grads = jnp.dot(own_ref[:, : 2 * D], jnp.concatenate([high, low], axis=1), preferred_element_type=F32)
    grads = grads[:, :TOK] + grads[:, TOK:]
    gram = total[2 * D + GS :].astype(BF16)
    grads = (
        grads[:HALF]
        - (grads[HALF : HALF + 1] + grads[HALF + 1 : HALF + 2])
        - jnp.dot(own_ref[:HALF, 2 * D :], jnp.concatenate([gram, gram], axis=0), preferred_element_type=F32)
    )
    scores = total[2 * D : 2 * D + GS]
    scores = jnp.concatenate([jnp.zeros((FEAT, TOK), F32), scores[80:] + scores[32:80]], axis=0).astype(BF16)
    queries = lax.dot_general(
        wide_ref[:, QUERY : QUERY + DEEP],
        jnp.concatenate([scores, scores], axis=1),
        NT,
        preferred_element_type=F32,
    )
    head = lax.broadcasted_iota(jnp.int32, (D, GS), 0) >> 5
    lane = lax.broadcasted_iota(jnp.int32, (D, GS), 1)
    queries = jnp.where((lane & 15) == head, queries, 0.0).reshape(HEADS, HEAD, GS)
    queries = jnp.concatenate([jnp.sum(queries, axis=0)] * ZED, axis=0)
    part_ref[:, 2 * D :] = jnp.where(lane[:HALF] < FEAT, grads, queries).astype(BF16)


def sum_z_kernel(part_ref, share_ref, total, tile):
    acc = part_ref[0].astype(F32)
    for source in range(1, ZED):
        acc = acc + part_ref[source].astype(F32)
    total[...] = acc
    block = acc[:, 2 * D :].astype(BF16)
    for target in range(RING):
        for c in range(8):
            tile[target, 2 * c : 2 * c + 2, :] = total[2 * target : 2 * target + 2, c * TOK : (c + 1) * TOK]
        share_ref[target, 0:16, :] = tile[target].astype(BF16)
        share_ref[target, 16:48, :] = block


def sum_lon_kernel(share_ref, kv_out, embed_out, query_out, tile, turned):
    acc = share_ref[0].astype(F32)
    for source in range(1, RING):
        acc = acc + share_ref[source].astype(F32)
    tile[...] = acc[:16]
    for c in range(8):
        kv_out[:, c * TOK : (c + 1) * TOK] = tile[2 * c : 2 * c + 2, :]
    embed_out[...] = acc[16:, :FEAT]
    turned[...] = acc[16:, :].T
    for a in range(LATENT):
        for h in range(HEADS):
            at = FEAT + a * HEADS + h
            query_out[a : a + 1, h * HEAD : (h + 1) * HEAD] = turned[at : at + 1, :]


def call(kernel, outs, in_specs, scratch, mib, name):
    return pl.pallas_call(
        kernel,
        out_shape=outs,
        in_specs=in_specs,
        out_specs=jax.tree.map(lambda _: VMEM, outs),
        scratch_shapes=scratch,
        compiler_params=params(mib),
        name=name,
    )


def on_device(level_patches, level_embed, embed_weight, kv_weight, query, band_levels, grad_out):
    lon = lax.axis_index("lon").astype(jnp.int32).reshape(1)
    core = (lax.axis_index("lat").astype(jnp.int32) & 1).reshape(1)
    slots = pl.pallas_call(
        slot_kernel,
        out_shape=shape(RING, FEAT, TOK),
        in_specs=[SMEM, HBM],
        out_specs=HBM,
        scratch_shapes=[pltpu.SemaphoreType.DMA((LEVELS,))],
        compiler_params=params(8),
        name="slots",
    )(lon, level_patches[0].T)
    tall, wide, own = call(
        prep_kernel,
        (shape(2 * D + 64, D), shape(D, 2 * D), shape(OWN, 2 * D + DEEP)),
        [SMEM] + [VMEM] * 5,
        [pltpu.VMEM((AUG, D), F32), pltpu.VMEM((DEEP, D), F32), pltpu.VMEM((D, DEEP), BF16)],
        24,
        "prep",
    )(core, kv_weight, embed_weight, level_embed, query, grad_out[0].transpose(1, 0, 2))
    recv = lax.all_to_all(slots, "lon", 0, 0, tiled=True)
    keep, send = call(
        main_kernel,
        (shape(LEFT, TOK, dtype=F32), shape(LEFT, TOK)),
        [SMEM, SMEM] + [VMEM] * 3,
        [
            pltpu.VMEM((LATENT, D, TOK), F32),
            pltpu.VMEM((DEEP, SPAN), BF16),
            pltpu.VMEM((D, SPAN), BF16),
            pltpu.VMEM((2 * D, SPAN), BF16),
            pltpu.VMEM((LEFT, SPAN), BF16),
            pltpu.VMEM((TOK, SPAN), BF16),
            pltpu.VMEM((1, SPAN), F32),
            pltpu.VMEM((AH, SPAN), F32),
            pltpu.VMEM((AH, SPAN), F32),
            pltpu.VMEM((AH, SPAN), F32),
        ],
        28,
        "main",
    )(lon, band_levels, recv, tall, wide)
    lats = lax.axis_size("lat")
    other = lax.ppermute(send, "lat", [(i, i ^ 1) for i in range(lats)])
    part = call(post_kernel, shape(HALF, ROW), [SMEM] + [VMEM] * 4, [], 16, "post")(core, keep, other, wide, own)
    parts = lax.all_to_all(
        part.reshape(ZED, HALF // ZED, ROW),
        "lat",
        0,
        0,
        tiled=True,
        axis_index_groups=[[2 * z + c for z in range(ZED)] for c in range(2)],
    )
    share = call(
        sum_z_kernel,
        shape(RING, SHARE, TOK),
        [VMEM],
        [pltpu.VMEM((HALF // ZED, ROW), F32), pltpu.VMEM((RING, 16, TOK), F32)],
        8,
        "sum_z",
    )(parts)
    shared = lax.all_to_all(share, "lon", 0, 0, tiled=True)
    kv_grad, embed_grad, query_grad = call(
        sum_lon_kernel,
        (shape(2, 2 * D, dtype=F32), shape(32, FEAT, dtype=F32), shape(LATENT, D, dtype=F32)),
        [VMEM],
        [pltpu.VMEM((16, TOK), F32), pltpu.VMEM((TOK, 32), F32)],
        8,
        "sum_lon",
    )(shared)
    return (kv_grad, embed_grad.T, query_grad)


def solution(mesh):
    placed = (P("lat", "lon", None), P(), P(), P(), P(), P("lat"), P("lat", "lon", None, None))
    return jax.shard_map(
        on_device,
        mesh=mesh,
        in_specs=placed,
        out_specs=(P(("lon", "lat"), None), P(None, "lat"), P()),
        check_vma=False,
    )
```

time: 71.2 us -> 66.3 us (0.931)
  Pallas kernels: 14 us -> 9.79 us
  waiting for transfers between devices: 5.02 us -> 3.41 us
  local copies, waits for them, and re-layouts: 3.6 us -> 4.46 us
    pallas_call x3, Pallas kernels: 12.1 us -> 7.97 us  [the longest x1 5.81 us: on_device(): call(main_kernel, (shape(LEFT, TOK, dtype=F32), shape(LEFT, TOK)), [SMEM,...]
    all_to_all x1, waiting for transfers between devices: 3.39 us -> 2.16 us  [on_device(): recv = lax.all_to_all(slots, 'lon', 0, 0, tiled=True)]
    unnamed x12 -> x16, local copies, waits for them, and re-layouts: 3.6 us -> 4.46 us
where the time goes in v6:
time: 66.3 us; the launch traced here: 65.7 us
  blocking collectives  36.6 us (55%)
  starting transfers between devices  9.99 us (15%)
  Pallas kernels  9.79 us (15%)
  local copies, waits for them, and re-layouts  4.46 us (7%)
  waiting for transfers between devices  3.41 us (5%)
  between operations  1.38 us (2%)
    all_to_all x1, blocking collectives, on_device(): lax.all_to_all(part.reshape(ZED, HALF // ZED, ROW), 'lat', 0, 0, tiled=Tr...  26.4 us
    all_to_all x1, blocking collectives, on_device(): shared = lax.all_to_all(share, 'lon', 0, 0, tiled=True)  10.3 us
    all_to_all x1, starting transfers between devices, on_device(): recv = lax.all_to_all(slots, 'lon', 0, 0, tiled=True)  7.61 us
    pallas_call x1, Pallas kernels, on_device(): call(main_kernel, (shape(LEFT, TOK, dtype=F32), shape(LEFT, TOK)), [SMEM,...  5.81 us
    unnamed x16, local copies, waits for them, and re-layouts  4.46 us
    ppermute x1, starting transfers between devices, on_device(): other = lax.ppermute(send, 'lat', [(i, i ^ 1) for i in range(lats)])  2.38 us
    all_to_all x1, waiting for transfers between devices, on_device(): recv = lax.all_to_all(slots, 'lon', 0, 0, tiled=True)  2.16 us
    pallas_call x1, Pallas kernels, on_device(): call(prep_kernel, (shape(2 * D + 64, D), shape(D, 2 * D), shape(OWN, 2 *...  1.55 us
  transfers between devices with their start and end apart: 2, of which 2 were waited for; matrix products, arithmetic and copies ran while one was open for 0% of the time, Pallas kernels for 2%

profile of v6, /device:TPU:1, one launch (start us, length us, event | category | flops | bytes accessed | tf_op | source)
XLA Modules:
  0.0 65.7 jit_solution(4088328650214482325)
XLA Ops:
  0.6 0.0 copy-start
  0.6 0.0 copy-start.4
  0.7 1.0 %copy-done.4 = bf16[1,1664,80]{1,2,0:T(8,128)(2,1)S(1)} copy-done((bf16[1,1664,80]{1,2,0:T(8,128)(2,1)S(1)}, bf16[1,1664,80]{1,2,0:T(8,128)(2,1)}, u32[]{:S(2)}) %copy-start.4) | copy-done | bytes 266264
  1.7 0.8 %slots.1 = bf16[16,80,128]{2,1,0:T(8,128)(2,1)} custom-call(s32[1]{0:T(128)} %bitcast.1.lon_ref, bf16[80,1664]{1,0:T(8,128)(2,1)S(1)} %bitcast.12), custom_call_target="tpu_custom_call" | custom-call | tf_op jit(solution)/shard_map/slots/pallas_call | solution.py:307
  2.5 7.6 %all-to-all-start = ((bf16[16,80,128]{2,1,0:T(8,128)(2,1)}), bf16[16,80,128]{2,1,0:T(8,128)(2,1)S(1)}, u32[]{:S(2)}, u32[]{:S(2)}) async-start(bf16[16,80,128]{2,1,0:T(8,128)(2,1)} %slots.1), calls=%async_computation | async-start | bytes 655360 | tf_op jit(solution)/shard_map/all_to_all | solution.py:324
  10.8 0.0 copy-done
  10.8 0.0 copy-done.6
  10.8 0.0 copy-start.3
  10.8 1.0 %copy-done.3 = bf16[1,128,3,512]{3,1,2,0:T(8,128)(2,1)S(1)} copy-done((bf16[1,128,3,512]{3,1,2,0:T(8,128)(2,1)S(1)}, bf16[1,128,3,512]{3,1,2,0:T(8,128)(2,1)}, u32[]{:S(2)}) %copy-start.3) | copy-done | bytes 393240
  11.8 0.9 %copy-done.5 = bf16[80,512]{1,0:T(8,128)(2,1)S(1)} copy-done((bf16[80,512]{1,0:T(8,128)(2,1)S(1)}, bf16[80,512]{1,0:T(8,128)(2,1)}, u32[]{:S(2)}) %copy-start.5) | copy-done | bytes 81944
  12.7 0.7 %copy-done.7 = bf16[3,512]{1,0:T(4,128)(2,1)S(1)} copy-done((bf16[3,512]{1,0:T(4,128)(2,1)S(1)}, bf16[3,512]{1,0:T(4,128)(2,1)}, u32[]{:S(2)}) %copy-start.7) | copy-done | bytes 3096
  13.4 1.6 %prep.1 = (bf16[1088,512]{1,0:T(8,128)(2,1)S(1)}, bf16[512,1024]{1,0:T(8,128)(2,1)S(1)}, bf16[288,1280]{1,0:T(8,128)(2,1)S(1)}) custom-call(s32[1]{0:T(128)} %bitcast.core_ref, bf16[512,1024]{1,0:T(8,128)(2,1)S(1)} %copy-done, bf16[80,512]{1,0:T(8,128)(2,1)S(1)} %copy-done.5, bf16[13,512]{1,0:T(8,128)(2,1)S(1)} %copy-done.6, bf16[3,512]{1,0:T(4,128)(2,1)S(1)} %copy-done.7, ...), custom_call_target="tpu_custom_call" | custom-call | tf_op jit(solution)/shard_map/prep/pallas_call | solution.py:316
  14.9 0.0 copy-start.1
  14.9 0.9 %copy-done.1 = bf16[288,1280]{1,0:T(8,128)(2,1)} copy-done((bf16[288,1280]{1,0:T(8,128)(2,1)}, bf16[288,1280]{1,0:T(8,128)(2,1)S(1)}, u32[]{:S(2)}) %copy-start.1) | copy-done | bytes 737304
  15.8 2.2 %all-to-all-done.recv_ref = bf16[16,80,128]{2,1,0:T(8,128)(2,1)S(1)} async-done(((bf16[16,80,128]{2,1,0:T(8,128)(2,1)}), bf16[16,80,128]{2,1,0:T(8,128)(2,1)S(1)}, u32[]{:S(2)}, u32[]{:S(2)}) %all-to-all-start) | async-done | bytes 327712 | tf_op jit(solution)/shard_map/all_to_all | solution.py:324
  18.0 5.8 %main.1 = (f32[1280,128]{1,0:T(8,128)S(1)}, bf16[1280,128]{1,0:T(8,128)(2,1)S(1)}) custom-call(s32[1]{0:T(128)} %bitcast.1.lon_ref, s32[1]{0:T(128)S(6)} %copy.10.count_ref, bf16[16,80,128]{2,1,0:T(8,128)(2,1)S(1)} %all-to-all-done.recv_ref, bf16[1088,512]{1,0:T(8,128)(2,1)S(1)} %get-tuple-element.11.tall_ref, bf16[512,1024]{1,0:T(8,128)(2,1)S(1)} %get-tuple-element.12.wide_ref), custom_call_target="tpu_custom_call" | custom-call | tf_op jit(solution)/shard_map/main/pallas_call | solution.py:325
  23.8 2.4 %collective-permute-start = (bf16[1280,128]{1,0:T(8,128)(2,1)S(1)}, bf16[1280,128]{1,0:T(8,128)(2,1)S(1)}, u32[]{:S(2)}, u32[]{:S(2)}) collective-permute-start(bf16[1280,128]{1,0:T(8,128)(2,1)S(1)} %get-tuple-element.14), channel_id=1, source_target_pairs={{0,1},{1,0},{2,3},{3,2},{4,5},{5,4},{6,7},{7,6},{8,9},{9,8},{10,11... | collective-permute-start | bytes 983048 | tf_op jit(solution)/shard_map/ppermute | solution.py:345
  26.1 1.3 %collective-permute-done.recv_ref = bf16[1280,128]{1,0:T(8,128)(2,1)S(1)} collective-permute-done((bf16[1280,128]{1,0:T(8,128)(2,1)S(1)}, bf16[1280,128]{1,0:T(8,128)(2,1)S(1)}, u32[]{:S(2)}, u32[]{:S(2)}) %collective-permute-start) | collective-permute-done | bytes 327712 | tf_op jit(solution)/shard_map/ppermute | solution.py:345
  27.4 0.0 copy-done.2
  27.4 0.6 post.1
  28.0 26.4 %all_to_all.15.part_ref = bf16[8,32,1152]{2,1,0:T(8,128)(2,1)S(1)} all-to-all(bf16[8,32,1152]{2,1,0:T(8,128)(2,1)S(1)} %bitcast.10), channel_id=1, replica_groups={{0,2,4,6,8,10,12,14},{1,3,5,7,9,11,13,15},{16,18,20,22,24,26,28,30},{17..., dimensions={0} | all-to-all | bytes 1179648 | tf_op jit(solution)/shard_map/all_to_all | solution.py:347
  54.4 0.2 sum_z.1
  54.6 10.3 %all_to_all.16.share_ref = bf16[16,48,128]{2,1,0:T(8,128)(2,1)S(1)} all-to-all(bf16[16,48,128]{2,1,0:T(8,128)(2,1)S(1)} %sum_z.1), channel_id=1, replica_groups=mesh['lon'=16,'lat'=16] {'lon'}, dimensions={0} | all-to-all | bytes 393216 | tf_op jit(solution)/shard_map/all_to_all | solution.py:363
  64.8 0.8 %sum_lon.1 = (f32[2,1024]{1,0:T(2,128)}, f32[32,80]{1,0:T(8,128)}, f32[3,512]{1,0:T(4,128)}) custom-call(bf16[16,48,128]{2,1,0:T(8,128)(2,1)S(1)} %all_to_all.16.share_ref), custom_call_target="tpu_custom_call" | custom-call | tf_op jit(solution)/shard_map/sum_lon/pallas_call | solution.py:364
  (4 shorter events, 0.0 us)
Async XLA Ops:
  0.6 10.2 %copy-start = (bf16[512,1024]{1,0:T(8,128)(2,1)S(1)}, bf16[512,1024]{1,0:T(8,128)(2,1)}, u32[]{:S(2)}) copy-start(bf16[512,1024]{1,0:T(8,128)(2,1)} %kvw_ref.1) | copy-start | bytes 3145732
  0.6 1.0 %copy-start.4 = (bf16[1,1664,80]{1,2,0:T(8,128)(2,1)S(1)}, bf16[1,1664,80]{1,2,0:T(8,128)(2,1)}, u32[]{:S(2)}) copy-start(bf16[1,1664,80]{1,2,0:T(8,128)(2,1)} %param.7) | copy-start | bytes 798724
  1.7 9.1 %copy-start.6 = (bf16[13,512]{1,0:T(8,128)(2,1)S(1)}, bf16[13,512]{1,0:T(8,128)(2,1)}, u32[]{:S(2)}) copy-start(bf16[13,512]{1,0:T(8,128)(2,1)} %level_ref.1) | copy-start | bytes 39940
  2.5 15.4 %all-to-all-start = ((bf16[16,80,128]{2,1,0:T(8,128)(2,1)}), bf16[16,80,128]{2,1,0:T(8,128)(2,1)S(1)}, u32[]{:S(2)}, u32[]{:S(2)}) async-start(bf16[16,80,128]{2,1,0:T(8,128)(2,1)} %slots.1), calls=%async_computation | async-start | bytes 655360 | tf_op jit(solution)/shard_map/all_to_all | solution.py:324
  10.8 1.0 %copy-start.3 = (bf16[1,128,3,512]{3,1,2,0:T(8,128)(2,1)S(1)}, bf16[1,128,3,512]{3,1,2,0:T(8,128)(2,1)}, u32[]{:S(2)}) copy-start(bf16[1,128,3,512]{3,1,2,0:T(8,128)(2,1)} %param.13) | copy-start | bytes 1179652
  11.8 0.9 %copy-start.5 = (bf16[80,512]{1,0:T(8,128)(2,1)S(1)}, bf16[80,512]{1,0:T(8,128)(2,1)}, u32[]{:S(2)}) copy-start(bf16[80,512]{1,0:T(8,128)(2,1)} %embed_w_ref.1) | copy-start | bytes 245764
  12.7 0.7 %copy-start.7 = (bf16[3,512]{1,0:T(4,128)(2,1)S(1)}, bf16[3,512]{1,0:T(4,128)(2,1)}, u32[]{:S(2)}) copy-start(bf16[3,512]{1,0:T(4,128)(2,1)} %query_ref.1) | copy-start | bytes 9220
  14.9 0.9 %copy-start.1 = (bf16[288,1280]{1,0:T(8,128)(2,1)}, bf16[288,1280]{1,0:T(8,128)(2,1)S(1)}, u32[]{:S(2)}) copy-start(bf16[288,1280]{1,0:T(8,128)(2,1)S(1)} %get-tuple-element.15.own_ref) | copy-start | bytes 2211844
  18.0 9.4 %copy-start.2 = (bf16[288,1280]{1,0:T(8,128)(2,1)S(1)}, bf16[288,1280]{1,0:T(8,128)(2,1)}, u32[]{:S(2)}) copy-start(bf16[288,1280]{1,0:T(8,128)(2,1)} %copy-done.1) | copy-start | bytes 2211844
  23.8 3.6 %collective-permute-start = (bf16[1280,128]{1,0:T(8,128)(2,1)S(1)}, bf16[1280,128]{1,0:T(8,128)(2,1)S(1)}, u32[]{:S(2)}, u32[]{:S(2)}) collective-permute-start(bf16[1280,128]{1,0:T(8,128)(2,1)S(1)} %get-tuple-element.14), channel_id=1, source_target_pairs={{0,1},{1,0},{2,3},{3,2},{4,5},{5,4},{6,7},{7,6},{8,9},{9,8},{10,11... | collective-permute-start | bytes 983048 | tf_op jit(solution)/shard_map/ppermute | solution.py:345

commit v7 on v6

--- a/solution.py
+++ b/solution.py
@@ -310,7 +310,7 @@
         in_specs=[SMEM, HBM],
         out_specs=HBM,
         scratch_shapes=[pltpu.SemaphoreType.DMA((LEVELS,))],
-        compiler_params=params(8),
+        compiler_params=params(60),
         name="slots",
     )(lon, level_patches[0].T)
     tall, wide, own = call(

time: 66.3 us -> 73.7 us (1.11)
  Pallas kernels: 9.79 us -> 18.2 us
  local copies, waits for them, and re-layouts: 4.46 us -> 3.44 us
    pallas_call x1, Pallas kernels: 0.81 us -> 9.29 us  [on_device(): pl.pallas_call(slot_kernel, out_shape=shape(RING, FEAT, TOK), in_specs=[S...]
    unnamed x16 -> x14, local copies, waits for them, and re-layouts: 4.46 us -> 3.44 us
where the time goes in v7:
time: 73.7 us; the launch traced here: 73.1 us
  blocking collectives  36.6 us (50%)
  Pallas kernels  18.2 us (25%)
  starting transfers between devices  9.97 us (14%)
  local copies, waits for them, and re-layouts  3.44 us (5%)
  waiting for transfers between devices  3.41 us (5%)
  between operations  1.38 us (2%)
    all_to_all x1, blocking collectives, on_device(): lax.all_to_all(part.reshape(ZED, HALF // ZED, ROW), 'lat', 0, 0, tiled=Tr...  26.4 us
    all_to_all x1, blocking collectives, on_device(): shared = lax.all_to_all(share, 'lon', 0, 0, tiled=True)  10.3 us
    pallas_call x1, Pallas kernels, on_device(): pl.pallas_call(slot_kernel, out_shape=shape(RING, FEAT, TOK), in_specs=[S...  9.29 us
    all_to_all x1, starting transfers between devices, on_device(): recv = lax.all_to_all(slots, 'lon', 0, 0, tiled=True)  7.6 us
    pallas_call x1, Pallas kernels, on_device(): call(main_kernel, (shape(LEFT, TOK, dtype=F32), shape(LEFT, TOK)), [SMEM,...  5.81 us
    unnamed x14, local copies, waits for them, and re-layouts  3.44 us
    ppermute x1, starting transfers between devices, on_device(): other = lax.ppermute(send, 'lat', [(i, i ^ 1) for i in range(lats)])  2.38 us
    all_to_all x1, waiting for transfers between devices, on_device(): recv = lax.all_to_all(slots, 'lon', 0, 0, tiled=True)  2.16 us
  transfers between devices with their start and end apart: 2, of which 2 were waited for; matrix products, arithmetic and copies ran while one was open for 0% of the time, Pallas kernels for 2%

profile of v7, /device:TPU:1, one launch (start us, length us, event | category | flops | bytes accessed | tf_op | source)
XLA Modules:
  0.0 73.1 jit_solution(975634187844421074)
XLA Ops:
  0.6 0.0 copy-start
  0.6 0.0 copy-start.5
  0.7 9.3 %slots.1 = bf16[16,80,128]{2,1,0:T(8,128)(2,1)} custom-call(s32[1]{0:T(128)} %bitcast.1.lon_ref, bf16[80,1664]{1,0:T(8,128)(2,1)} %bitcast.12), custom_call_target="tpu_custom_call" | custom-call | tf_op jit(solution)/shard_map/slots/pallas_call | solution.py:307
  10.0 7.6 %all-to-all-start = ((bf16[16,80,128]{2,1,0:T(8,128)(2,1)}), bf16[16,80,128]{2,1,0:T(8,128)(2,1)S(1)}, u32[]{:S(2)}, u32[]{:S(2)}) async-start(bf16[16,80,128]{2,1,0:T(8,128)(2,1)} %slots.1), calls=%async_computation | async-start | bytes 655360 | tf_op jit(solution)/shard_map/all_to_all | solution.py:324
  18.2 0.0 copy-done
  18.2 0.0 copy-done.5
  18.2 0.0 copy-start.3
  18.2 1.0 %copy-done.3 = bf16[1,128,3,512]{3,1,2,0:T(8,128)(2,1)S(1)} copy-done((bf16[1,128,3,512]{3,1,2,0:T(8,128)(2,1)S(1)}, bf16[1,128,3,512]{3,1,2,0:T(8,128)(2,1)}, u32[]{:S(2)}) %copy-start.3) | copy-done | bytes 393240
  19.2 0.0 copy-start.4
  19.2 0.9 %copy-done.4 = bf16[80,512]{1,0:T(8,128)(2,1)S(1)} copy-done((bf16[80,512]{1,0:T(8,128)(2,1)S(1)}, bf16[80,512]{1,0:T(8,128)(2,1)}, u32[]{:S(2)}) %copy-start.4) | copy-done | bytes 81944
  20.1 0.7 copy-done.6
  20.8 1.5 %prep.1 = (bf16[1088,512]{1,0:T(8,128)(2,1)S(1)}, bf16[512,1024]{1,0:T(8,128)(2,1)S(1)}, bf16[288,1280]{1,0:T(8,128)(2,1)S(1)}) custom-call(s32[1]{0:T(128)} %bitcast.core_ref, bf16[512,1024]{1,0:T(8,128)(2,1)S(1)} %copy-done, bf16[80,512]{1,0:T(8,128)(2,1)S(1)} %copy-done.4, bf16[13,512]{1,0:T(8,128)(2,1)S(1)} %copy-done.5, bf16[3,512]{1,0:T(4,128)(2,1)S(1)} %copy-done.6, ...), custom_call_target="tpu_custom_call" | custom-call | tf_op jit(solution)/shard_map/prep/pallas_call | solution.py:316
  22.4 0.0 copy-start.1
  22.4 0.9 %copy-done.1 = bf16[288,1280]{1,0:T(8,128)(2,1)} copy-done((bf16[288,1280]{1,0:T(8,128)(2,1)}, bf16[288,1280]{1,0:T(8,128)(2,1)S(1)}, u32[]{:S(2)}) %copy-start.1) | copy-done | bytes 737304
  23.2 2.2 %all-to-all-done.recv_ref = bf16[16,80,128]{2,1,0:T(8,128)(2,1)S(1)} async-done(((bf16[16,80,128]{2,1,0:T(8,128)(2,1)}), bf16[16,80,128]{2,1,0:T(8,128)(2,1)S(1)}, u32[]{:S(2)}, u32[]{:S(2)}) %all-to-all-start) | async-done | bytes 327712 | tf_op jit(solution)/shard_map/all_to_all | solution.py:324
  25.4 5.8 %main.1 = (f32[1280,128]{1,0:T(8,128)S(1)}, bf16[1280,128]{1,0:T(8,128)(2,1)S(1)}) custom-call(s32[1]{0:T(128)} %bitcast.1.lon_ref, s32[1]{0:T(128)S(6)} %copy.10.count_ref, bf16[16,80,128]{2,1,0:T(8,128)(2,1)S(1)} %all-to-all-done.recv_ref, bf16[1088,512]{1,0:T(8,128)(2,1)S(1)} %get-tuple-element.11.tall_ref, bf16[512,1024]{1,0:T(8,128)(2,1)S(1)} %get-tuple-element.12.wide_ref), custom_call_target="tpu_custom_call" | custom-call | tf_op jit(solution)/shard_map/main/pallas_call | solution.py:325
  31.2 2.4 %collective-permute-start = (bf16[1280,128]{1,0:T(8,128)(2,1)S(1)}, bf16[1280,128]{1,0:T(8,128)(2,1)S(1)}, u32[]{:S(2)}, u32[]{:S(2)}) collective-permute-start(bf16[1280,128]{1,0:T(8,128)(2,1)S(1)} %get-tuple-element.14), channel_id=1, source_target_pairs={{0,1},{1,0},{2,3},{3,2},{4,5},{5,4},{6,7},{7,6},{8,9},{9,8},{10,11... | collective-permute-start | bytes 983048 | tf_op jit(solution)/shard_map/ppermute | solution.py:345
  33.6 1.3 %collective-permute-done.recv_ref = bf16[1280,128]{1,0:T(8,128)(2,1)S(1)} collective-permute-done((bf16[1280,128]{1,0:T(8,128)(2,1)S(1)}, bf16[1280,128]{1,0:T(8,128)(2,1)S(1)}, u32[]{:S(2)}, u32[]{:S(2)}) %collective-permute-start) | collective-permute-done | bytes 327712 | tf_op jit(solution)/shard_map/ppermute | solution.py:345
  34.8 0.0 copy-done.2
  34.8 0.6 post.1
  35.4 26.4 %all_to_all.15.part_ref = bf16[8,32,1152]{2,1,0:T(8,128)(2,1)S(1)} all-to-all(bf16[8,32,1152]{2,1,0:T(8,128)(2,1)S(1)} %bitcast.10), channel_id=1, replica_groups={{0,2,4,6,8,10,12,14},{1,3,5,7,9,11,13,15},{16,18,20,22,24,26,28,30},{17..., dimensions={0} | all-to-all | bytes 1179648 | tf_op jit(solution)/shard_map/all_to_all | solution.py:347
  61.8 0.2 sum_z.1
  62.0 10.3 %all_to_all.16.share_ref = bf16[16,48,128]{2,1,0:T(8,128)(2,1)S(1)} all-to-all(bf16[16,48,128]{2,1,0:T(8,128)(2,1)S(1)} %sum_z.1), channel_id=1, replica_groups=mesh['lon'=16,'lat'=16] {'lon'}, dimensions={0} | all-to-all | bytes 393216 | tf_op jit(solution)/shard_map/all_to_all | solution.py:363
  72.2 0.8 %sum_lon.1 = (f32[2,1024]{1,0:T(2,128)}, f32[32,80]{1,0:T(8,128)}, f32[3,512]{1,0:T(4,128)}) custom-call(bf16[16,48,128]{2,1,0:T(8,128)(2,1)S(1)} %all_to_all.16.share_ref), custom_call_target="tpu_custom_call" | custom-call | tf_op jit(solution)/shard_map/sum_lon/pallas_call | solution.py:364
  (2 shorter events, 0.0 us)
Async XLA Ops:
  0.6 17.6 %copy-start = (bf16[512,1024]{1,0:T(8,128)(2,1)S(1)}, bf16[512,1024]{1,0:T(8,128)(2,1)}, u32[]{:S(2)}) copy-start(bf16[512,1024]{1,0:T(8,128)(2,1)} %kvw_ref.1) | copy-start | bytes 3145732
  0.6 17.6 %copy-start.5 = (bf16[13,512]{1,0:T(8,128)(2,1)S(1)}, bf16[13,512]{1,0:T(8,128)(2,1)}, u32[]{:S(2)}) copy-start(bf16[13,512]{1,0:T(8,128)(2,1)} %level_ref.1) | copy-start | bytes 39940
  10.0 15.4 %all-to-all-start = ((bf16[16,80,128]{2,1,0:T(8,128)(2,1)}), bf16[16,80,128]{2,1,0:T(8,128)(2,1)S(1)}, u32[]{:S(2)}, u32[]{:S(2)}) async-start(bf16[16,80,128]{2,1,0:T(8,128)(2,1)} %slots.1), calls=%async_computation | async-start | bytes 655360 | tf_op jit(solution)/shard_map/all_to_all | solution.py:324
  18.2 1.0 %copy-start.3 = (bf16[1,128,3,512]{3,1,2,0:T(8,128)(2,1)S(1)}, bf16[1,128,3,512]{3,1,2,0:T(8,128)(2,1)}, u32[]{:S(2)}) copy-start(bf16[1,128,3,512]{3,1,2,0:T(8,128)(2,1)} %param.13) | copy-start | bytes 1179652
  19.2 0.9 %copy-start.4 = (bf16[80,512]{1,0:T(8,128)(2,1)S(1)}, bf16[80,512]{1,0:T(8,128)(2,1)}, u32[]{:S(2)}) copy-start(bf16[80,512]{1,0:T(8,128)(2,1)} %embed_w_ref.1) | copy-start | bytes 245764
  20.1 0.7 copy-start.6
  22.4 0.9 %copy-start.1 = (bf16[288,1280]{1,0:T(8,128)(2,1)}, bf16[288,1280]{1,0:T(8,128)(2,1)S(1)}, u32[]{:S(2)}) copy-start(bf16[288,1280]{1,0:T(8,128)(2,1)S(1)} %get-tuple-element.15.own_ref) | copy-start | bytes 2211844
  25.4 9.5 %copy-start.2 = (bf16[288,1280]{1,0:T(8,128)(2,1)S(1)}, bf16[288,1280]{1,0:T(8,128)(2,1)}, u32[]{:S(2)}) copy-start(bf16[288,1280]{1,0:T(8,128)(2,1)} %copy-done.1) | copy-start | bytes 2211844
  31.2 3.6 %collective-permute-start = (bf16[1280,128]{1,0:T(8,128)(2,1)S(1)}, bf16[1280,128]{1,0:T(8,128)(2,1)S(1)}, u32[]{:S(2)}, u32[]{:S(2)}) collective-permute-start(bf16[1280,128]{1,0:T(8,128)(2,1)S(1)} %get-tuple-element.14), channel_id=1, source_target_pairs={{0,1},{1,0},{2,3},{3,2},{4,5},{5,4},{6,7},{7,6},{8,9},{9,8},{10,11... | collective-permute-start | bytes 983048 | tf_op jit(solution)/shard_map/ppermute | solution.py:345

commit v8 on v6

--- a/solution.py
+++ b/solution.py
@@ -66,7 +66,8 @@
 
 
 def prep_kernel(
-    core_ref, kvw_ref, embed_w_ref, level_ref, query_ref, grad_ref, tall_ref, wide_ref, own_ref, rows, spread, plain
+    core_ref, kvw_ref, embed_w_ref, level_ref, query_ref, grad_ref, tall_ref, wide_ref, own_ref, ready_ref,
+    rows, spread, plain,
 ):
     position = lax.broadcasted_iota(jnp.int32, (D, D), 0)
     feature = lax.broadcasted_iota(jnp.int32, (D, D), 1)
@@ -102,6 +103,7 @@
     row = lax.broadcasted_iota(jnp.int32, (OWN - HALF, 2 * D), 0)
     own_ref[HALF:, : 2 * D] = jnp.where(row == 0, high, jnp.where(row == 1, mean - high, 0.0)).astype(BF16)
     own_ref[HALF:, 2 * D :] = jnp.zeros((OWN - HALF, DEEP), BF16)
+    ready_ref[...] = rows[:16, :TOK]
     head = lax.broadcasted_iota(jnp.int32, (HEADS, D), 0)
     owner = lax.broadcasted_iota(jnp.int32, (HEADS, D), 1) >> 5
     spread[:32, :] = jnp.zeros((32, D), F32)
@@ -118,7 +120,7 @@
 
 
 def main_kernel(
-    lon_ref, count_ref, recv_ref, tall_ref, wide_ref,
+    lon_ref, count_ref, recv_ref, tall_ref, wide_ref, ready_ref,
     keep_out, send_out,
     g_s, paug_s, hid_s, kv_s, left_s, pin_s, inv_s, sc_s, ga_s, w_s,
 ):
@@ -313,19 +315,21 @@
         compiler_params=params(8),
         name="slots",
     )(lon, level_patches[0].T)
-    tall, wide, own = call(
+    tall, wide, own, ready = call(
         prep_kernel,
-        (shape(2 * D + 64, D), shape(D, 2 * D), shape(OWN, 2 * D + DEEP)),
+        (shape(2 * D + 64, D), shape(D, 2 * D), shape(OWN, 2 * D + DEEP), shape(16, TOK, dtype=F32)),
         [SMEM] + [VMEM] * 5,
         [pltpu.VMEM((AUG, D), F32), pltpu.VMEM((DEEP, D), F32), pltpu.VMEM((D, DEEP), BF16)],
         24,
         "prep",
     )(core, kv_weight, embed_weight, level_embed, query, grad_out[0].transpose(1, 0, 2))
     recv = lax.all_to_all(slots, "lon", 0, 0, tiled=True)
+    lats = lax.axis_size("lat")
+    ready = lax.ppermute(ready, "lat", [(i, (i + lats // 2) % lats) for i in range(lats)])
     keep, send = call(
         main_kernel,
         (shape(LEFT, TOK, dtype=F32), shape(LEFT, TOK)),
-        [SMEM, SMEM] + [VMEM] * 3,
+        [SMEM, SMEM] + [VMEM] * 4,
         [
             pltpu.VMEM((LATENT, D, TOK), F32),
             pltpu.VMEM((DEEP, SPAN), BF16),
@@ -340,8 +344,7 @@
         ],
         28,
         "main",
-    )(lon, band_levels, recv, tall, wide)
-    lats = lax.axis_size("lat")
+    )(lon, band_levels, recv, tall, wide, ready)
     other = lax.ppermute(send, "lat", [(i, i ^ 1) for i in range(lats)])
     part = call(post_kernel, shape(HALF, ROW), [SMEM] + [VMEM] * 4, [], 16, "post")(core, keep, other, wide, own)
     parts = lax.all_to_all(

time: 66.3 us -> 73.2 us (1.10)
  starting transfers between devices: 9.99 us -> 16.4 us
  blocking collectives: 36.6 us -> 38.9 us
  waiting for transfers between devices: 3.41 us -> 1.65 us
    ppermute x0 -> x1, starting transfers between devices: none -> 6.91 us  [on_device(): lax.ppermute(ready, 'lat', [(i, (i + lats // 2) % lats) for i in range(la...]
    all_to_all x1, blocking collectives: 10.3 us -> 13.8 us  [on_device(): shared = lax.all_to_all(share, 'lon', 0, 0, tiled=True)]
    all_to_all x1, waiting for transfers between devices: 2.16 us -> 0.01 us  [on_device(): recv = lax.all_to_all(slots, 'lon', 0, 0, tiled=True)]
    all_to_all x1, blocking collectives: 26.4 us -> 25.1 us  [on_device(): lax.all_to_all(part.reshape(ZED, HALF // ZED, ROW), 'lat', 0, 0, tiled=Tr...]
  transfers between devices with their start and end apart: 2 -> 3, of which waited for: 2 -> 2; matrix products, arithmetic and copies ran while one was open for 0% -> 0% of each run, Pallas kernels for 2% -> 2%
where the time goes in v8:
time: 73.2 us; the launch traced here: 72.6 us
  blocking collectives  38.9 us (53%)
  starting transfers between devices  16.4 us (22%)
  Pallas kernels  9.81 us (13%)
  local copies, waits for them, and re-layouts  4.47 us (6%)
  waiting for transfers between devices  1.65 us (2%)
  between operations  1.38 us (2%)
    all_to_all x1, blocking collectives, on_device(): lax.all_to_all(part.reshape(ZED, HALF // ZED, ROW), 'lat', 0, 0, tiled=Tr...  25.1 us
    all_to_all x1, blocking collectives, on_device(): shared = lax.all_to_all(share, 'lon', 0, 0, tiled=True)  13.8 us
    all_to_all x1, starting transfers between devices, on_device(): recv = lax.all_to_all(slots, 'lon', 0, 0, tiled=True)  7.62 us
    ppermute x1, starting transfers between devices, on_device(): lax.ppermute(ready, 'lat', [(i, (i + lats // 2) % lats) for i in range(la...  6.91 us
    pallas_call x1, Pallas kernels, on_device(): call(main_kernel, (shape(LEFT, TOK, dtype=F32), shape(LEFT, TOK)), [SMEM,...  5.81 us
    unnamed x16, local copies, waits for them, and re-layouts  4.47 us
    ppermute x1, starting transfers between devices, on_device(): other = lax.ppermute(send, 'lat', [(i, i ^ 1) for i in range(lats)])  1.91 us
    pallas_call x1, Pallas kernels, on_device(): call(prep_kernel, (shape(2 * D + 64, D), shape(D, 2 * D), shape(OWN, 2 *...  1.55 us
  transfers between devices with their start and end apart: 3, of which 2 were waited for; matrix products, arithmetic and copies ran while one was open for 0% of the time, Pallas kernels for 2%

profile of v8, /device:TPU:1, one launch (start us, length us, event | category | flops | bytes accessed | tf_op | source)
XLA Modules:
  0.0 72.6 jit_solution(2573321811085275407)
XLA Ops:
  0.6 0.0 copy-start
  0.6 0.0 copy-start.4
  0.7 1.0 %copy-done.4 = bf16[1,1664,80]{1,2,0:T(8,128)(2,1)S(1)} copy-done((bf16[1,1664,80]{1,2,0:T(8,128)(2,1)S(1)}, bf16[1,1664,80]{1,2,0:T(8,128)(2,1)}, u32[]{:S(2)}) %copy-start.4) | copy-done | bytes 266264
  1.7 0.8 %slots.1 = bf16[16,80,128]{2,1,0:T(8,128)(2,1)} custom-call(s32[1]{0:T(128)} %bitcast.1.lon_ref, bf16[80,1664]{1,0:T(8,128)(2,1)S(1)} %bitcast.12), custom_call_target="tpu_custom_call" | custom-call | tf_op jit(solution)/shard_map/slots/pallas_call | solution.py:309
  2.5 7.6 %all-to-all-start = ((bf16[16,80,128]{2,1,0:T(8,128)(2,1)}), bf16[16,80,128]{2,1,0:T(8,128)(2,1)S(1)}, u32[]{:S(2)}, u32[]{:S(2)}) async-start(bf16[16,80,128]{2,1,0:T(8,128)(2,1)} %slots.1), calls=%async_computation | async-start | bytes 655360 | tf_op jit(solution)/shard_map/all_to_all | solution.py:326
  10.1 0.0 copy-done
  10.2 0.0 copy-done.6
  10.2 0.0 copy-start.3
  10.2 1.0 %copy-done.3 = bf16[1,128,3,512]{3,1,2,0:T(8,128)(2,1)S(1)} copy-done((bf16[1,128,3,512]{3,1,2,0:T(8,128)(2,1)S(1)}, bf16[1,128,3,512]{3,1,2,0:T(8,128)(2,1)}, u32[]{:S(2)}) %copy-start.3) | copy-done | bytes 393240
  11.2 0.9 %copy-done.5 = bf16[80,512]{1,0:T(8,128)(2,1)S(1)} copy-done((bf16[80,512]{1,0:T(8,128)(2,1)S(1)}, bf16[80,512]{1,0:T(8,128)(2,1)}, u32[]{:S(2)}) %copy-start.5) | copy-done | bytes 81944
  12.1 0.7 copy-done.7
  12.7 1.6 %prep.1 = (bf16[1088,512]{1,0:T(8,128)(2,1)S(1)}, bf16[512,1024]{1,0:T(8,128)(2,1)S(1)}, bf16[288,1280]{1,0:T(8,128)(2,1)S(1)}, f32[16,128]{1,0:T(8,128)S(1)}) custom-call(s32[1]{0:T(128)} %bitcast.core_ref, bf16[512,1024]{1,0:T(8,128)(2,1)S(1)} %copy-done, bf16[80,512]{1,0:T(8,128)(2,1)S(1)} %copy-done.5, bf16[13,512]{1,0:T(8,128)(2,1)S(1)} %copy-done.6, ...), custom_call_target="tpu_custom_call" | custom-call | tf_op jit(solution)/shard_map/prep/pallas_call | solution.py:318
  14.3 0.9 %copy-done.1 = bf16[288,1280]{1,0:T(8,128)(2,1)} copy-done((bf16[288,1280]{1,0:T(8,128)(2,1)}, bf16[288,1280]{1,0:T(8,128)(2,1)S(1)}, u32[]{:S(2)}) %copy-start.1) | copy-done | bytes 737304
  15.2 6.9 %collective-permute-start = (f32[16,128]{1,0:T(8,128)S(1)}, f32[16,128]{1,0:T(8,128)S(1)}, u32[]{:S(2)}, u32[]{:S(2)}) collective-permute-start(f32[16,128]{1,0:T(8,128)S(1)} %get-tuple-element.14), channel_id=1, source_target_pairs={{0,8},{1,9},{2,10},{3,11},{4,12},{5,13},{6,14},{7,15},{8,0},{9,1},... | collective-permute-start | bytes 24584 | tf_op jit(solution)/shard_map/ppermute | solution.py:328
  22.7 0.4 collective-permute-done.ready_ref
  23.1 0.0 all-to-all-done.recv_ref
  23.1 5.8 %main.1 = (f32[1280,128]{1,0:T(8,128)S(1)}, bf16[1280,128]{1,0:T(8,128)(2,1)S(1)}) custom-call(s32[1]{0:T(128)} %bitcast.1.lon_ref, s32[1]{0:T(128)S(6)} %copy.10.count_ref, bf16[16,80,128]{2,1,0:T(8,128)(2,1)S(1)} %all-to-all-done.recv_ref, bf16[1088,512]{1,0:T(8,128)(2,1)S(1)} %get-tuple-element.12.tall_ref, ...), custom_call_target="tpu_custom_call" | custom-call | tf_op jit(solution)/shard_map/main/pallas_call | solution.py:329
  28.9 1.9 %collective-permute-start.1 = (bf16[1280,128]{1,0:T(8,128)(2,1)S(1)}, bf16[1280,128]{1,0:T(8,128)(2,1)S(1)}, u32[]{:S(2)}, u32[]{:S(2)}) collective-permute-start(bf16[1280,128]{1,0:T(8,128)(2,1)S(1)} %get-tuple-element.16), channel_id=1, source_target_pairs={{0,1},{1,0},{2,3},{3,2},{4,5},{5,4},{6,7},{7,6},{8,9},{9,8},{10,11... | collective-permute-start | bytes 983048 | tf_op jit(solution)/shard_map/ppermute | solution.py:348
  30.8 1.3 %collective-permute-done.1.recv_ref = bf16[1280,128]{1,0:T(8,128)(2,1)S(1)} collective-permute-done((bf16[1280,128]{1,0:T(8,128)(2,1)S(1)}, bf16[1280,128]{1,0:T(8,128)(2,1)S(1)}, u32[]{:S(2)}, u32[]{:S(2)}) %collective-permute-start.1) | collective-permute-done | bytes 327712 | tf_op jit(solution)/shard_map/ppermute | solution.py:348
  32.1 0.6 post.1
  32.7 25.1 %all_to_all.15.part_ref = bf16[8,32,1152]{2,1,0:T(8,128)(2,1)S(1)} all-to-all(bf16[8,32,1152]{2,1,0:T(8,128)(2,1)S(1)} %bitcast.10), channel_id=1, replica_groups={{0,2,4,6,8,10,12,14},{1,3,5,7,9,11,13,15},{16,18,20,22,24,26,28,30},{17..., dimensions={0} | all-to-all | bytes 1179648 | tf_op jit(solution)/shard_map/all_to_all | solution.py:350
  57.9 0.2 sum_z.1
  58.0 13.8 %all_to_all.16.share_ref = bf16[16,48,128]{2,1,0:T(8,128)(2,1)S(1)} all-to-all(bf16[16,48,128]{2,1,0:T(8,128)(2,1)S(1)} %sum_z.1), channel_id=1, replica_groups=mesh['lon'=16,'lat'=16] {'lon'}, dimensions={0} | all-to-all | bytes 393216 | tf_op jit(solution)/shard_map/all_to_all | solution.py:366
  71.8 0.8 %sum_lon.1 = (f32[2,1024]{1,0:T(2,128)}, f32[32,80]{1,0:T(8,128)}, f32[3,512]{1,0:T(4,128)}) custom-call(bf16[16,48,128]{2,1,0:T(8,128)(2,1)S(1)} %all_to_all.16.share_ref), custom_call_target="tpu_custom_call" | custom-call | tf_op jit(solution)/shard_map/sum_lon/pallas_call | solution.py:367
  (6 shorter events, 0.0 us)
Async XLA Ops:
  0.6 9.5 %copy-start = (bf16[512,1024]{1,0:T(8,128)(2,1)S(1)}, bf16[512,1024]{1,0:T(8,128)(2,1)}, u32[]{:S(2)}) copy-start(bf16[512,1024]{1,0:T(8,128)(2,1)} %kvw_ref.1) | copy-start | bytes 3145732
  0.6 1.0 %copy-start.4 = (bf16[1,1664,80]{1,2,0:T(8,128)(2,1)S(1)}, bf16[1,1664,80]{1,2,0:T(8,128)(2,1)}, u32[]{:S(2)}) copy-start(bf16[1,1664,80]{1,2,0:T(8,128)(2,1)} %param.7) | copy-start | bytes 798724
  1.7 8.5 %copy-start.6 = (bf16[13,512]{1,0:T(8,128)(2,1)S(1)}, bf16[13,512]{1,0:T(8,128)(2,1)}, u32[]{:S(2)}) copy-start(bf16[13,512]{1,0:T(8,128)(2,1)} %level_ref.1) | copy-start | bytes 39940
  2.5 20.6 %all-to-all-start = ((bf16[16,80,128]{2,1,0:T(8,128)(2,1)}), bf16[16,80,128]{2,1,0:T(8,128)(2,1)S(1)}, u32[]{:S(2)}, u32[]{:S(2)}) async-start(bf16[16,80,128]{2,1,0:T(8,128)(2,1)} %slots.1), calls=%async_computation | async-start | bytes 655360 | tf_op jit(solution)/shard_map/all_to_all | solution.py:326
  10.2 1.0 %copy-start.3 = (bf16[1,128,3,512]{3,1,2,0:T(8,128)(2,1)S(1)}, bf16[1,128,3,512]{3,1,2,0:T(8,128)(2,1)}, u32[]{:S(2)}) copy-start(bf16[1,128,3,512]{3,1,2,0:T(8,128)(2,1)} %param.13) | copy-start | bytes 1179652
  11.2 0.9 %copy-start.5 = (bf16[80,512]{1,0:T(8,128)(2,1)S(1)}, bf16[80,512]{1,0:T(8,128)(2,1)}, u32[]{:S(2)}) copy-start(bf16[80,512]{1,0:T(8,128)(2,1)} %embed_w_ref.1) | copy-start | bytes 245764
  12.1 0.7 copy-start.7
  14.3 0.9 %copy-start.1 = (bf16[288,1280]{1,0:T(8,128)(2,1)}, bf16[288,1280]{1,0:T(8,128)(2,1)S(1)}, u32[]{:S(2)}) copy-start(bf16[288,1280]{1,0:T(8,128)(2,1)S(1)} %get-tuple-element.17.own_ref) | copy-start | bytes 2211844
  15.2 7.9 %collective-permute-start = (f32[16,128]{1,0:T(8,128)S(1)}, f32[16,128]{1,0:T(8,128)S(1)}, u32[]{:S(2)}, u32[]{:S(2)}) collective-permute-start(f32[16,128]{1,0:T(8,128)S(1)} %get-tuple-element.14), channel_id=1, source_target_pairs={{0,8},{1,9},{2,10},{3,11},{4,12},{5,13},{6,14},{7,15},{8,0},{9,1},... | collective-permute-start | bytes 24584 | tf_op jit(solution)/shard_map/ppermute | solution.py:328
  23.1 9.0 %copy-start.2 = (bf16[288,1280]{1,0:T(8,128)(2,1)S(1)}, bf16[288,1280]{1,0:T(8,128)(2,1)}, u32[]{:S(2)}) copy-start(bf16[288,1280]{1,0:T(8,128)(2,1)} %copy-done.1) | copy-start | bytes 2211844
  28.9 3.2 %collective-permute-start.1 = (bf16[1280,128]{1,0:T(8,128)(2,1)S(1)}, bf16[1280,128]{1,0:T(8,128)(2,1)S(1)}, u32[]{:S(2)}, u32[]{:S(2)}) collective-permute-start(bf16[1280,128]{1,0:T(8,128)(2,1)S(1)} %get-tuple-element.16), channel_id=1, source_target_pairs={{0,1},{1,0},{2,3},{3,2},{4,5},{5,4},{6,7},{7,6},{8,9},{9,8},{10,11... | collective-permute-start | bytes 983048 | tf_op jit(solution)/shard_map/ppermute | solution.py:348

commit v9 on v6

--- a/solution.py
+++ b/solution.py
@@ -34,6 +34,7 @@
 QBD = 256
 GRAD = 384
 QUERY = 768
+RAW = 1024
 DEEP = 256
 ROW = 2 * D + TOK
 SHARE = 48
@@ -79,6 +80,10 @@
     rows[:FEAT, :] = embed_w_ref[...].astype(F32)
     rows[FEAT : FEAT + LEVELS, :] = level_ref[...].astype(F32)
     weights = rows[...]
+    spread[...] = jnp.zeros_like(spread)
+    spread[:AUG, :] = weights
+    plain[:, :TOK] = spread[:TOK, :].T.astype(BF16)
+    wide_ref[:, RAW : RAW + TOK] = jnp.dot(reorder, plain[:, :TOK], preferred_element_type=F32).astype(BF16)
     weights = weights - jnp.mean(weights, axis=1, keepdims=True)
     high = weights.astype(BF16)
     spread[...] = jnp.zeros_like(spread)
@@ -129,8 +134,7 @@
     left_s[2 * D : 2 * D + 32, :] = jnp.zeros((32, SPAN), BF16)
     left_s[2 * D + GS + AUG :, :] = jnp.zeros((TOK - AUG, SPAN), BF16)
     pin_s[AUG:, :] = jnp.zeros((TOK - AUG, SPAN), BF16)
-    for start in (AUG, TOK + AUG):
-        paug_s[start : start + TOK - AUG, :] = jnp.zeros((TOK - AUG, SPAN), BF16)
+    paug_s[AUG:, :] = jnp.zeros((TOK - AUG, SPAN), BF16)
 
     def lanes_of(group):
         return slice(group[0] * TOK, (group[-1] + 1) * TOK)
@@ -142,10 +146,10 @@
             lanes = slice(l * TOK, (l + 1) * TOK)
             patches = recv_ref[(RING * l + lon) // LEVELS]
             one_hot = jnp.where(row == l, 1.0, 0.0).astype(BF16)
-            for start in (0, TOK):
-                paug_s[start : start + FEAT, lanes] = patches
-                paug_s[start + FEAT : start + AUG, lanes] = one_hot
-        center = jnp.dot(wide_ref[:, WAUG : WAUG + DEEP], paug_s[:, at], preferred_element_type=F32)
+            paug_s[:FEAT, lanes] = patches
+            paug_s[FEAT:AUG, lanes] = one_hot
+        embedded = jnp.dot(wide_ref[:, RAW : RAW + TOK], paug_s[:, at], preferred_element_type=F32)
+        center = embedded - jnp.mean(embedded, axis=0, keepdims=True)
         inv_std = lax.rsqrt(jnp.mean(center * center, axis=0, keepdims=True) + EPSILON)
         inv_s[:, at] = inv_std
         hid_s[:, at] = (center * inv_std).astype(BF16)
@@ -315,7 +319,7 @@
     )(lon, level_patches[0].T)
     tall, wide, own = call(
         prep_kernel,
-        (shape(2 * D + 64, D), shape(D, 2 * D), shape(OWN, 2 * D + DEEP)),
+        (shape(2 * D + 64, D), shape(D, RAW + TOK), shape(OWN, 2 * D + DEEP)),
         [SMEM] + [VMEM] * 5,
         [pltpu.VMEM((AUG, D), F32), pltpu.VMEM((DEEP, D), F32), pltpu.VMEM((D, DEEP), BF16)],
         24,
@@ -328,7 +332,7 @@
         [SMEM, SMEM] + [VMEM] * 3,
         [
             pltpu.VMEM((LATENT, D, TOK), F32),
-            pltpu.VMEM((DEEP, SPAN), BF16),
+            pltpu.VMEM((TOK, SPAN), BF16),
             pltpu.VMEM((D, SPAN), BF16),
             pltpu.VMEM((2 * D, SPAN), BF16),
             pltpu.VMEM((LEFT, SPAN), BF16),

time: 66.3 us -> 66.4 us (level)
  local copies, waits for them, and re-layouts: 4.46 us -> 3.17 us
  waiting for transfers between devices: 3.41 us -> 4.35 us
    unnamed x16 -> x12, local copies, waits for them, and re-layouts: 4.46 us -> 3.17 us
    all_to_all x1, waiting for transfers between devices: 2.16 us -> 3.09 us  [on_device(): recv = lax.all_to_all(slots, 'lon', 0, 0, tiled=True)]
  transfers between devices with their start and end apart: 2 -> 2, of which waited for: 2 -> 2; matrix products, arithmetic and copies ran while one was open for 0% -> 0% of each run, Pallas kernels for 2% -> 3%
where the time goes in v9:
time: 66.4 us; the launch traced here: 65.8 us
  blocking collectives  36.6 us (55%)
  Pallas kernels  10.3 us (16%)
  starting transfers between devices  9.98 us (15%)
  waiting for transfers between devices  4.35 us (7%)
  local copies, waits for them, and re-layouts  3.17 us (5%)
  between operations  1.38 us (2%)
    all_to_all x1, blocking collectives, on_device(): lax.all_to_all(part.reshape(ZED, HALF // ZED, ROW), 'lat', 0, 0, tiled=Tr...  26.4 us
    all_to_all x1, blocking collectives, on_device(): shared = lax.all_to_all(share, 'lon', 0, 0, tiled=True)  10.2 us
    all_to_all x1, starting transfers between devices, on_device(): recv = lax.all_to_all(slots, 'lon', 0, 0, tiled=True)  7.6 us
    pallas_call x1, Pallas kernels, on_device(): call(main_kernel, (shape(LEFT, TOK, dtype=F32), shape(LEFT, TOK)), [SMEM,...  6.05 us
    unnamed x12, local copies, waits for them, and re-layouts  3.17 us
    all_to_all x1, waiting for transfers between devices, on_device(): recv = lax.all_to_all(slots, 'lon', 0, 0, tiled=True)  3.09 us
    ppermute x1, starting transfers between devices, on_device(): other = lax.ppermute(send, 'lat', [(i, i ^ 1) for i in range(lats)])  2.38 us
    pallas_call x1, Pallas kernels, on_device(): call(prep_kernel, (shape(2 * D + 64, D), shape(D, RAW + TOK), shape(OWN,...  1.82 us
  transfers between devices with their start and end apart: 2, of which 2 were waited for; matrix products, arithmetic and copies ran while one was open for 0% of the time, Pallas kernels for 3%

profile of v9, /device:TPU:1, one launch (start us, length us, event | category | flops | bytes accessed | tf_op | source)
XLA Modules:
  0.0 65.8 jit_solution(13888518632150248489)
XLA Ops:
  0.6 0.0 copy-start.5
  0.6 0.0 copy-start.2
  0.7 0.9 %copy-done.2 = bf16[1,1664,80]{1,2,0:T(8,128)(2,1)S(1)} copy-done((bf16[1,1664,80]{1,2,0:T(8,128)(2,1)S(1)}, bf16[1,1664,80]{1,2,0:T(8,128)(2,1)}, u32[]{:S(2)}) %copy-start.2) | copy-done | bytes 266264
  1.6 0.0 copy-start.3
  1.6 0.0 copy-start.4
  1.6 0.8 %slots.1 = bf16[16,80,128]{2,1,0:T(8,128)(2,1)} custom-call(s32[1]{0:T(128)} %bitcast.1.lon_ref, bf16[80,1664]{1,0:T(8,128)(2,1)S(1)} %bitcast.12), custom_call_target="tpu_custom_call" | custom-call | tf_op jit(solution)/shard_map/slots/pallas_call | solution.py:311
  2.4 7.6 %all-to-all-start = ((bf16[16,80,128]{2,1,0:T(8,128)(2,1)}), bf16[16,80,128]{2,1,0:T(8,128)(2,1)S(1)}, u32[]{:S(2)}, u32[]{:S(2)}) async-start(bf16[16,80,128]{2,1,0:T(8,128)(2,1)} %slots.1), calls=%async_computation | async-start | bytes 655360 | tf_op jit(solution)/shard_map/all_to_all | solution.py:328
  10.7 0.0 copy-done.5
  10.7 0.0 copy-done.3
  10.7 0.0 copy-done.4
  10.7 0.0 copy-start
  10.7 1.2 %copy-done = bf16[512,1024]{1,0:T(8,128)(2,1)S(1)} copy-done((bf16[512,1024]{1,0:T(8,128)(2,1)S(1)}, bf16[512,1024]{1,0:T(8,128)(2,1)}, u32[]{:S(2)}) %copy-start) | copy-done | bytes 1048600
  12.0 0.0 copy-start.1
  12.0 1.0 %copy-done.1 = bf16[1,128,3,512]{3,1,2,0:T(8,128)(2,1)S(1)} copy-done((bf16[1,128,3,512]{3,1,2,0:T(8,128)(2,1)S(1)}, bf16[1,128,3,512]{3,1,2,0:T(8,128)(2,1)}, u32[]{:S(2)}) %copy-start.1) | copy-done | bytes 393240
  12.9 1.8 %prep.1 = (bf16[1088,512]{1,0:T(8,128)(2,1)S(1)}, bf16[512,1152]{1,0:T(8,128)(2,1)S(1)}, bf16[288,1280]{1,0:T(8,128)(2,1)S(1)}) custom-call(s32[1]{0:T(128)} %bitcast.core_ref, bf16[512,1024]{1,0:T(8,128)(2,1)S(1)} %copy-done, bf16[80,512]{1,0:T(8,128)(2,1)S(1)} %copy-done.3, bf16[13,512]{1,0:T(8,128)(2,1)S(1)} %copy-done.4, bf16[3,512]{1,0:T(4,128)(2,1)S(1)} %copy-done.5, ...), custom_call_target="tpu_custom_call" | custom-call | tf_op jit(solution)/shard_map/prep/pallas_call | solution.py:320
  14.8 3.1 %all-to-all-done.recv_ref = bf16[16,80,128]{2,1,0:T(8,128)(2,1)S(1)} async-done(((bf16[16,80,128]{2,1,0:T(8,128)(2,1)}), bf16[16,80,128]{2,1,0:T(8,128)(2,1)S(1)}, u32[]{:S(2)}, u32[]{:S(2)}) %all-to-all-start) | async-done | bytes 327712 | tf_op jit(solution)/shard_map/all_to_all | solution.py:328
  17.9 6.0 %main.1 = (f32[1280,128]{1,0:T(8,128)S(1)}, bf16[1280,128]{1,0:T(8,128)(2,1)S(1)}) custom-call(s32[1]{0:T(128)} %bitcast.1.lon_ref, s32[1]{0:T(128)S(6)} %copy.10.count_ref, bf16[16,80,128]{2,1,0:T(8,128)(2,1)S(1)} %all-to-all-done.recv_ref, bf16[1088,512]{1,0:T(8,128)(2,1)S(1)} %get-tuple-element.11.tall_ref, bf16[512,1152]{1,0:T(8,128)(2,1)S(1)} %get-tuple-element.12.wide_ref), custom_call_target="tpu_custom_call" | custom-call | tf_op jit(solution)/shard_map/main/pallas_call | solution.py:329
  23.9 2.4 %collective-permute-start = (bf16[1280,128]{1,0:T(8,128)(2,1)S(1)}, bf16[1280,128]{1,0:T(8,128)(2,1)S(1)}, u32[]{:S(2)}, u32[]{:S(2)}) collective-permute-start(bf16[1280,128]{1,0:T(8,128)(2,1)S(1)} %get-tuple-element.14), channel_id=1, source_target_pairs={{0,1},{1,0},{2,3},{3,2},{4,5},{5,4},{6,7},{7,6},{8,9},{9,8},{10,11... | collective-permute-start | bytes 983048 | tf_op jit(solution)/shard_map/ppermute | solution.py:349
  26.3 1.3 %collective-permute-done.recv_ref = bf16[1280,128]{1,0:T(8,128)(2,1)S(1)} collective-permute-done((bf16[1280,128]{1,0:T(8,128)(2,1)S(1)}, bf16[1280,128]{1,0:T(8,128)(2,1)S(1)}, u32[]{:S(2)}, u32[]{:S(2)}) %collective-permute-start) | collective-permute-done | bytes 327712 | tf_op jit(solution)/shard_map/ppermute | solution.py:349
  27.6 0.6 post.1
  28.2 26.4 %all_to_all.15.part_ref = bf16[8,32,1152]{2,1,0:T(8,128)(2,1)S(1)} all-to-all(bf16[8,32,1152]{2,1,0:T(8,128)(2,1)S(1)} %bitcast.10), channel_id=1, replica_groups={{0,2,4,6,8,10,12,14},{1,3,5,7,9,11,13,15},{16,18,20,22,24,26,28,30},{17..., dimensions={0} | all-to-all | bytes 1179648 | tf_op jit(solution)/shard_map/all_to_all | solution.py:351
  54.6 0.2 sum_z.1
  54.7 10.2 %all_to_all.16.share_ref = bf16[16,48,128]{2,1,0:T(8,128)(2,1)S(1)} all-to-all(bf16[16,48,128]{2,1,0:T(8,128)(2,1)S(1)} %sum_z.1), channel_id=1, replica_groups=mesh['lon'=16,'lat'=16] {'lon'}, dimensions={0} | all-to-all | bytes 393216 | tf_op jit(solution)/shard_map/all_to_all | solution.py:367
  64.9 0.8 %sum_lon.1 = (f32[2,1024]{1,0:T(2,128)}, f32[32,80]{1,0:T(8,128)}, f32[3,512]{1,0:T(4,128)}) custom-call(bf16[16,48,128]{2,1,0:T(8,128)(2,1)S(1)} %all_to_all.16.share_ref), custom_call_target="tpu_custom_call" | custom-call | tf_op jit(solution)/shard_map/sum_lon/pallas_call | solution.py:368
Async XLA Ops:
  0.6 10.1 %copy-start.5 = (bf16[3,512]{1,0:T(4,128)(2,1)S(1)}, bf16[3,512]{1,0:T(4,128)(2,1)}, u32[]{:S(2)}) copy-start(bf16[3,512]{1,0:T(4,128)(2,1)} %query_ref.1) | copy-start | bytes 9220
  0.6 1.0 %copy-start.2 = (bf16[1,1664,80]{1,2,0:T(8,128)(2,1)S(1)}, bf16[1,1664,80]{1,2,0:T(8,128)(2,1)}, u32[]{:S(2)}) copy-start(bf16[1,1664,80]{1,2,0:T(8,128)(2,1)} %param.7) | copy-start | bytes 798724
  1.6 9.1 %copy-start.3 = (bf16[80,512]{1,0:T(8,128)(2,1)S(1)}, bf16[80,512]{1,0:T(8,128)(2,1)}, u32[]{:S(2)}) copy-start(bf16[80,512]{1,0:T(8,128)(2,1)} %embed_w_ref.1) | copy-start | bytes 245764
  1.6 9.1 %copy-start.4 = (bf16[13,512]{1,0:T(8,128)(2,1)S(1)}, bf16[13,512]{1,0:T(8,128)(2,1)}, u32[]{:S(2)}) copy-start(bf16[13,512]{1,0:T(8,128)(2,1)} %level_ref.1) | copy-start | bytes 39940
  2.4 15.4 %all-to-all-start = ((bf16[16,80,128]{2,1,0:T(8,128)(2,1)}), bf16[16,80,128]{2,1,0:T(8,128)(2,1)S(1)}, u32[]{:S(2)}, u32[]{:S(2)}) async-start(bf16[16,80,128]{2,1,0:T(8,128)(2,1)} %slots.1), calls=%async_computation | async-start | bytes 655360 | tf_op jit(solution)/shard_map/all_to_all | solution.py:328
  10.7 1.2 %copy-start = (bf16[512,1024]{1,0:T(8,128)(2,1)S(1)}, bf16[512,1024]{1,0:T(8,128)(2,1)}, u32[]{:S(2)}) copy-start(bf16[512,1024]{1,0:T(8,128)(2,1)} %kvw_ref.1) | copy-start | bytes 3145732
  12.0 1.0 %copy-start.1 = (bf16[1,128,3,512]{3,1,2,0:T(8,128)(2,1)S(1)}, bf16[1,128,3,512]{3,1,2,0:T(8,128)(2,1)}, u32[]{:S(2)}) copy-start(bf16[1,128,3,512]{3,1,2,0:T(8,128)(2,1)} %param.13) | copy-start | bytes 1179652
  23.9 3.6 %collective-permute-start = (bf16[1280,128]{1,0:T(8,128)(2,1)S(1)}, bf16[1280,128]{1,0:T(8,128)(2,1)S(1)}, u32[]{:S(2)}, u32[]{:S(2)}) collective-permute-start(bf16[1280,128]{1,0:T(8,128)(2,1)S(1)} %get-tuple-element.14), channel_id=1, source_target_pairs={{0,1},{1,0},{2,3},{3,2},{4,5},{5,4},{6,7},{7,6},{8,9},{9,8},{10,11... | collective-permute-start | bytes 983048 | tf_op jit(solution)/shard_map/ppermute | solution.py:349

commit v10 on v9

--- a/solution.py
+++ b/solution.py
@@ -24,7 +24,7 @@
 LATENT = 3
 AH = LATENT * HEADS
 GS = 128
-LEFT = 2 * D + 2 * GS
+LEFT = D + 2 * GS
 OWN = D // 2 + 32
 NT = (((1,), (1,)), ((), ()))
 RING = 16
@@ -131,8 +131,8 @@
     count = count_ref[0]
     for a in range(LATENT):
         g_s[a] = wide_ref[:, GRAD + a * TOK : GRAD + (a + 1) * TOK].astype(F32)
-    left_s[2 * D : 2 * D + 32, :] = jnp.zeros((32, SPAN), BF16)
-    left_s[2 * D + GS + AUG :, :] = jnp.zeros((TOK - AUG, SPAN), BF16)
+    left_s[D : D + 32, :] = jnp.zeros((32, SPAN), BF16)
+    left_s[D + GS + AUG :, :] = jnp.zeros((TOK - AUG, SPAN), BF16)
     pin_s[AUG:, :] = jnp.zeros((TOK - AUG, SPAN), BF16)
     paug_s[AUG:, :] = jnp.zeros((TOK - AUG, SPAN), BF16)
 
@@ -201,17 +201,13 @@
         grad_score = attention * (grad_attn - inner)
         slope = jnp.sum(grad_score * sc_s[:, lanes] + weight * grad_attn, axis=0, keepdims=True)
         scale = slope * inv_s[:, lanes] * (1.0 / D)
-        left_s[2 * D + GS : 2 * D + GS + AUG, lanes] = (paug_s[:AUG, lanes].astype(F32) * scale).astype(BF16)
+        left_s[D + GS : D + GS + AUG, lanes] = (paug_s[:AUG, lanes].astype(F32) * scale).astype(BF16)
         grad_score = grad_score * SCORE_SCALE
         high = grad_score.astype(BF16)
-        left_s[2 * D + 32 : 2 * D + 80, lanes] = (grad_score - high.astype(F32)).astype(BF16)
-        left_s[2 * D + 80 : 2 * D + GS, lanes] = high
-
-    def grad_kv(group):
-        at = lanes_of(group)
-        left_s[:D, at] = jnp.dot(
-            wide_ref[:, QBD : QBD + GS], left_s[2 * D : 2 * D + GS, at], preferred_element_type=F32
-        ).astype(BF16)
+        left_s[D + 32 : D + 80, lanes] = (grad_score - high.astype(F32)).astype(BF16)
+        left_s[D + 80 : D + GS, lanes] = high
+
+    def grad_values_of(group):
         for h in range(HEADS):
             rows = slice(h * HEAD, (h + 1) * HEAD)
             grads = [g_s[a, rows, :] for a in range(LATENT)]
@@ -221,9 +217,9 @@
                 for a in range(LATENT):
                     term = w_s[a * HEADS + h : a * HEADS + h + 1, lanes] * grads[a]
                     grad_values = term if grad_values is None else grad_values + term
-                left_s[D + h * HEAD : D + (h + 1) * HEAD, lanes] = grad_values.astype(BF16)
-
-    grad_kv(every)
+                left_s[rows, lanes] = grad_values.astype(BF16)
+
+    grad_values_of(every)
 
     outer = lax.dot_general(left_s[...], pin_s[...], NT, preferred_element_type=F32)
     keep_out[...] = outer
@@ -232,7 +228,16 @@
 
 def post_kernel(core_ref, keep_ref, recv_ref, wide_ref, own_ref, part_ref):
     total = keep_ref[...] + recv_ref[...].astype(F32)
-    outer = total[: 2 * D]
+    scores = total[D : D + GS]
+    scores = scores[80:] + scores[32:80]
+    high = scores.astype(BF16)
+    low = (scores - high.astype(F32)).astype(BF16)
+    outer = jnp.dot(
+        wide_ref[:, QBD : QBD + GS],
+        jnp.concatenate([jnp.zeros((32, TOK), BF16), low, high], axis=0),
+        preferred_element_type=F32,
+    )
+    outer = jnp.concatenate([outer, total[:D]], axis=0)
     high = outer.astype(BF16)
     low = (outer - high.astype(F32)).astype(BF16)
     start = pl.multiple_of(core_ref[0] * HALF, HALF)
@@ -244,14 +249,13 @@
     ).astype(BF16)
     grads = jnp.dot(own_ref[:, : 2 * D], jnp.concatenate([high, low], axis=1), preferred_element_type=F32)
     grads = grads[:, :TOK] + grads[:, TOK:]
-    gram = total[2 * D + GS :].astype(BF16)
+    gram = total[D + GS :].astype(BF16)
     grads = (
         grads[:HALF]
         - (grads[HALF : HALF + 1] + grads[HALF + 1 : HALF + 2])
         - jnp.dot(own_ref[:HALF, 2 * D :], jnp.concatenate([gram, gram], axis=0), preferred_element_type=F32)
     )
-    scores = total[2 * D : 2 * D + GS]
-    scores = jnp.concatenate([jnp.zeros((FEAT, TOK), F32), scores[80:] + scores[32:80]], axis=0).astype(BF16)
+    scores = jnp.concatenate([jnp.zeros((FEAT, TOK), F32), scores], axis=0).astype(BF16)
     queries = lax.dot_general(
         wide_ref[:, QUERY : QUERY + DEEP],
         jnp.concatenate([scores, scores], axis=1),

time: 66.4 us -> 66.1 us (level)
  no operation moved by 1% of the time
where the time goes in v10:
time: 66.1 us; the launch traced here: 65.5 us
  blocking collectives  36.6 us (55%)
  Pallas kernels  10.2 us (15%)
  starting transfers between devices  9.97 us (15%)
  waiting for transfers between devices  4.16 us (6%)
  local copies, waits for them, and re-layouts  3.17 us (5%)
  between operations  1.38 us (2%)
    all_to_all x1, blocking collectives, on_device(): lax.all_to_all(part.reshape(ZED, HALF // ZED, ROW), 'lat', 0, 0, tiled=Tr...  26.4 us
    all_to_all x1, blocking collectives, on_device(): shared = lax.all_to_all(share, 'lon', 0, 0, tiled=True)  10.2 us
    all_to_all x1, starting transfers between devices, on_device(): recv = lax.all_to_all(slots, 'lon', 0, 0, tiled=True)  7.6 us
    pallas_call x1, Pallas kernels, on_device(): call(main_kernel, (shape(LEFT, TOK, dtype=F32), shape(LEFT, TOK)), [SMEM,...  5.82 us
    unnamed x12, local copies, waits for them, and re-layouts  3.17 us
    all_to_all x1, waiting for transfers between devices, on_device(): recv = lax.all_to_all(slots, 'lon', 0, 0, tiled=True)  3.09 us
    ppermute x1, starting transfers between devices, on_device(): other = lax.ppermute(send, 'lat', [(i, i ^ 1) for i in range(lats)])  2.37 us
    pallas_call x1, Pallas kernels, on_device(): call(prep_kernel, (shape(2 * D + 64, D), shape(D, RAW + TOK), shape(OWN,...  1.82 us
  transfers between devices with their start and end apart: 2, of which 2 were waited for; matrix products, arithmetic and copies ran while one was open for 0% of the time, Pallas kernels for 3%

profile of v10, /device:TPU:1, one launch (start us, length us, event | category | flops | bytes accessed | tf_op | source)
XLA Modules:
  0.0 65.5 jit_solution(4311321099615240072)
XLA Ops:
  0.6 0.0 copy-start.5
  0.6 0.0 copy-start.2
  0.7 0.9 %copy-done.2 = bf16[1,1664,80]{1,2,0:T(8,128)(2,1)S(1)} copy-done((bf16[1,1664,80]{1,2,0:T(8,128)(2,1)S(1)}, bf16[1,1664,80]{1,2,0:T(8,128)(2,1)}, u32[]{:S(2)}) %copy-start.2) | copy-done | bytes 266264
  1.6 0.0 copy-start.3
  1.6 0.0 copy-start.4
  1.6 0.8 %slots.1 = bf16[16,80,128]{2,1,0:T(8,128)(2,1)} custom-call(s32[1]{0:T(128)} %bitcast.1.lon_ref, bf16[80,1664]{1,0:T(8,128)(2,1)S(1)} %bitcast.12), custom_call_target="tpu_custom_call" | custom-call | tf_op jit(solution)/shard_map/slots/pallas_call | solution.py:315
  2.4 7.6 %all-to-all-start = ((bf16[16,80,128]{2,1,0:T(8,128)(2,1)}), bf16[16,80,128]{2,1,0:T(8,128)(2,1)S(1)}, u32[]{:S(2)}, u32[]{:S(2)}) async-start(bf16[16,80,128]{2,1,0:T(8,128)(2,1)} %slots.1), calls=%async_computation | async-start | bytes 655360 | tf_op jit(solution)/shard_map/all_to_all | solution.py:332
  10.7 0.0 copy-done.5
  10.7 0.0 copy-done.3
  10.7 0.0 copy-done.4
  10.7 0.0 copy-start
  10.7 1.2 %copy-done = bf16[512,1024]{1,0:T(8,128)(2,1)S(1)} copy-done((bf16[512,1024]{1,0:T(8,128)(2,1)S(1)}, bf16[512,1024]{1,0:T(8,128)(2,1)}, u32[]{:S(2)}) %copy-start) | copy-done | bytes 1048600
  12.0 0.0 copy-start.1
  12.0 1.0 %copy-done.1 = bf16[1,128,3,512]{3,1,2,0:T(8,128)(2,1)S(1)} copy-done((bf16[1,128,3,512]{3,1,2,0:T(8,128)(2,1)S(1)}, bf16[1,128,3,512]{3,1,2,0:T(8,128)(2,1)}, u32[]{:S(2)}) %copy-start.1) | copy-done | bytes 393240
  12.9 1.8 %prep.1 = (bf16[1088,512]{1,0:T(8,128)(2,1)S(1)}, bf16[512,1152]{1,0:T(8,128)(2,1)S(1)}, bf16[288,1280]{1,0:T(8,128)(2,1)S(1)}) custom-call(s32[1]{0:T(128)} %bitcast.core_ref, bf16[512,1024]{1,0:T(8,128)(2,1)S(1)} %copy-done, bf16[80,512]{1,0:T(8,128)(2,1)S(1)} %copy-done.3, bf16[13,512]{1,0:T(8,128)(2,1)S(1)} %copy-done.4, bf16[3,512]{1,0:T(4,128)(2,1)S(1)} %copy-done.5, ...), custom_call_target="tpu_custom_call" | custom-call | tf_op jit(solution)/shard_map/prep/pallas_call | solution.py:324
  14.8 3.1 %all-to-all-done.recv_ref = bf16[16,80,128]{2,1,0:T(8,128)(2,1)S(1)} async-done(((bf16[16,80,128]{2,1,0:T(8,128)(2,1)}), bf16[16,80,128]{2,1,0:T(8,128)(2,1)S(1)}, u32[]{:S(2)}, u32[]{:S(2)}) %all-to-all-start) | async-done | bytes 327712 | tf_op jit(solution)/shard_map/all_to_all | solution.py:332
  17.9 5.8 %main.1 = (f32[768,128]{1,0:T(8,128)S(1)}, bf16[768,128]{1,0:T(8,128)(2,1)S(1)}) custom-call(s32[1]{0:T(128)} %bitcast.1.lon_ref, s32[1]{0:T(128)S(6)} %copy.10.count_ref, bf16[16,80,128]{2,1,0:T(8,128)(2,1)S(1)} %all-to-all-done.recv_ref, bf16[1088,512]{1,0:T(8,128)(2,1)S(1)} %get-tuple-element.11.tall_ref, bf16[512,1152]{1,0:T(8,128)(2,1)S(1)} %get-tuple-element.12.wide_ref), custom_call_target="tpu_custom_call" | custom-call | tf_op jit(solution)/shard_map/main/pallas_call | solution.py:333
  23.7 2.4 %collective-permute-start = (bf16[768,128]{1,0:T(8,128)(2,1)S(1)}, bf16[768,128]{1,0:T(8,128)(2,1)S(1)}, u32[]{:S(2)}, u32[]{:S(2)}) collective-permute-start(bf16[768,128]{1,0:T(8,128)(2,1)S(1)} %get-tuple-element.14), channel_id=1, source_target_pairs={{0,1},{1,0},{2,3},{3,2},{4,5},{5,4},{6,7},{7,6},{8,9},{9,8},{10,11... | collective-permute-start | bytes 589832 | tf_op jit(solution)/shard_map/ppermute | solution.py:353
  26.1 1.1 %collective-permute-done.recv_ref = bf16[768,128]{1,0:T(8,128)(2,1)S(1)} collective-permute-done((bf16[768,128]{1,0:T(8,128)(2,1)S(1)}, bf16[768,128]{1,0:T(8,128)(2,1)S(1)}, u32[]{:S(2)}, u32[]{:S(2)}) %collective-permute-start) | collective-permute-done | bytes 196640 | tf_op jit(solution)/shard_map/ppermute | solution.py:353
  27.1 0.8 %post.1 = bf16[256,1152]{1,0:T(8,128)(2,1)S(1)} custom-call(s32[1]{0:T(128)} %bitcast.core_ref, f32[768,128]{1,0:T(8,128)S(1)} %get-tuple-element.13.keep_ref, bf16[768,128]{1,0:T(8,128)(2,1)S(1)} %collective-permute-done.recv_ref, bf16[512,1152]{1,0:T(8,128)(2,1)S(1)} %get-tuple-element.12.wide_ref, bf16[288,1280]{1,0:T(8,128)(2,1)S(1)} %get-tuple-element.15.own_ref), custom_call_target="tpu_custom_call" | custom-call | tf_op jit(solution)/shard_map/post/pallas_call | solution.py:354
  27.9 26.4 %all_to_all.15.part_ref = bf16[8,32,1152]{2,1,0:T(8,128)(2,1)S(1)} all-to-all(bf16[8,32,1152]{2,1,0:T(8,128)(2,1)S(1)} %bitcast.10), channel_id=1, replica_groups={{0,2,4,6,8,10,12,14},{1,3,5,7,9,11,13,15},{16,18,20,22,24,26,28,30},{17..., dimensions={0} | all-to-all | bytes 1179648 | tf_op jit(solution)/shard_map/all_to_all | solution.py:355
  54.3 0.2 sum_z.1
  54.5 10.2 %all_to_all.16.share_ref = bf16[16,48,128]{2,1,0:T(8,128)(2,1)S(1)} all-to-all(bf16[16,48,128]{2,1,0:T(8,128)(2,1)S(1)} %sum_z.1), channel_id=1, replica_groups=mesh['lon'=16,'lat'=16] {'lon'}, dimensions={0} | all-to-all | bytes 393216 | tf_op jit(solution)/shard_map/all_to_all | solution.py:371
  64.7 0.8 %sum_lon.1 = (f32[2,1024]{1,0:T(2,128)}, f32[32,80]{1,0:T(8,128)}, f32[3,512]{1,0:T(4,128)}) custom-call(bf16[16,48,128]{2,1,0:T(8,128)(2,1)S(1)} %all_to_all.16.share_ref), custom_call_target="tpu_custom_call" | custom-call | tf_op jit(solution)/shard_map/sum_lon/pallas_call | solution.py:372
Async XLA Ops:
  0.6 10.1 %copy-start.5 = (bf16[3,512]{1,0:T(4,128)(2,1)S(1)}, bf16[3,512]{1,0:T(4,128)(2,1)}, u32[]{:S(2)}) copy-start(bf16[3,512]{1,0:T(4,128)(2,1)} %query_ref.1) | copy-start | bytes 9220
  0.6 1.0 %copy-start.2 = (bf16[1,1664,80]{1,2,0:T(8,128)(2,1)S(1)}, bf16[1,1664,80]{1,2,0:T(8,128)(2,1)}, u32[]{:S(2)}) copy-start(bf16[1,1664,80]{1,2,0:T(8,128)(2,1)} %param.7) | copy-start | bytes 798724
  1.6 9.1 %copy-start.3 = (bf16[80,512]{1,0:T(8,128)(2,1)S(1)}, bf16[80,512]{1,0:T(8,128)(2,1)}, u32[]{:S(2)}) copy-start(bf16[80,512]{1,0:T(8,128)(2,1)} %embed_w_ref.1) | copy-start | bytes 245764
  1.6 9.1 %copy-start.4 = (bf16[13,512]{1,0:T(8,128)(2,1)S(1)}, bf16[13,512]{1,0:T(8,128)(2,1)}, u32[]{:S(2)}) copy-start(bf16[13,512]{1,0:T(8,128)(2,1)} %level_ref.1) | copy-start | bytes 39940
  2.4 15.4 %all-to-all-start = ((bf16[16,80,128]{2,1,0:T(8,128)(2,1)}), bf16[16,80,128]{2,1,0:T(8,128)(2,1)S(1)}, u32[]{:S(2)}, u32[]{:S(2)}) async-start(bf16[16,80,128]{2,1,0:T(8,128)(2,1)} %slots.1), calls=%async_computation | async-start | bytes 655360 | tf_op jit(solution)/shard_map/all_to_all | solution.py:332
  10.7 1.2 %copy-start = (bf16[512,1024]{1,0:T(8,128)(2,1)S(1)}, bf16[512,1024]{1,0:T(8,128)(2,1)}, u32[]{:S(2)}) copy-start(bf16[512,1024]{1,0:T(8,128)(2,1)} %kvw_ref.1) | copy-start | bytes 3145732
  12.0 1.0 %copy-start.1 = (bf16[1,128,3,512]{3,1,2,0:T(8,128)(2,1)S(1)}, bf16[1,128,3,512]{3,1,2,0:T(8,128)(2,1)}, u32[]{:S(2)}) copy-start(bf16[1,128,3,512]{3,1,2,0:T(8,128)(2,1)} %param.13) | copy-start | bytes 1179652
  23.7 3.4 %collective-permute-start = (bf16[768,128]{1,0:T(8,128)(2,1)S(1)}, bf16[768,128]{1,0:T(8,128)(2,1)S(1)}, u32[]{:S(2)}, u32[]{:S(2)}) collective-permute-start(bf16[768,128]{1,0:T(8,128)(2,1)S(1)} %get-tuple-element.14), channel_id=1, source_target_pairs={{0,1},{1,0},{2,3},{3,2},{4,5},{5,4},{6,7},{7,6},{8,9},{9,8},{10,11... | collective-permute-start | bytes 589832 | tf_op jit(solution)/shard_map/ppermute | solution.py:353

commit v11 on v10

--- a/solution.py
+++ b/solution.py
@@ -219,9 +219,13 @@
                     grad_values = term if grad_values is None else grad_values + term
                 left_s[rows, lanes] = grad_values.astype(BF16)
 
-    grad_values_of(every)
-
-    outer = lax.dot_general(left_s[...], pin_s[...], NT, preferred_element_type=F32)
+    outer = None
+    for group in (every[:6], every[6:]):
+        grad_values_of(group)
+        at = lanes_of(group)
+        term = lax.dot_general(left_s[:, at], pin_s[:, at], NT, preferred_element_type=F32)
+        outer = term if outer is None else outer + term
+
     keep_out[...] = outer
     send_out[...] = outer.astype(BF16)
 

time: 66.1 us -> 65.4 us (0.989)
  Pallas kernels: 10.2 us -> 9.52 us
    pallas_call x1, Pallas kernels: 5.82 us -> 5.11 us  [on_device(): call(main_kernel, (shape(LEFT, TOK, dtype=F32), shape(LEFT, TOK)), [SMEM,...]
where the time goes in v11:
time: 65.4 us; the launch traced here: 64.8 us
  blocking collectives  36.6 us (56%)
  starting transfers between devices  9.98 us (15%)
  Pallas kernels  9.52 us (15%)
  waiting for transfers between devices  4.16 us (6%)
  local copies, waits for them, and re-layouts  3.17 us (5%)
  between operations  1.38 us (2%)
    all_to_all x1, blocking collectives, on_device(): lax.all_to_all(part.reshape(ZED, HALF // ZED, ROW), 'lat', 0, 0, tiled=Tr...  26.4 us
    all_to_all x1, blocking collectives, on_device(): shared = lax.all_to_all(share, 'lon', 0, 0, tiled=True)  10.2 us
    all_to_all x1, starting transfers between devices, on_device(): recv = lax.all_to_all(slots, 'lon', 0, 0, tiled=True)  7.6 us
    pallas_call x1, Pallas kernels, on_device(): call(main_kernel, (shape(LEFT, TOK, dtype=F32), shape(LEFT, TOK)), [SMEM,...  5.11 us
    unnamed x12, local copies, waits for them, and re-layouts  3.17 us
    all_to_all x1, waiting for transfers between devices, on_device(): recv = lax.all_to_all(slots, 'lon', 0, 0, tiled=True)  3.09 us
    ppermute x1, starting transfers between devices, on_device(): other = lax.ppermute(send, 'lat', [(i, i ^ 1) for i in range(lats)])  2.38 us
    pallas_call x1, Pallas kernels, on_device(): call(prep_kernel, (shape(2 * D + 64, D), shape(D, RAW + TOK), shape(OWN,...  1.82 us
  transfers between devices with their start and end apart: 2, of which 2 were waited for; matrix products, arithmetic and copies ran while one was open for 0% of the time, Pallas kernels for 3%

profile of v11, /device:TPU:1, one launch (start us, length us, event | category | flops | bytes accessed | tf_op | source)
XLA Modules:
  0.0 64.8 jit_solution(15497662456051204258)
XLA Ops:
  0.6 0.0 copy-start.5
  0.6 0.0 copy-start.2
  0.7 0.9 %copy-done.2 = bf16[1,1664,80]{1,2,0:T(8,128)(2,1)S(1)} copy-done((bf16[1,1664,80]{1,2,0:T(8,128)(2,1)S(1)}, bf16[1,1664,80]{1,2,0:T(8,128)(2,1)}, u32[]{:S(2)}) %copy-start.2) | copy-done | bytes 266264
  1.6 0.0 copy-start.3
  1.6 0.0 copy-start.4
  1.6 0.8 %slots.1 = bf16[16,80,128]{2,1,0:T(8,128)(2,1)} custom-call(s32[1]{0:T(128)} %bitcast.1.lon_ref, bf16[80,1664]{1,0:T(8,128)(2,1)S(1)} %bitcast.12), custom_call_target="tpu_custom_call" | custom-call | tf_op jit(solution)/shard_map/slots/pallas_call | solution.py:319
  2.4 7.6 %all-to-all-start = ((bf16[16,80,128]{2,1,0:T(8,128)(2,1)}), bf16[16,80,128]{2,1,0:T(8,128)(2,1)S(1)}, u32[]{:S(2)}, u32[]{:S(2)}) async-start(bf16[16,80,128]{2,1,0:T(8,128)(2,1)} %slots.1), calls=%async_computation | async-start | bytes 655360 | tf_op jit(solution)/shard_map/all_to_all | solution.py:336
  10.7 0.0 copy-done.5
  10.7 0.0 copy-done.3
  10.7 0.0 copy-done.4
  10.7 0.0 copy-start
  10.7 1.2 %copy-done = bf16[512,1024]{1,0:T(8,128)(2,1)S(1)} copy-done((bf16[512,1024]{1,0:T(8,128)(2,1)S(1)}, bf16[512,1024]{1,0:T(8,128)(2,1)}, u32[]{:S(2)}) %copy-start) | copy-done | bytes 1048600
  12.0 0.0 copy-start.1
  12.0 1.0 %copy-done.1 = bf16[1,128,3,512]{3,1,2,0:T(8,128)(2,1)S(1)} copy-done((bf16[1,128,3,512]{3,1,2,0:T(8,128)(2,1)S(1)}, bf16[1,128,3,512]{3,1,2,0:T(8,128)(2,1)}, u32[]{:S(2)}) %copy-start.1) | copy-done | bytes 393240
  12.9 1.8 %prep.1 = (bf16[1088,512]{1,0:T(8,128)(2,1)S(1)}, bf16[512,1152]{1,0:T(8,128)(2,1)S(1)}, bf16[288,1280]{1,0:T(8,128)(2,1)S(1)}) custom-call(s32[1]{0:T(128)} %bitcast.core_ref, bf16[512,1024]{1,0:T(8,128)(2,1)S(1)} %copy-done, bf16[80,512]{1,0:T(8,128)(2,1)S(1)} %copy-done.3, bf16[13,512]{1,0:T(8,128)(2,1)S(1)} %copy-done.4, bf16[3,512]{1,0:T(4,128)(2,1)S(1)} %copy-done.5, ...), custom_call_target="tpu_custom_call" | custom-call | tf_op jit(solution)/shard_map/prep/pallas_call | solution.py:328
  14.8 3.1 %all-to-all-done.recv_ref = bf16[16,80,128]{2,1,0:T(8,128)(2,1)S(1)} async-done(((bf16[16,80,128]{2,1,0:T(8,128)(2,1)}), bf16[16,80,128]{2,1,0:T(8,128)(2,1)S(1)}, u32[]{:S(2)}, u32[]{:S(2)}) %all-to-all-start) | async-done | bytes 327712 | tf_op jit(solution)/shard_map/all_to_all | solution.py:336
  17.9 5.1 %main.1 = (f32[768,128]{1,0:T(8,128)S(1)}, bf16[768,128]{1,0:T(8,128)(2,1)S(1)}) custom-call(s32[1]{0:T(128)} %bitcast.1.lon_ref, s32[1]{0:T(128)S(6)} %copy.10.count_ref, bf16[16,80,128]{2,1,0:T(8,128)(2,1)S(1)} %all-to-all-done.recv_ref, bf16[1088,512]{1,0:T(8,128)(2,1)S(1)} %get-tuple-element.11.tall_ref, bf16[512,1152]{1,0:T(8,128)(2,1)S(1)} %get-tuple-element.12.wide_ref), custom_call_target="tpu_custom_call" | custom-call | tf_op jit(solution)/shard_map/main/pallas_call | solution.py:337
  23.0 2.4 %collective-permute-start = (bf16[768,128]{1,0:T(8,128)(2,1)S(1)}, bf16[768,128]{1,0:T(8,128)(2,1)S(1)}, u32[]{:S(2)}, u32[]{:S(2)}) collective-permute-start(bf16[768,128]{1,0:T(8,128)(2,1)S(1)} %get-tuple-element.14), channel_id=1, source_target_pairs={{0,1},{1,0},{2,3},{3,2},{4,5},{5,4},{6,7},{7,6},{8,9},{9,8},{10,11... | collective-permute-start | bytes 589832 | tf_op jit(solution)/shard_map/ppermute | solution.py:357
  25.4 1.1 %collective-permute-done.recv_ref = bf16[768,128]{1,0:T(8,128)(2,1)S(1)} collective-permute-done((bf16[768,128]{1,0:T(8,128)(2,1)S(1)}, bf16[768,128]{1,0:T(8,128)(2,1)S(1)}, u32[]{:S(2)}, u32[]{:S(2)}) %collective-permute-start) | collective-permute-done | bytes 196640 | tf_op jit(solution)/shard_map/ppermute | solution.py:357
  26.4 0.8 %post.1 = bf16[256,1152]{1,0:T(8,128)(2,1)S(1)} custom-call(s32[1]{0:T(128)} %bitcast.core_ref, f32[768,128]{1,0:T(8,128)S(1)} %get-tuple-element.13.keep_ref, bf16[768,128]{1,0:T(8,128)(2,1)S(1)} %collective-permute-done.recv_ref, bf16[512,1152]{1,0:T(8,128)(2,1)S(1)} %get-tuple-element.12.wide_ref, bf16[288,1280]{1,0:T(8,128)(2,1)S(1)} %get-tuple-element.15.own_ref), custom_call_target="tpu_custom_call" | custom-call | tf_op jit(solution)/shard_map/post/pallas_call | solution.py:358
  27.2 26.4 %all_to_all.15.part_ref = bf16[8,32,1152]{2,1,0:T(8,128)(2,1)S(1)} all-to-all(bf16[8,32,1152]{2,1,0:T(8,128)(2,1)S(1)} %bitcast.10), channel_id=1, replica_groups={{0,2,4,6,8,10,12,14},{1,3,5,7,9,11,13,15},{16,18,20,22,24,26,28,30},{17..., dimensions={0} | all-to-all | bytes 1179648 | tf_op jit(solution)/shard_map/all_to_all | solution.py:359
  53.6 0.2 sum_z.1
  53.7 10.2 %all_to_all.16.share_ref = bf16[16,48,128]{2,1,0:T(8,128)(2,1)S(1)} all-to-all(bf16[16,48,128]{2,1,0:T(8,128)(2,1)S(1)} %sum_z.1), channel_id=1, replica_groups=mesh['lon'=16,'lat'=16] {'lon'}, dimensions={0} | all-to-all | bytes 393216 | tf_op jit(solution)/shard_map/all_to_all | solution.py:375
  63.9 0.8 %sum_lon.1 = (f32[2,1024]{1,0:T(2,128)}, f32[32,80]{1,0:T(8,128)}, f32[3,512]{1,0:T(4,128)}) custom-call(bf16[16,48,128]{2,1,0:T(8,128)(2,1)S(1)} %all_to_all.16.share_ref), custom_call_target="tpu_custom_call" | custom-call | tf_op jit(solution)/shard_map/sum_lon/pallas_call | solution.py:376
Async XLA Ops:
  0.6 10.1 %copy-start.5 = (bf16[3,512]{1,0:T(4,128)(2,1)S(1)}, bf16[3,512]{1,0:T(4,128)(2,1)}, u32[]{:S(2)}) copy-start(bf16[3,512]{1,0:T(4,128)(2,1)} %query_ref.1) | copy-start | bytes 9220
  0.6 1.0 %copy-start.2 = (bf16[1,1664,80]{1,2,0:T(8,128)(2,1)S(1)}, bf16[1,1664,80]{1,2,0:T(8,128)(2,1)}, u32[]{:S(2)}) copy-start(bf16[1,1664,80]{1,2,0:T(8,128)(2,1)} %param.7) | copy-start | bytes 798724
  1.6 9.1 %copy-start.3 = (bf16[80,512]{1,0:T(8,128)(2,1)S(1)}, bf16[80,512]{1,0:T(8,128)(2,1)}, u32[]{:S(2)}) copy-start(bf16[80,512]{1,0:T(8,128)(2,1)} %embed_w_ref.1) | copy-start | bytes 245764
  1.6 9.1 %copy-start.4 = (bf16[13,512]{1,0:T(8,128)(2,1)S(1)}, bf16[13,512]{1,0:T(8,128)(2,1)}, u32[]{:S(2)}) copy-start(bf16[13,512]{1,0:T(8,128)(2,1)} %level_ref.1) | copy-start | bytes 39940
  2.4 15.4 %all-to-all-start = ((bf16[16,80,128]{2,1,0:T(8,128)(2,1)}), bf16[16,80,128]{2,1,0:T(8,128)(2,1)S(1)}, u32[]{:S(2)}, u32[]{:S(2)}) async-start(bf16[16,80,128]{2,1,0:T(8,128)(2,1)} %slots.1), calls=%async_computation | async-start | bytes 655360 | tf_op jit(solution)/shard_map/all_to_all | solution.py:336
  10.7 1.2 %copy-start = (bf16[512,1024]{1,0:T(8,128)(2,1)S(1)}, bf16[512,1024]{1,0:T(8,128)(2,1)}, u32[]{:S(2)}) copy-start(bf16[512,1024]{1,0:T(8,128)(2,1)} %kvw_ref.1) | copy-start | bytes 3145732
  12.0 1.0 %copy-start.1 = (bf16[1,128,3,512]{3,1,2,0:T(8,128)(2,1)S(1)}, bf16[1,128,3,512]{3,1,2,0:T(8,128)(2,1)}, u32[]{:S(2)}) copy-start(bf16[1,128,3,512]{3,1,2,0:T(8,128)(2,1)} %param.13) | copy-start | bytes 1179652
  23.0 3.5 %collective-permute-start = (bf16[768,128]{1,0:T(8,128)(2,1)S(1)}, bf16[768,128]{1,0:T(8,128)(2,1)S(1)}, u32[]{:S(2)}, u32[]{:S(2)}) collective-permute-start(bf16[768,128]{1,0:T(8,128)(2,1)S(1)} %get-tuple-element.14), channel_id=1, source_target_pairs={{0,1},{1,0},{2,3},{3,2},{4,5},{5,4},{6,7},{7,6},{8,9},{9,8},{10,11... | collective-permute-start | bytes 589832 | tf_op jit(solution)/shard_map/ppermute | solution.py:357
